TPU v7x, 32 devices: a whole 2x2x4 slice. The times are simulated.
32 devices in a mesh: tile: 8 (over z, y), layer: 4 (over x, core).
Axes of the slice: x: 2, y: 2, z: 4, core: 2. Of those that a mesh axis runs over, the one named last changes fastest.
Arguments:
- forcing: float32 [16, 16, 64, 512], P('layer', None, 'tile'), may hold values from -6 to 6
- vert_coupling: float32 [16, 64, 512], P(None, 'tile', 'layer'), may hold values from 0.25 to 4
- horiz_coupling: float32 [64, 512], P('tile'), may hold values from 0.25 to 2
- basal_velocity: float32 [64, 512], P('tile', 'layer'), may hold values from 0.5 to 10
- group_label: int32 [64, 512], P('tile', 'layer'), may hold values from 0 to 511
- ice_mask: int32 [64, 512], P('tile', 'layer'), may hold values 0 or 1
Outputs:
- adjoint: float32 [16, 16, 64, 512], P('layer', None, 'tile')
- sensitivity: float32 [16, 512], replicated
All inputs are finite; a program needn't handle non-finite values. No bound on the sum of `ice_mask` on one device may be relied on, other than what follows from the above.
Results may differ from a plain program's by a relative error of at most 0.0001.
Values sent between devices are 32-bit elements; how exact they have to be, the bound alone decides.
No kernel may reach another device: no remote copies, remote signals or barrier semaphores. Data moves between devices by JAX's collectives and lax.ppermute only.
A program may use at most 64 MiB of HBM per device.

v0:
```python
import jax
import jax.numpy as jnp
from jax import lax
from jax.sharding import PartitionSpec as P

GROUPS = 512


def with_halo(block, sides, width):
    for axis, dim in sides:
        count = lax.axis_size(axis)
        forward = [(i, i + 1) for i in range(count - 1)]
        backward = [(target, source) for source, target in forward]
        low = lax.ppermute(
            lax.slice_in_dim(block, block.shape[dim] - width, None, axis=dim), axis, forward
        )
        high = lax.ppermute(lax.slice_in_dim(block, 0, width, axis=dim), axis, backward)
        block = jnp.concatenate([low, block, high], axis=dim)
    return block


def column_solve(rhs, sub_diag, full_diag, super_diag):

    def forward(running, layer_in):
        c_prime, d_prime = running
        sub_k, diag_k, super_k, rhs_k = layer_in
        pivot = diag_k - sub_k * c_prime
        c_next = super_k / pivot
        d_next = (rhs_k - sub_k * d_prime) / pivot
        return ((c_next, d_next), (c_next, d_next))

    start = (jnp.zeros_like(full_diag[0]), jnp.zeros_like(rhs[0]))
    _, (c_all, d_all) = lax.scan(forward, start, (sub_diag, full_diag, super_diag, rhs))

    def backward(solved_up, layer_in):
        c_here, d_here = layer_in
        solved = d_here - c_here * solved_up
        return (solved, solved)

    _, result = lax.scan(backward, jnp.zeros_like(rhs[0]), (c_all, d_all), reverse=True)
    return result


def vertical_apply(field, sub_diag, vert_diag, super_diag):
    zero_layer = jnp.zeros_like(field[:1])
    below = jnp.concatenate([zero_layer, field[:-1]], axis=0)
    above = jnp.concatenate([field[1:], zero_layer], axis=0)
    return vert_diag * field + sub_diag * below + super_diag * above


def five_point(field, padded, coupling_here):
    return coupling_here * (
        4.0 * field
        - padded[:, :, :-2, 1:-1]
        - padded[:, :, 2:, 1:-1]
        - padded[:, :, 1:-1, :-2]
        - padded[:, :, 1:-1, 2:]
    )


def to_columns(field):
    return lax.all_to_all(field, "layer", split_axis=3, concat_axis=0, tiled=True)


def to_layers(field):
    return lax.all_to_all(field, "layer", split_axis=0, concat_axis=3, tiled=True)


def shards(forcing, vert_coupling, horiz_coupling, basal_velocity, group_label, ice_mask):
    width_col = vert_coupling.shape[2]
    rows_tile = vert_coupling.shape[1]
    layer_pos = lax.axis_index("layer")
    coupling_col = lax.dynamic_slice_in_dim(horiz_coupling, layer_pos * width_col, width_col, 1)
    coupling = vert_coupling[:, None]
    zero_layer = jnp.zeros_like(coupling[:1])
    coupling_next = jnp.concatenate([coupling[1:], zero_layer], axis=0)
    sub_diag = jnp.concatenate([zero_layer, -coupling[1:]], axis=0)
    super_diag = -coupling_next
    vert_diag = coupling + coupling_next
    full_diag = vert_diag + 4.0 * coupling_col
    forcing_col = to_columns(forcing)
    adjoint_col = column_solve(forcing_col, sub_diag, full_diag, super_diag)
    adjoint_lay = to_layers(adjoint_col)
    rows_ext = with_halo(adjoint_lay, (("tile", 2),), 1)
    padded = jnp.pad(rows_ext, ((0, 0), (0, 0), (0, 0), (1, 1)))
    residual = to_columns(forcing - five_point(adjoint_lay, padded, horiz_coupling))
    residual = residual - vertical_apply(adjoint_col, sub_diag, vert_diag, super_diag)
    adjoint_col = adjoint_col + column_solve(residual, sub_diag, full_diag, super_diag)
    weight = vert_coupling[0] * basal_velocity * ice_mask.astype(jnp.float32)
    functionals = adjoint_col.shape[1]
    weighted = (adjoint_col[0] * weight).reshape(functionals, rows_tile * width_col)
    labels_flat = group_label.reshape(-1)
    indicator = (labels_flat[:, None] == jnp.arange(GROUPS, dtype=jnp.int32)[None, :]).astype(
        jnp.float32
    )
    partial_sums = jnp.dot(
        weighted, indicator, precision=lax.Precision.HIGHEST, preferred_element_type=jnp.float32
    )
    totals = lax.psum(partial_sums, ("tile", "layer"))
    columns_all = lax.axis_size("tile") * rows_tile * horiz_coupling.shape[1]
    sensitivity = -totals * (columns_all / GROUPS) ** (-0.5)
    adjoint = to_layers(adjoint_col)
    return (adjoint, sensitivity)


def solution(mesh):
    in_specs = (
        P("layer", None, "tile", None),
        P(None, "tile", "layer"),
        P("tile", None),
        P("tile", "layer"),
        P("tile", "layer"),
        P("tile", "layer"),
    )
    out_specs = (P("layer", None, "tile", None), P())
    return jax.shard_map(shards, mesh=mesh, in_specs=in_specs, out_specs=out_specs, check_vma=False)
```

profile of v0, /device:TPU:0, one launch (start us, length us, event | category | flops | bytes accessed | tf_op | source)
XLA Modules:
  0.0 216.5 jit_solution(11688051651057699620)
XLA Ops:
  0.6 8.4 %copy.27 = f32[4,16,8,512]{1,2,0,3:T(8,128)} copy(f32[4,16,8,512]{3,2,1,0:T(8,128)} %param.14) | data formatting | bytes 2097152 | tf_op args[0]
  9.0 6.4 %reshape.20 = f32[4,1,65536]{2,1,0:T(1,128)} reshape(f32[512,4,8,16]{3,2,1,0:T(8,128)} %bitcast.144) | data formatting | bytes 2097152
  15.4 4.3 %all-to-all-start = ((f32[4,1,65536]{2,1,0:T(1,128)}), f32[4,1,65536]{2,1,0:T(1,128)S(1)}, u32[]{:S(2)}, u32[]{:S(2)}) async-start(f32[4,1,65536]{2,1,0:T(1,128)} %reshape.20), calls=%async_computation | async-start | bytes 2097152 | tf_op jit(solution)/shard_map/all_to_all | solution.py:62
  19.8 14.4 %all-to-all-done = f32[4,1,65536]{2,1,0:T(1,128)S(1)} async-done(((f32[4,1,65536]{2,1,0:T(1,128)}), f32[4,1,65536]{2,1,0:T(1,128)S(1)}, u32[]{:S(2)}, u32[]{:S(2)}) %all-to-all-start) | async-done | bytes 1048608 | tf_op jit(solution)/shard_map/all_to_all | solution.py:62
  34.7 3.6 %reduce = f32[4,65536]{1,0:T(4,128)S(1)} reduce(f32[4,1,65536]{2,1,0:T(1,128)S(1)} %all-to-all-done, f32[]{:T(128)} %broadcast.90), dimensions={1}, to_apply=%all_to_all.52.reduce_sub_computation | reduce | bytes 2097156 | tf_op jit(solution)/shard_map/all_to_all | solution.py:62
  38.3 6.2 %reshape.21 = f32[512,4,8,16]{3,2,1,0:T(8,128)} reshape(f32[4,65536]{1,0:T(4,128)S(1)} %reduce) | data formatting | bytes 2097152
  44.4 6.6 %copy.28 = f32[4,4,16,8,128]{4,3,2,1,0:T(8,128)S(1)} copy(f32[4,4,16,8,128]{2,3,1,4,0:T(8,128)} %bitcast.141) | data formatting | bytes 2097152 | tf_op jit(solution)/shard_map/all_to_all | solution.py:62
  51.2 1.1 while.68
  52.4 1.0 while.69
  53.4 16.9 %all_to_all.72 = f32[16,16,8,128]{3,2,1,0:T(8,128)S(1)} all-to-all(f32[16,16,8,128]{3,2,1,0:T(8,128)S(1)} %get-tuple-element.306), channel_id=1, replica_groups=mesh['tile'=8,'layer'=4] {'layer'}, dimensions={0} | all-to-all | bytes 2097152 | tf_op jit(solution)/shard_map/all_to_all | solution.py:66
  71.5 4.3 %collective-permute-start = (f32[4,16,1,512]{3,1,2,0:T(8,128)S(1)}, f32[4,16,1,512]{3,1,2,0:T(8,128)S(1)}, u32[]{:S(2)}, u32[]{:S(2)}) collective-permute-start(f32[4,16,1,512]{3,1,2,0:T(8,128)S(1)} %get-tuple-element.534), channel_id=1, source_target_pairs={{0,4},{4,8},{8,12},{12,16},{16,20},{20,24},{24,28},{1,5},{5,9},{9,... | collective-permute-start | bytes 393224 | tf_op jit(solution)/shard_map/ppermute | solution.py:14
  75.8 1.5 collective-permute-start.1
  77.3 1.0 collective-permute-done
  78.3 4.4 %collective-permute-done.1 = f32[4,16,1,512]{3,1,2,0:T(8,128)S(1)} collective-permute-done((f32[4,16,1,512]{3,1,2,0:T(8,128)S(1)}, f32[4,16,1,512]{3,1,2,0:T(8,128)S(1)}, u32[]{:S(2)}, u32[]{:S(2)}) %collective-permute-start.1) | collective-permute-done | bytes 131104 | tf_op jit(solution)/shard_map/ppermute | solution.py:17
  83.1 1.1 fusion.7
  84.2 7.5 %copy.33 = f32[4,16,8,512]{1,2,0,3:T(8,128)} copy(f32[4,16,8,512]{3,1,2,0:T(8,128)S(1)} %fusion.7) | data formatting | bytes 2097152 | tf_op jit(solution)/shard_map/sub | solution.py:86
  91.8 6.4 %reshape.22 = f32[4,1,65536]{2,1,0:T(1,128)} reshape(f32[512,4,8,16]{3,2,1,0:T(8,128)} %bitcast.142) | data formatting | bytes 2097152
  98.1 3.5 %all-to-all-start.2 = ((f32[4,1,65536]{2,1,0:T(1,128)}), f32[4,1,65536]{2,1,0:T(1,128)S(1)}, u32[]{:S(2)}, u32[]{:S(2)}) async-start(f32[4,1,65536]{2,1,0:T(1,128)} %reshape.22), calls=%async_computation.2 | async-start | bytes 2097152 | tf_op jit(solution)/shard_map/all_to_all | solution.py:62
  101.7 1.5 fusion.22
  103.2 12.9 %all-to-all-done.2 = f32[4,1,65536]{2,1,0:T(1,128)S(1)} async-done(((f32[4,1,65536]{2,1,0:T(1,128)}), f32[4,1,65536]{2,1,0:T(1,128)S(1)}, u32[]{:S(2)}, u32[]{:S(2)}) %all-to-all-start.2) | async-done | bytes 1048608 | tf_op jit(solution)/shard_map/all_to_all | solution.py:62
  116.1 3.6 %reduce.1 = f32[4,65536]{1,0:T(4,128)S(1)} reduce(f32[4,1,65536]{2,1,0:T(1,128)S(1)} %all-to-all-done.2, f32[]{:T(128)} %broadcast.90), dimensions={1}, to_apply=%all_to_all.60.reduce_sub_computation | reduce | bytes 2097156 | tf_op jit(solution)/shard_map/all_to_all | solution.py:62
  119.7 6.2 %reshape.23 = f32[512,4,8,16]{3,2,1,0:T(8,128)} reshape(f32[4,65536]{1,0:T(4,128)S(1)} %reduce.1) | data formatting | bytes 2097152
  125.9 6.7 %copy.34 = f32[4,4,16,8,128]{4,3,2,1,0:T(8,128)S(1)} copy(f32[4,4,16,8,128]{2,3,1,4,0:T(8,128)} %bitcast.143) | data formatting | bytes 2097152 | tf_op jit(solution)/shard_map/all_to_all | solution.py:62
  132.6 2.6 %bitcast_subtract_fusion.4 = f32[16,16,8,128]{3,2,1,0:T(8,128)} fusion(f32[4,4,16,8,128]{4,3,2,1,0:T(8,128)S(1)} %copy.34, f32[15,16,8,128]{3,2,1,0:T(8,128)} %get-tuple-element.533, f32[15,16,8,128]{3,2,1,0:T(8,128)S(1)} %copy-done.1, f32[16,16,8,128]{3,2,1,0:T(8,128)S(1)} %get-tuple-element.306, f32[16,8,128]{2,1,0:T(8,128)S(1)} %get-tuple-element.540, ...), kind=kLoop, calls=%fused_computation.41 | loop fusion | flops 1572864 | bytes 5308416 | tf_op jit(solution)/shard_map/sub | solution.py:87
  135.4 25.5 %while.70 = (s32[]{:T(128)}, f32[1,8,128]{2,1,0:T(8,128)S(1)}, f32[16,8,128]{2,1,0:T(8,128)S(1)}, f32[16,1,8,128]{3,2,1,0:T(8,128)S(1)}, f32[16,16,8,128]{3,2,1,...) while((s32[]{:T(128)}, f32[1,8,128]{2,1,0:T(8,128)S(1)}, ...), condition=%wide.region_5.6_spmd.clone, body=%wide.region_4.5_spmd.clone.sunk | while | flops 69635 | bytes 303232 | solution.py:33
  136.1 0.9 bitcast_dynamic-update-slice_fusion.16
  137.7 0.9 bitcast_dynamic-update-slice_fusion.16
  139.3 0.9 bitcast_dynamic-update-slice_fusion.16
  140.9 0.9 bitcast_dynamic-update-slice_fusion.16
  142.5 0.9 bitcast_dynamic-update-slice_fusion.16
  144.1 0.9 bitcast_dynamic-update-slice_fusion.16
  145.7 0.9 bitcast_dynamic-update-slice_fusion.16
  147.3 0.9 bitcast_dynamic-update-slice_fusion.16
  148.9 0.9 bitcast_dynamic-update-slice_fusion.16
  150.5 0.9 bitcast_dynamic-update-slice_fusion.16
  152.1 0.9 bitcast_dynamic-update-slice_fusion.16
  153.6 0.9 bitcast_dynamic-update-slice_fusion.16
  155.2 0.9 bitcast_dynamic-update-slice_fusion.16
  156.8 0.9 bitcast_dynamic-update-slice_fusion.16
  158.4 0.9 bitcast_dynamic-update-slice_fusion.16
  160.0 0.9 bitcast_dynamic-update-slice_fusion.16
  161.0 1.0 while.71
  162.0 1.1 add.79
  163.1 3.6 %all-to-all-start.3 = ((f32[16,16,8,128]{3,2,1,0:T(8,128)}), f32[16,16,8,128]{3,2,1,0:T(8,128)S(1)}, u32[]{:S(2)}, u32[]{:S(2)}) async-start(f32[16,16,8,128]{3,2,1,0:T(8,128)} %add.79), calls=%async_computation.3 | async-start | bytes 2097152 | tf_op jit(solution)/shard_map/all_to_all | solution.py:66
  166.8 0.8 slice.57
  167.6 0.8 fusion.4
  168.4 46.3 %psum.7 = f32[16,512]{1,0:T(8,128)S(1)} all-reduce(f32[16,512]{1,0:T(8,128)S(1)} %fusion.4), channel_id=1, replica_groups=mesh['tile'=8,'layer'=4] {'tile','layer'}, use_global_device_ids=true, to_apply=%region_8.9 | all-reduce | flops 8192 | bytes 65536 | tf_op jit(solution)/shard_map/psum | solution.py:99
  215.4 1.1 copy.46
  (156 shorter events, 16.1 us)
Async XLA Ops:
  15.4 4.3 %copy-start.6 = (f32[8,512]{1,0:T(8,128)S(1)}, f32[8,512]{1,0:T(8,128)}, u32[]{:S(2)}) copy-start(f32[8,512]{1,0:T(8,128)} %param.16) | copy-start | bytes 49156
  15.4 4.4 %copy-start.2 = (f32[16,8,128]{2,1,0:T(8,128)S(1)}, f32[16,8,128]{2,1,0:T(8,128)}, u32[]{:S(2)}) copy-start(f32[16,8,128]{2,1,0:T(8,128)} %param.15) | copy-start | bytes 196612
  15.4 18.8 %all-to-all-start = ((f32[4,1,65536]{2,1,0:T(1,128)}), f32[4,1,65536]{2,1,0:T(1,128)S(1)}, u32[]{:S(2)}, u32[]{:S(2)}) async-start(f32[4,1,65536]{2,1,0:T(1,128)} %reshape.20), calls=%async_computation | async-start | bytes 2097152 | tf_op jit(solution)/shard_map/all_to_all | solution.py:62
  52.3 18.0 %copy-start.3 = (f32[16,1,8,128]{3,2,1,0:T(8,128)}, f32[16,1,8,128]{3,2,1,0:T(8,128)S(1)}, u32[]{:S(2)}) copy-start(f32[16,1,8,128]{3,2,1,0:T(8,128)S(1)} %get-tuple-element.867) | copy-start | bytes 196612
  52.3 18.0 %copy-start.4 = (f32[16,1,8,128]{3,2,1,0:T(8,128)}, f32[16,1,8,128]{3,2,1,0:T(8,128)S(1)}, u32[]{:S(2)}) copy-start(f32[16,1,8,128]{3,2,1,0:T(8,128)S(1)} %get-tuple-element.868) | copy-start | bytes 196612
  52.3 18.0 %copy-start.5 = (f32[16,1,8,128]{3,2,1,0:T(8,128)}, f32[16,1,8,128]{3,2,1,0:T(8,128)S(1)}, u32[]{:S(2)}) copy-start(f32[16,1,8,128]{3,2,1,0:T(8,128)S(1)} %get-tuple-element.869) | copy-start | bytes 196612
  71.4 11.7 %copy-start = (f32[4,16,8,512]{3,2,1,0:T(8,128)S(1)}, f32[4,16,8,512]{3,2,1,0:T(8,128)}, u32[]{:S(2)}) copy-start(f32[4,16,8,512]{3,2,1,0:T(8,128)} %param.14) | copy-start | bytes 3145732
  71.5 6.8 %collective-permute-start = (f32[4,16,1,512]{3,1,2,0:T(8,128)S(1)}, f32[4,16,1,512]{3,1,2,0:T(8,128)S(1)}, u32[]{:S(2)}, u32[]{:S(2)}) collective-permute-start(f32[4,16,1,512]{3,1,2,0:T(8,128)S(1)} %get-tuple-element.534), channel_id=1, source_target_pairs={{0,4},{4,8},{8,12},{12,16},{16,20},{20,24},{24,28},{1,5},{5,9},{9,... | collective-permute-start | bytes 393224 | tf_op jit(solution)/shard_map/ppermute | solution.py:14
  75.8 6.9 %collective-permute-start.1 = (f32[4,16,1,512]{3,1,2,0:T(8,128)S(1)}, f32[4,16,1,512]{3,1,2,0:T(8,128)S(1)}, u32[]{:S(2)}, u32[]{:S(2)}) collective-permute-start(f32[4,16,1,512]{3,1,2,0:T(8,128)S(1)} %get-tuple-element.535), channel_id=1, source_target_pairs={{4,0},{8,4},{12,8},{16,12},{20,16},{24,20},{28,24},{5,1},{9,5},{13... | collective-permute-start | bytes 393224 | tf_op jit(solution)/shard_map/ppermute | solution.py:17
  98.1 18.0 %all-to-all-start.2 = ((f32[4,1,65536]{2,1,0:T(1,128)}), f32[4,1,65536]{2,1,0:T(1,128)S(1)}, u32[]{:S(2)}, u32[]{:S(2)}) async-start(f32[4,1,65536]{2,1,0:T(1,128)} %reshape.22), calls=%async_computation.2 | async-start | bytes 2097152 | tf_op jit(solution)/shard_map/all_to_all | solution.py:62
  125.9 6.7 %copy-start.1 = (f32[15,16,8,128]{3,2,1,0:T(8,128)S(1)}, f32[15,16,8,128]{3,2,1,0:T(8,128)}, u32[]{:S(2)}) copy-start(f32[15,16,8,128]{3,2,1,0:T(8,128)} %get-tuple-element.532) | copy-start | bytes 2949124
  163.1 3.7 %copy-start.7 = (f32[8,128]{1,0:T(8,128)S(1)}, f32[8,128]{1,0:T(8,128)}, u32[]{:S(2)}) copy-start(f32[8,128]{1,0:T(8,128)} %param.17) | copy-start | bytes 12292
  163.1 3.7 %copy-start.8 = (s32[8,128]{1,0:T(8,128)S(1)}, s32[8,128]{1,0:T(8,128)}, u32[]{:S(2)}) copy-start(s32[8,128]{1,0:T(8,128)} %param.19) | copy-start | bytes 12292
  163.1 4.5 %copy-start.9 = (s32[8,128]{1,0:T(8,128)S(1)}, s32[8,128]{1,0:T(8,128)}, u32[]{:S(2)}) copy-start(s32[8,128]{1,0:T(8,128)} %param.18) | copy-start | bytes 12292
  163.1 52.3 %all-to-all-start.3 = ((f32[16,16,8,128]{3,2,1,0:T(8,128)}), f32[16,16,8,128]{3,2,1,0:T(8,128)S(1)}, u32[]{:S(2)}, u32[]{:S(2)}) async-start(f32[16,16,8,128]{3,2,1,0:T(8,128)} %add.79), calls=%async_computation.3 | async-start | bytes 2097152 | tf_op jit(solution)/shard_map/all_to_all | solution.py:66
where the time goes:
time: 219 us; the launch traced here: 217 us
  blocking collectives  63.2 us (29%)
  local copies, waits for them, and re-layouts  60.2 us (27%)
  other arithmetic  39.6 us (18%)
  waiting for transfers between devices  32.6 us (15%)
  starting transfers between devices  17.3 us (8%)
    psum x1, blocking collectives, shards(): totals = lax.psum(partial_sums, ('tile', 'layer'))  46.3 us
    unnamed x25, local copies, waits for them, and re-layouts  33.5 us
    all_to_all x2, waiting for transfers between devices, to_columns(): lax.all_to_all(field, 'layer', split_axis=3, concat_axis=0, tiled=True)  27.2 us
    dynamic_update_slice x96, other arithmetic, column_solve(): lax.scan(forward, start, (sub_diag, full_diag, super_diag, rhs))  26.4 us
    all_to_all x1, blocking collectives, to_layers(): lax.all_to_all(field, 'layer', split_axis=0, concat_axis=3, tiled=True)  16.9 us
    all_to_all x3, local copies, waits for them, and re-layouts, to_columns(): lax.all_to_all(field, 'layer', split_axis=3, concat_axis=0, tiled=True)  13.9 us
    all_to_all x2, starting transfers between devices, to_columns(): lax.all_to_all(field, 'layer', split_axis=3, concat_axis=0, tiled=True)  7.86 us
    sub x1, local copies, waits for them, and re-layouts, shards(): forcing - five_point(adjoint_lay, padded, horiz_coupling)  7.51 us
  transfers between devices with their start and end apart: 5, of which 4 were waited for; matrix products, arithmetic and copies ran while one was open for 2% of the time, Pallas kernels for 0%

commit v1 on v0

v1 whole, which is shorter than its diff:
```python
import functools

import jax
import jax.numpy as jnp
from jax import lax
from jax.experimental import pallas as pl
from jax.experimental.pallas import tpu as pltpu
from jax.sharding import PartitionSpec as P

GROUPS = 512
LANES = 128
VMEM_BYTES = 48 * 1024 * 1024
UP, DOWN, LEFT, RIGHT = range(4)


def position():
    layer = lax.axis_index("layer")
    return layer // 2, layer % 2


def edge_flags():
    tile = lax.axis_index("tile")
    last = lax.axis_size("tile") - 1
    return (
        jnp.where(tile > 0, 1.0, 0.0).astype(jnp.float32),
        jnp.where(tile < last, 1.0, 0.0).astype(jnp.float32),
    )


def moved(plane, direction, halo=None):
    rows, width = plane.shape
    axis = 0 if direction in (UP, DOWN) else 1
    size = plane.shape[axis]
    first = direction in (UP, LEFT)
    rolled = pltpu.roll(plane, 1 if first else size - 1, axis)
    at_edge = lax.broadcasted_iota(jnp.int32, plane.shape, axis) == (0 if first else size - 1)
    filler = jnp.zeros_like(plane) if halo is None else jnp.broadcast_to(halo, plane.shape)
    return jnp.where(at_edge, filler, rolled)


def chip_factors(planes, side, layers):
    half = layers // 2
    horiz = planes(layers + 2)

    def coupling(j):
        if j == 0:
            return planes(0) * jnp.where(side == 0, 1.0, 0.0)
        return planes(jnp.where(side == 0, j, layers - j))

    multiplier, inverse = [None], []
    below = coupling(0)
    for j in range(half):
        above = coupling(j + 1)
        pivot = below + above + 4.0 * horiz
        if j > 0:
            pivot = pivot - below * multiplier[j]
        inverse.append(1.0 / pivot)
        multiplier.append(above * inverse[j])
        below = above
    return multiplier, inverse, below


def unit_response(multiplier, inverse):
    half = len(inverse)
    response = [None] * half
    response[half - 1] = inverse[half - 1]
    for j in range(half - 2, -1, -1):
        response[j] = multiplier[j + 1] * response[j + 1]
    return response


def chip_solve(values, multiplier, inverse):
    half = len(values)
    swept = [values[0]]
    for j in range(1, half):
        swept.append(values[j] + multiplier[j] * swept[j - 1])
    solved = [None] * half
    solved[half - 1] = swept[half - 1] * inverse[half - 1]
    for j in range(half - 2, -1, -1):
        solved[j] = swept[j] * inverse[j] + multiplier[j + 1] * solved[j + 1]
    return solved


def assemble_kernel(own, peer, cross, diag, horiz, planes, row_first, row_last):
    layer = lax.axis_index("layer")
    count = own.shape[0]
    for k, block in enumerate((own, peer, cross, diag)):
        start = pl.multiple_of(jnp.bitwise_xor(layer, k) * LANES, LANES)
        planes[0:count, :, pl.ds(start, LANES)] = block[...]
    planes[count] = horiz[...]
    rows = planes.shape[1]
    for k in range(count + 1):
        row_first[k : k + 1, :] = planes[k, 0:1, :]
        row_last[k : k + 1, :] = planes[k, rows - 1 : rows, :]
    for k in range(count + 1, row_first.shape[0]):
        row_first[k : k + 1, :] = planes[0, 0:1, :]
        row_last[k : k + 1, :] = planes[0, 0:1, :]


def load_forcing(own, received, gathered, sems):
    _, core = position()
    held, functionals = received.shape[0], received.shape[1]
    copies = (
        pltpu.make_async_copy(
            own.at[:, pl.ds(core * functionals, functionals)],
            gathered.at[pl.ds(core * held, held)],
            sems.at[0],
        ),
        pltpu.make_async_copy(received, gathered.at[pl.ds((1 - core) * held, held)], sems.at[1]),
    )
    for copy in copies:
        copy.start()
    return copies


def local_kernel(own, received, planes, local, boundary, row_first, row_last, gathered, factors, sems):
    side, _ = position()
    copies = load_forcing(own, received, gathered, sems)
    layers = planes.shape[0] - 3
    half, functionals, rows, _ = local.shape
    multiplier, inverse, _ = chip_factors(lambda k: planes[k], side, layers)
    for j in range(half):
        factors[0, j] = multiplier[j + 1]
        factors[1, j] = inverse[j]
    for copy in copies:
        copy.wait()

    def step(f, carry):
        values = [gathered[side * (half - 1) + (1 - 2 * side) * j, f] for j in range(half)]
        solved = chip_solve(
            values,
            [None] + [factors[0, j] for j in range(half)],
            [factors[1, j] for j in range(half)],
        )
        for j in range(half):
            local[j, f] = solved[j]
            row_first[pl.ds(j * functionals + f, 1), :] = solved[j][0:1]
            row_last[pl.ds(j * functionals + f, 1), :] = solved[j][rows - 1 : rows]
        boundary[f] = solved[half - 1]
        return carry

    lax.fori_loop(0, functionals, step, 0)


def column_kernel(own, received, planes, above, below, sums, gathered, weights, halo, terms, outer, sems, *, scale):
    side, core = position()
    copies = load_forcing(own, received, gathered, sems)
    layers = planes.shape[0] - 3
    half, functionals, rows, width = gathered.shape
    has_above, has_below = edge_flags()
    top_row = lax.broadcasted_iota(jnp.int32, halo.shape[1:], 0) == 0
    for k in range(layers + 3):
        halo[k] = jnp.where(
            top_row,
            jnp.broadcast_to(above[k : k + 1, :], halo.shape[1:]),
            jnp.broadcast_to(below[k : k + 1, :], halo.shape[1:]),
        )
    halo_live = jnp.where(top_row, has_above, has_below)

    def factor(get):
        multiplier, inverse = [None], []
        horiz = get(layers + 2)
        low = get(0)
        for k in range(layers):
            high = get(k + 1) if k + 1 < layers else jnp.zeros_like(low)
            pivot = low + high + 4.0 * horiz
            if k > 0:
                pivot = pivot - low * multiplier[k]
            inverse.append(1.0 / pivot)
            multiplier.append(high * inverse[k])
            low = high
        return multiplier, inverse

    def bed_row(multiplier, inverse):
        swept = [jnp.ones_like(inverse[0])]
        for k in range(1, layers):
            swept.append(multiplier[k] * swept[k - 1])
        solved = [None] * layers
        solved[layers - 1] = swept[layers - 1] * inverse[layers - 1]
        for k in range(layers - 2, -1, -1):
            solved[k] = swept[k] * inverse[k] + multiplier[k + 1] * solved[k + 1]
        return solved

    halo_multiplier, halo_inverse = factor(lambda k: halo[k])
    halo_scale = halo[layers] * halo[layers + 2] * halo_live
    for k, value in enumerate(bed_row(halo_multiplier, halo_inverse)):
        halo[k] = value * halo_scale
    multiplier, inverse = factor(lambda k: planes[k])
    weight = planes[layers]
    spread = weight * planes[layers + 2]
    for k, value in enumerate(bed_row(multiplier, inverse)):
        weights[4, k] = value
    for direction in (UP, DOWN, LEFT, RIGHT):
        source = []
        for k in range(layers):
            edge = None
            if direction == UP:
                edge = halo[k, 0:1, :]
            if direction == DOWN:
                edge = halo[k, 1:2, :]
            source.append(moved(weights[4, k] * spread, direction, edge))
        for k, value in enumerate(chip_solve(source, multiplier, inverse)):
            weights[direction, k] = value
    for k in range(layers):
        weights[4, k] = weights[4, k] * weight
    for copy in copies:
        copy.wait()

    def step(f, carry):
        values = [gathered[m, f] for m in range(half)]

        def total(kind):
            out = values[0] * weights[kind, side * half]
            for m in range(1, half):
                out = out + values[m] * weights[kind, side * half + m]
            return out

        to_up, to_down = total(UP), total(DOWN)
        here = total(4) + moved(to_up, DOWN) + moved(to_down, UP)
        here = here + moved(total(LEFT), RIGHT) + moved(total(RIGHT), LEFT)
        terms[f] = here
        outer[0, pl.ds(f, 1), :] = to_up[0:1]
        outer[1, pl.ds(f, 1), :] = to_down[rows - 1 : rows]
        return carry

    lax.fori_loop(0, functionals, step, 0)

    groups_low = lax.broadcasted_iota(jnp.int32, (LANES, width), 0)
    blocks = GROUPS // LANES

    def grouped(values, labels):
        label = labels.astype(jnp.int32)
        parts = []
        for b in range(blocks):
            inside = jnp.broadcast_to((label // LANES) == b, values.shape)
            parts.append(jnp.where(inside, values, 0.0))
        left = jnp.concatenate(parts, axis=0)
        high = left.astype(jnp.bfloat16)
        rest = left - high.astype(jnp.float32)
        middle = rest.astype(jnp.bfloat16)
        low = (rest - middle.astype(jnp.float32)).astype(jnp.bfloat16)
        left = jnp.concatenate([high, middle, low], axis=0)
        match = jnp.where(jnp.broadcast_to(label % LANES, groups_low.shape) == groups_low, 1.0, 0.0)
        return lax.dot_general(
            left,
            match.astype(jnp.bfloat16),
            (((1,), (1,)), ((), ())),
            preferred_element_type=jnp.float32,
        )

    total = grouped(outer[0], above[layers + 1 : layers + 2, :])
    total = total + grouped(outer[1], below[layers + 1 : layers + 2, :])
    for y in range(rows):
        total = total + grouped(terms[:, y, :], planes[layers + 1, y : y + 1, :])
    size = blocks * functionals
    total = (total[0:size] + total[size : 2 * size] + total[2 * size :]) * scale
    sums[...] = jnp.zeros_like(sums)
    start = pl.multiple_of(core * functionals, functionals)
    for b in range(blocks):
        sums[pl.ds(start, functionals), b * LANES : (b + 1) * LANES] = total[
            b * functionals : (b + 1) * functionals
        ]


def middle_kernel(local, planes, halo_up, halo_down, base, message, factors):
    side, _ = position()
    layers = planes.shape[0] - 3
    half, functionals, rows, _ = local.shape
    has_above, has_below = edge_flags()
    multiplier, inverse, _ = chip_factors(lambda k: planes[k], side, layers)
    for j in range(half):
        factors[0, j] = multiplier[j + 1]
        factors[1, j] = inverse[j]
    inner = (half - 1) * functionals
    message[functionals * rows : functionals * (rows + 1), :] = halo_up[inner : inner + functionals, :]
    message[functionals * (rows + 1) :, :] = halo_down[inner : inner + functionals, :]

    def step(f, carry):
        horiz = planes[layers + 2]
        residual = []
        for j in range(half):
            here = local[j, f]
            around = moved(here, UP, halo_up[pl.ds(j * functionals + f, 1), :] * has_above)
            around = around + moved(here, DOWN, halo_down[pl.ds(j * functionals + f, 1), :] * has_below)
            around = around + moved(here, LEFT) + moved(here, RIGHT)
            residual.append(horiz * around)
        solved = chip_solve(
            residual,
            [None] + [factors[0, j] for j in range(half)],
            [factors[1, j] for j in range(half)],
        )
        for j in range(half):
            solved[j] = local[j, f] + solved[j]
            base[j, f] = solved[j]
        message[pl.ds(pl.multiple_of(f * rows, rows), rows), :] = solved[half - 1]
        return carry

    lax.fori_loop(0, functionals, step, 0)


def coefficient_kernel(planes, above, below, spread, spread_other, response, ends, halo, halo_response):
    side, _ = position()
    layers = planes.shape[0] - 3
    half = layers // 2
    has_above, has_below = edge_flags()
    top_row = lax.broadcasted_iota(jnp.int32, halo.shape[1:], 0) == 0
    for k in range(layers + 3):
        halo[k] = jnp.where(
            top_row,
            jnp.broadcast_to(above[k : k + 1, :], halo.shape[1:]),
            jnp.broadcast_to(below[k : k + 1, :], halo.shape[1:]),
        )
    halo_live = jnp.where(top_row, has_above, has_below)

    def both(get):
        multiplier, inverse, kappa = chip_factors(get, side, layers)
        unit = unit_response(multiplier, inverse)
        multiplier_other, inverse_other, _ = chip_factors(get, 1 - side, layers)
        unit_other = unit_response(multiplier_other, inverse_other)
        mine, other = kappa * unit[half - 1], kappa * unit_other[half - 1]
        return multiplier, inverse, kappa, unit, unit_other, (mine, other, 1.0 / (1.0 - mine * other))

    _, _, kappa, unit, unit_other, corner = both(lambda k: halo[k])
    rows_halo = halo.shape[1]
    for i in range(3):
        ends[i + 3, 0:rows_halo] = corner[i] * halo_live if i == 2 else corner[i]
    for j in range(half):
        halo_response[0, j] = kappa * unit[j] * halo_live
        halo_response[1, j] = kappa * unit_other[j] * halo_live
    multiplier, inverse, kappa, unit, unit_other, corner = both(lambda k: planes[k])
    for i in range(3):
        ends[i] = corner[i]
    horiz = planes[layers + 2]
    mine = [kappa * unit[j] for j in range(half)]
    other = [kappa * unit_other[j] for j in range(half)]
    for j in range(half):
        response[j] = mine[j]
    for direction in (UP, DOWN, LEFT, RIGHT):
        source, total = [], jnp.zeros_like(horiz)
        for j in range(half):
            edges = (None, None)
            if direction in (UP, DOWN):
                edges = tuple(halo_response[i, j, direction : direction + 1, :] for i in range(2))
            source.append(horiz * moved(mine[j], direction, edges[0]))
            total = total + unit_other[j] * moved(other[j], direction, edges[1])
        spread_other[direction] = horiz * total
        for j, value in enumerate(chip_solve(source, multiplier, inverse)):
            spread[direction, j] = value


def final_kernel(
    base, boundary, boundary_other, message, halo_up, halo_down, spread, spread_other, response, ends,
    kept, sent, halo_mine, halo_other,
):
    side, core = position()
    half, functionals, rows, _ = base.shape
    held = half // 2
    inner = (half - 1) * functionals
    for i, rows_in in enumerate((halo_up, halo_down)):
        near = rows_in[inner : inner + functionals, :]
        start = functionals * (rows + i)
        far = message[start : start + functionals, :]
        mine, other, inverse = (ends[k, i : i + 1, :] for k in (3, 4, 5))
        live = jnp.where(inverse == 0.0, 0.0, 1.0)
        value = (far + other * near) * inverse
        halo_other[i] = value
        halo_mine[i] = (near + mine * value) * live

    def step(f, carry):
        near = boundary[f]
        mine, other, inverse = ends[0], ends[1], ends[2]
        value = (boundary_other[f] + other * near) * inverse
        value_mine = near + mine * value

        def around(plane, edges):
            return [
                moved(plane, UP, edges[0, pl.ds(f, 1), :]),
                moved(plane, DOWN, edges[1, pl.ds(f, 1), :]),
                moved(plane, LEFT),
                moved(plane, RIGHT),
            ]

        value_around = around(value, halo_other)
        mine_around = around(value_mine, halo_mine)
        last = base[half - 1, f]
        last_other = message[pl.ds(pl.multiple_of(f * rows, rows), rows), :]
        for d in range(4):
            last = last + spread[d, half - 1] * value_around[d]
            last_other = last_other + spread_other[d] * mine_around[d]
        second = (last_other + other * last) * inverse
        for group in range(2):
            solved = []
            for i in range(held):
                m = group * held + i
                j = jnp.where(side == 0, m, half - 1 - m)
                out = base[j, f] + response[j] * second
                for d in range(4):
                    out = out + spread[d, j] * value_around[d]
                solved.append(out)

            @pl.when(core == group)
            def _():
                for i in range(held):
                    kept[i, core * functionals + f] = solved[i]

            @pl.when(core != group)
            def _():
                for i in range(held):
                    sent[i, f] = solved[i]

        return carry

    lax.fori_loop(0, functionals, step, 0)


def call(kernel, out_shapes, scratch=(), any_inputs=0, **cost):
    def run(*operands):
        in_specs = [
            pl.BlockSpec(memory_space=pl.ANY if i < any_inputs else pltpu.VMEM)
            for i in range(len(operands))
        ]
        return pl.pallas_call(
            kernel,
            out_shape=[jax.ShapeDtypeStruct(s, jnp.float32) for s in out_shapes],
            in_specs=in_specs,
            out_specs=[pl.BlockSpec(memory_space=pltpu.VMEM) for _ in out_shapes],
            scratch_shapes=list(scratch),
            compiler_params=pltpu.CompilerParams(vmem_limit_bytes=VMEM_BYTES),
            cost_estimate=pl.CostEstimate(
                flops=cost.get("flops", 1000000), bytes_accessed=2000000, transcendentals=0
            ),
        )(*operands)

    return run


def shards(forcing, vert_coupling, horiz_coupling, basal_velocity, group_label, ice_mask):
    layers, rows, width_block = vert_coupling.shape
    held, functionals_all, _, width = forcing.shape
    half, functionals = layers // 2, functionals_all // 2
    tiles = lax.axis_size("tile")
    core = lax.axis_index("layer") % 2
    f32 = jnp.float32

    def across(array, bits):
        return lax.ppermute(array, "layer", [(i, i ^ bits) for i in range(4)])

    def to_next(array):
        return lax.ppermute(array, "tile", [(i, (i + 1) % tiles) for i in range(tiles)])

    def to_previous(array):
        return lax.ppermute(array, "tile", [((i + 1) % tiles, i) for i in range(tiles)])

    weight = vert_coupling[0] * basal_velocity * ice_mask.astype(f32)
    block = jnp.concatenate([vert_coupling, weight[None], group_label.astype(f32)[None]], axis=0)
    block_cross = across(block, 2)
    block_peer = across(block, 1)
    forcing_sent = lax.dynamic_slice_in_dim(forcing, (1 - core) * functionals, functionals, 1)
    forcing_received = across(forcing_sent, 1)
    block_diag = across(block_cross, 1)

    count = layers + 3
    edge_rows = -(-count // 8) * 8
    planes, plane_first, plane_last = call(
        assemble_kernel, [(count, rows, width), (edge_rows, width), (edge_rows, width)]
    )(block, block_peer, block_cross, block_diag, horiz_coupling)
    above = to_next(plane_last)
    below = to_previous(plane_first)

    gathered = pltpu.VMEM((half, functionals, rows, width), f32)
    factors = pltpu.VMEM((2, half, rows, width), f32)
    stack = half * functionals
    local, boundary, local_first, local_last = call(
        local_kernel,
        [(half, functionals, rows, width), (functionals, rows, width), (stack, width), (stack, width)],
        [gathered, factors, pltpu.SemaphoreType.DMA((2,))],
        any_inputs=2,
    )(forcing, forcing_received, planes)
    boundary_other = across(boundary, 2)
    halo_up = to_next(local_last)
    halo_down = to_previous(local_first)

    columns_all = tiles * rows * width
    halo_planes = pltpu.VMEM((count, 8, width), f32)
    (sums,) = call(
        functools.partial(column_kernel, scale=-((columns_all / GROUPS) ** -0.5)),
        [(functionals_all, GROUPS)],
        [
            gathered,
            pltpu.VMEM((5, layers, rows, width), f32),
            halo_planes,
            pltpu.VMEM((functionals, rows, width), f32),
            pltpu.VMEM((2, functionals, width), f32),
            pltpu.SemaphoreType.DMA((2,)),
        ],
        any_inputs=2,
    )(forcing, forcing_received, planes, above, below)

    sums = sums + across(sums, 1)
    sums = sums + across(sums, 3)
    step = 1
    while step < tiles:
        pairs = [(4 * t + i, 4 * (t ^ step) + (i ^ 1)) for t in range(tiles) for i in range(4)]
        sums = sums + lax.ppermute(sums, ("tile", "layer"), pairs)
        step *= 2

    spread, spread_other, response, ends = call(
        coefficient_kernel,
        [(4, half, rows, width), (4, rows, width), (half, rows, width), (6, rows, width)],
        [halo_planes, pltpu.VMEM((2, half, 8, width), f32)],
    )(planes, above, below)

    base, message = call(
        middle_kernel,
        [(half, functionals, rows, width), (functionals * (rows + 2), width)],
        [factors],
    )(local, planes, halo_up, halo_down)
    message_other = across(message, 2)

    kept, sent = call(
        final_kernel,
        [(held, functionals_all, rows, width), (held, functionals, rows, width)],
        [pltpu.VMEM((2, functionals, width), f32), pltpu.VMEM((2, functionals, width), f32)],
    )(base, boundary, boundary_other, message_other, halo_up, halo_down, spread, spread_other, response, ends)
    received = across(sent, 1)
    adjoint = lax.dynamic_update_slice_in_dim(kept, received, (1 - core) * functionals, 1)
    return (adjoint, sums)


def solution(mesh):
    in_specs = (
        P("layer", None, "tile", None),
        P(None, "tile", "layer"),
        P("tile", None),
        P("tile", "layer"),
        P("tile", "layer"),
        P("tile", "layer"),
    )
    out_specs = (P("layer", None, "tile", None), P())
    return jax.shard_map(shards, mesh=mesh, in_specs=in_specs, out_specs=out_specs, check_vma=False)
```

time: 219 us -> 54.8 us (0.25)
  blocking collectives: 63.2 us -> 0 us
  local copies, waits for them, and re-layouts: 60.2 us -> 2.36 us
  other arithmetic: 39.6 us -> 2.2 us
  waiting for transfers between devices: 32.6 us -> 20.6 us
  Pallas kernels: 0 us -> 6.78 us
  starting transfers between devices: 17.3 us -> 21.2 us
    psum x1 -> x0, blocking collectives: 46.3 us -> none  [shards(): totals = lax.psum(partial_sums, ('tile', 'layer'))]
    unnamed x25 -> x14, local copies, waits for them, and re-layouts: 33.5 us -> 1.15 us
    all_to_all x3 -> x0, waiting for transfers between devices: 27.2 us -> none  [the longest x2 27.2 us: to_columns(): lax.all_to_all(field, 'layer', split_axis=3, concat_axis=0, tiled=True)]
    dynamic_update_slice x96 -> x0, other arithmetic: 26.4 us -> none  [column_solve(): lax.scan(forward, start, (sub_diag, full_diag, super_diag, rhs))]
    all_to_all x1 -> x0, blocking collectives: 16.9 us -> none  [to_layers(): lax.all_to_all(field, 'layer', split_axis=0, concat_axis=3, tiled=True)]
    all_to_all x6 -> x0, local copies, waits for them, and re-layouts: 16.1 us -> none  [the longest x3 13.9 us: to_columns(): lax.all_to_all(field, 'layer', split_axis=3, concat_axis=0, tiled=True)]
    ppermute x2 -> x16, starting transfers between devices: 5.76 us -> 21.2 us  [the longest x9 7.57 us: across(): return lax.ppermute(array, 'layer', [(i, i ^ bits) for i in range(4)])]
    ppermute x2 -> x16, waiting for transfers between devices: 5.38 us -> 20.6 us  [the longest x3 7.18 us: shards(): sums = sums + lax.ppermute(sums, ('tile', 'layer'), pairs)]
  transfers between devices with their start and end apart: 5 -> 16, of which waited for: 4 -> 10; matrix products, arithmetic and copies ran while one was open for 2% -> 4% of each run, Pallas kernels for 0% -> 5%
where the time goes in v1:
time: 54.8 us; the launch traced here: 54 us
  starting transfers between devices  21.2 us (39%)
  waiting for transfers between devices  20.6 us (38%)
  Pallas kernels  6.78 us (12%)
  local copies, waits for them, and re-layouts  2.36 us (4%)
  other arithmetic  2.2 us (4%)
  between operations  0.79 us (1%)
    ppermute x9, starting transfers between devices, across(): return lax.ppermute(array, 'layer', [(i, i ^ bits) for i in range(4)])  7.57 us
    ppermute x2, starting transfers between devices, to_previous(): lax.ppermute(array, 'tile', [((i + 1) % tiles, i) for i in range(tiles)])  7.54 us
    ppermute x3, waiting for transfers between devices, shards(): sums = sums + lax.ppermute(sums, ('tile', 'layer'), pairs)  7.18 us
    pallas_call x6, Pallas kernels, run(): pl.pallas_call(kernel, out_shape=[jax.ShapeDtypeStruct(s, jnp.float32) fo...  6.78 us
    ppermute x9, waiting for transfers between devices, across(): return lax.ppermute(array, 'layer', [(i, i ^ bits) for i in range(4)])  6.37 us
    ppermute x2, waiting for transfers between devices, to_next(): lax.ppermute(array, 'tile', [(i, (i + 1) % tiles) for i in range(tiles)])  5.92 us
    ppermute x3, starting transfers between devices, shards(): sums = sums + lax.ppermute(sums, ('tile', 'layer'), pairs)  3.74 us
    ppermute x2, starting transfers between devices, to_next(): lax.ppermute(array, 'tile', [(i, (i + 1) % tiles) for i in range(tiles)])  2.38 us
  transfers between devices with their start and end apart: 16, of which 10 were waited for; matrix products, arithmetic and copies ran while one was open for 4% of the time, Pallas kernels for 5%

profile of v1, /device:TPU:0, one launch (start us, length us, event | category | flops | bytes accessed | tf_op | source)
XLA Modules:
  0.0 54.0 jit_solution(3854757439527923617)
XLA Ops:
  0.7 1.2 %constant_dynamic-slice_fusion = f32[4,8,8,512]{3,2,1,0:T(8,128)S(1)} fusion(f32[4,16,8,512]{3,2,1,0:T(8,128)} %own.3, s32[]{:T(128)S(6)} %select_n.12), kind=kLoop, calls=%fused_computation.6 | loop fusion | bytes 1048580 | tf_op jit(solution)/shard_map/dynamic_slice | solution.py:458
  1.8 0.0 copy-start.3
  1.8 0.0 copy-start.4
  1.9 0.5 collective-permute-start
  2.4 0.1 copy-done.3
  2.5 0.0 copy-done.4
  2.5 0.7 %fusion.1 = f32[1,8,128]{2,1,0:T(8,128)S(1)} fusion(f32[8,128]{1,0:T(8,128)S(1)} %copy-done.3, s32[8,128]{1,0:T(8,128)S(1)} %copy-done.4, f32[16,8,128]{2,1,0:T(8,128)} %param.7), kind=kLoop, calls=%fused_computation.3 | loop fusion | flops 3072 | bytes 16384 | tf_op jit(solution)/shard_map/broadcast_in_dim | solution.py:455
  3.2 0.9 %pad_maximum_fusion.own = f32[18,8,128]{2,1,0:T(8,128)S(1)} fusion(f32[1,8,128]{2,1,0:T(8,128)S(1)} %convert_bitcast_fusion, f32[1,8,128]{2,1,0:T(8,128)S(1)} %fusion.1, f32[16,8,128]{2,1,0:T(8,128)} %param.7), kind=kLoop, calls=%fused_computation | loop fusion | flops 36864 | bytes 147456 | tf_op jit(solution)/shard_map/concatenate | solution.py:455
  4.1 2.9 %collective-permute-start.2 = (f32[18,8,128]{2,1,0:T(8,128)S(1)}, f32[18,8,128]{2,1,0:T(8,128)S(1)}, u32[]{:S(2)}, u32[]{:S(2)}) collective-permute-start(f32[18,8,128]{2,1,0:T(8,128)S(1)} %pad_maximum_fusion.own), channel_id=1, source_target_pairs={{0,2},{1,3},{2,0},{3,1},{4,6},{5,7},{6,4},{7,5},{8,10},{9,11},{10,... | collective-permute-start | bytes 221192 | tf_op jit(solution)/shard_map/ppermute | solution.py:446
  7.0 0.0 collective-permute-start.1
  7.0 2.3 %collective-permute-done.2.cross = f32[18,8,128]{2,1,0:T(8,128)S(1)} collective-permute-done((f32[18,8,128]{2,1,0:T(8,128)S(1)}, f32[18,8,128]{2,1,0:T(8,128)S(1)}, u32[]{:S(2)}, u32[]{:S(2)}) %collective-permute-start.2) | collective-permute-done | bytes 73760 | tf_op jit(solution)/shard_map/ppermute | solution.py:446
  9.4 0.0 collective-permute-start.3
  9.4 0.0 collective-permute-done.1.peer
  9.4 1.3 %collective-permute-done.3.diag = f32[18,8,128]{2,1,0:T(8,128)S(1)} collective-permute-done((f32[18,8,128]{2,1,0:T(8,128)S(1)}, f32[18,8,128]{2,1,0:T(8,128)S(1)}, u32[]{:S(2)}, u32[]{:S(2)}) %collective-permute-start.3) | collective-permute-done | bytes 73760 | tf_op jit(solution)/shard_map/ppermute | solution.py:446
  10.6 0.1 shard_map.77
  10.7 0.0 collective-permute-done.received
  10.7 0.6 %shard_map.78 = (f32[8,8,8,512]{3,2,1,0:T(8,128)S(1)}, f32[8,8,512]{2,1,0:T(8,128)S(1)}, f32[64,512]{1,0:T(8,128)S(1)}, f32[64,512]{1,0:T(8,128)S(1)}) custom-call(f32[4,16,8,512]{3,2,1,0:T(8,128)S(1)} %copy-done, f32[4,8,8,512]{3,2,1,0:T(8,128)S(1)} %collective-permute-done.received, f32[19,8,512]{2,1,0:T(8,128)S(1)} %get-tuple-element.17.planes), custom_call_target="tpu_custom_call" | custom-call | flops 1000000 | bytes 2000000 | tf_op jit(solution)/shard_map/pallas_call | solution.py:422
  11.3 2.1 %collective-permute-start.4 = (f32[64,512]{1,0:T(8,128)S(1)}, f32[64,512]{1,0:T(8,128)S(1)}, u32[]{:S(2)}, u32[]{:S(2)}) collective-permute-start(f32[64,512]{1,0:T(8,128)S(1)} %get-tuple-element.19), channel_id=1, source_target_pairs={{0,4},{4,8},{8,12},{12,16},{16,20},{20,24},{24,28},{28,0},{1,5},{5... | collective-permute-start | bytes 393224 | tf_op jit(solution)/shard_map/ppermute | solution.py:449
  13.4 3.1 %collective-permute-start.5 = (f32[64,512]{1,0:T(8,128)S(1)}, f32[64,512]{1,0:T(8,128)S(1)}, u32[]{:S(2)}, u32[]{:S(2)}) collective-permute-start(f32[64,512]{1,0:T(8,128)S(1)} %get-tuple-element.20), channel_id=1, source_target_pairs={{4,0},{8,4},{12,8},{16,12},{20,16},{24,20},{28,24},{0,28},{5,1},{9... | collective-permute-start | bytes 393224 | tf_op jit(solution)/shard_map/ppermute | solution.py:452
  16.5 3.9 %collective-permute-done.4.halo_up = f32[64,512]{1,0:T(8,128)S(1)} collective-permute-done((f32[64,512]{1,0:T(8,128)S(1)}, f32[64,512]{1,0:T(8,128)S(1)}, u32[]{:S(2)}, u32[]{:S(2)}) %collective-permute-start.4) | collective-permute-done | bytes 131104 | tf_op jit(solution)/shard_map/ppermute | solution.py:449
  20.4 1.1 %collective-permute-done.5.halo_down = f32[64,512]{1,0:T(8,128)S(1)} collective-permute-done((f32[64,512]{1,0:T(8,128)S(1)}, f32[64,512]{1,0:T(8,128)S(1)}, u32[]{:S(2)}, u32[]{:S(2)}) %collective-permute-start.5) | collective-permute-done | bytes 131104 | tf_op jit(solution)/shard_map/ppermute | solution.py:452
  21.5 1.3 %shard_map.79 = (f32[8,8,8,512]{3,2,1,0:T(8,128)S(1)}, f32[80,512]{1,0:T(8,128)S(1)}) custom-call(f32[8,8,8,512]{3,2,1,0:T(8,128)S(1)} %get-tuple-element.18.local, f32[19,8,512]{2,1,0:T(8,128)S(1)} %get-tuple-element.17.planes, f32[64,512]{1,0:T(8,128)S(1)} %collective-permute-done.4.halo_up, f32[64,512]{1,0:T(8,128)S(1)} %collective-permute-done.5.halo_down), custom_call_target="tpu_custom_call" | custom-call | flops 1000000 | bytes 2000000 | tf_op jit(solution)/shard_map/pallas_call | solution.py:422
  22.8 1.6 %collective-permute-start.7 = (f32[80,512]{1,0:T(8,128)S(1)}, f32[80,512]{1,0:T(8,128)S(1)}, u32[]{:S(2)}, u32[]{:S(2)}) collective-permute-start(f32[80,512]{1,0:T(8,128)S(1)} %get-tuple-element.23), channel_id=1, source_target_pairs={{0,2},{1,3},{2,0},{3,1},{4,6},{5,7},{6,4},{7,5},{8,10},{9,11},{10,... | collective-permute-start | bytes 491528 | tf_op jit(solution)/shard_map/ppermute | solution.py:446
  24.4 0.5 collective-permute-start.6
  24.9 0.3 collective-permute-start.8
  25.2 4.4 %collective-permute-start.9 = (f32[24,512]{1,0:T(8,128)S(1)}, f32[24,512]{1,0:T(8,128)S(1)}, u32[]{:S(2)}, u32[]{:S(2)}) collective-permute-start(f32[24,512]{1,0:T(8,128)S(1)} %get-tuple-element.25), channel_id=1, source_target_pairs={{4,0},{8,4},{12,8},{16,12},{20,16},{24,20},{28,24},{0,28},{5,1},{9... | collective-permute-start | bytes 147464 | tf_op jit(solution)/shard_map/ppermute | solution.py:452
  29.6 2.1 %collective-permute-done.8.above = f32[24,512]{1,0:T(8,128)S(1)} collective-permute-done((f32[24,512]{1,0:T(8,128)S(1)}, f32[24,512]{1,0:T(8,128)S(1)}, u32[]{:S(2)}, u32[]{:S(2)}) %collective-permute-start.8) | collective-permute-done | bytes 49184 | tf_op jit(solution)/shard_map/ppermute | solution.py:449
  31.7 0.0 collective-permute-done.9.below
  31.7 0.4 shard_map.80
  32.1 0.0 collective-permute-done.6.boundary_other
  32.1 0.0 collective-permute-done.7.message
  32.1 2.2 %shard_map.81 = (f32[4,16,8,512]{3,2,1,0:T(8,128)}, f32[4,8,8,512]{3,2,1,0:T(8,128)S(1)}) custom-call(f32[8,8,8,512]{3,2,1,0:T(8,128)S(1)} %get-tuple-element.21.base, f32[8,8,512]{2,1,0:T(8,128)S(1)} %get-tuple-element.22.boundary, f32[8,8,512]{2,1,0:T(8,128)S(1)} %collective-permute-done.6.boundary_other, f32[80,512]{1,0:T(8,128)S(1)} %collective-permute-done.7.message, ...), custom_call_target="tpu_custom_call" | custom-call | flops 1000000 | bytes 2000000 | tf_op jit(solution)/shard_map/pallas_call | solution.py:422
  34.3 0.0 collective-permute-start.10
  34.3 2.3 %shard_map.82 = f32[16,512]{1,0:T(8,128)S(1)} custom-call(f32[4,16,8,512]{3,2,1,0:T(8,128)S(1)} %copy-done, f32[4,8,8,512]{3,2,1,0:T(8,128)S(1)} %collective-permute-done.received, f32[19,8,512]{2,1,0:T(8,128)S(1)} %get-tuple-element.17.planes, f32[24,512]{1,0:T(8,128)S(1)} %collective-permute-done.8.above, f32[24,512]{1,0:T(8,128)S(1)} %collective-permute-done.9.below), custom_call_target="tpu_custom_call" | custom-call | flops 1000000 | bytes 2000000 | tf_op jit(solution)/shard_map/pallas_call | solution.py:422
  36.6 0.6 %collective-permute-start.11 = (f32[16,512]{1,0:T(8,128)S(1)}, f32[16,512]{1,0:T(8,128)S(1)}, u32[]{:S(2)}, u32[]{:S(2)}) collective-permute-start(f32[16,512]{1,0:T(8,128)S(1)} %shard_map.82), channel_id=1, source_target_pairs={{0,1},{1,0},{2,3},{3,2},{4,5},{5,4},{6,7},{7,6},{8,9},{9,8},{10,11... | collective-permute-start | bytes 98312 | tf_op jit(solution)/shard_map/ppermute | solution.py:446
  37.1 0.9 %collective-permute-done.11 = f32[16,512]{1,0:T(8,128)S(1)} collective-permute-done((f32[16,512]{1,0:T(8,128)S(1)}, f32[16,512]{1,0:T(8,128)S(1)}, u32[]{:S(2)}, u32[]{:S(2)}) %collective-permute-start.11) | collective-permute-done | bytes 32800 | tf_op jit(solution)/shard_map/ppermute | solution.py:446
  38.0 1.4 %collective-permute-start.12 = (f32[16,512]{1,0:T(8,128)S(1)}, f32[16,512]{1,0:T(8,128)S(1)}, u32[]{:S(2)}, u32[]{:S(2)}) collective-permute-start(f32[16,512]{1,0:T(8,128)S(1)} %add.25), channel_id=1, source_target_pairs={{0,3},{1,2},{2,1},{3,0},{4,7},{5,6},{6,5},{7,4},{8,11},{9,10},{10,... | collective-permute-start | bytes 98312 | tf_op jit(solution)/shard_map/ppermute | solution.py:446
  39.5 1.9 %collective-permute-done.12 = f32[16,512]{1,0:T(8,128)S(1)} collective-permute-done((f32[16,512]{1,0:T(8,128)S(1)}, f32[16,512]{1,0:T(8,128)S(1)}, u32[]{:S(2)}, u32[]{:S(2)}) %collective-permute-start.12) | collective-permute-done | bytes 32800 | tf_op jit(solution)/shard_map/ppermute | solution.py:446
  41.4 0.8 %collective-permute-start.13 = (f32[16,512]{1,0:T(8,128)S(1)}, f32[16,512]{1,0:T(8,128)S(1)}, u32[]{:S(2)}, u32[]{:S(2)}) collective-permute-start(f32[16,512]{1,0:T(8,128)S(1)} %add.26), channel_id=1, source_target_pairs={{0,5},{1,4},{2,7},{3,6},{4,1},{5,0},{6,3},{7,2},{8,13},{9,12},{10,... | collective-permute-start | bytes 98312 | tf_op jit(solution)/shard_map/ppermute | solution.py:504
  42.2 2.5 %collective-permute-done.13 = f32[16,512]{1,0:T(8,128)S(1)} collective-permute-done((f32[16,512]{1,0:T(8,128)S(1)}, f32[16,512]{1,0:T(8,128)S(1)}, u32[]{:S(2)}, u32[]{:S(2)}) %collective-permute-start.13) | collective-permute-done | bytes 32800 | tf_op jit(solution)/shard_map/ppermute | solution.py:504
  44.7 0.9 %collective-permute-start.14 = (f32[16,512]{1,0:T(8,128)S(1)}, f32[16,512]{1,0:T(8,128)S(1)}, u32[]{:S(2)}, u32[]{:S(2)}) collective-permute-start(f32[16,512]{1,0:T(8,128)S(1)} %add.27), channel_id=1, source_target_pairs={{0,9},{1,8},{2,11},{3,10},{4,13},{5,12},{6,15},{7,14},{8,1},{9,0},... | collective-permute-start | bytes 98312 | tf_op jit(solution)/shard_map/ppermute | solution.py:504
  45.6 2.5 %collective-permute-done.14 = f32[16,512]{1,0:T(8,128)S(1)} collective-permute-done((f32[16,512]{1,0:T(8,128)S(1)}, f32[16,512]{1,0:T(8,128)S(1)}, u32[]{:S(2)}, u32[]{:S(2)}) %collective-permute-start.14) | collective-permute-done | bytes 32800 | tf_op jit(solution)/shard_map/ppermute | solution.py:504
  48.1 2.0 %collective-permute-start.15 = (f32[16,512]{1,0:T(8,128)S(1)}, f32[16,512]{1,0:T(8,128)S(1)}, u32[]{:S(2)}, u32[]{:S(2)}) collective-permute-start(f32[16,512]{1,0:T(8,128)S(1)} %add.28), channel_id=1, source_target_pairs={{0,17},{1,16},{2,19},{3,18},{4,21},{5,20},{6,23},{7,22},{8,25},{9,... | collective-permute-start | bytes 98312 | tf_op jit(solution)/shard_map/ppermute | solution.py:504
  50.1 2.2 %collective-permute-done.15 = f32[16,512]{1,0:T(8,128)S(1)} collective-permute-done((f32[16,512]{1,0:T(8,128)S(1)}, f32[16,512]{1,0:T(8,128)S(1)}, u32[]{:S(2)}, u32[]{:S(2)}) %collective-permute-start.15) | collective-permute-done | bytes 32800 | tf_op jit(solution)/shard_map/ppermute | solution.py:504
  52.3 0.6 %add.29 = f32[16,512]{1,0:T(8,128)} add(f32[16,512]{1,0:T(8,128)S(1)} %add.28, f32[16,512]{1,0:T(8,128)S(1)} %collective-permute-done.15) | non-fusion elementwise | flops 8192 | bytes 98304 | tf_op jit(solution)/shard_map/add | solution.py:504
  52.9 0.0 collective-permute-done.10
  53.0 0.0 copy-start.6
  53.0 1.0 %copy-done.6 = f32[4,16,8,512]{3,2,1,0:T(8,128)} copy-done((f32[4,16,8,512]{3,2,1,0:T(8,128)}, f32[4,16,8,512]{3,2,1,0:T(8,128)S(1)}, u32[]{:S(2)}) %copy-start.6) | copy-done | bytes 1048600
  (14 shorter events, 0.1 us)
Async XLA Ops:
  0.6 10.1 %copy-start = (f32[4,16,8,512]{3,2,1,0:T(8,128)S(1)}, f32[4,16,8,512]{3,2,1,0:T(8,128)}, u32[]{:S(2)}) copy-start(f32[4,16,8,512]{3,2,1,0:T(8,128)} %own.3) | copy-start | bytes 3145732
  0.7 1.7 %copy-start.2 = (s32[8,128]{1,0:T(8,128)S(1)}, s32[8,128]{1,0:T(8,128)}, u32[]{:S(2)}) copy-start(s32[8,128]{1,0:T(8,128)} %param.10) | copy-start | bytes 12292
  1.8 0.7 %copy-start.3 = (f32[8,128]{1,0:T(8,128)S(1)}, f32[8,128]{1,0:T(8,128)}, u32[]{:S(2)}) copy-start(f32[8,128]{1,0:T(8,128)} %param.9) | copy-start | bytes 12292
  1.8 0.7 %copy-start.4 = (s32[8,128]{1,0:T(8,128)S(1)}, s32[8,128]{1,0:T(8,128)}, u32[]{:S(2)}) copy-start(s32[8,128]{1,0:T(8,128)} %param.11) | copy-start | bytes 12292
  1.9 8.9 %collective-permute-start = (f32[4,8,8,512]{3,2,1,0:T(8,128)S(1)}, f32[4,8,8,512]{3,2,1,0:T(8,128)S(1)}, u32[]{:S(2)}, u32[]{:S(2)}) collective-permute-start(f32[4,8,8,512]{3,2,1,0:T(8,128)S(1)} %constant_dynamic-slice_fusion), channel_id=1, source_target_pairs={{0,1},{1,0},{2,3},{3,2},{4,5},{5,4},{6,7},{7,6},{8,9},{9,8},{10,11... | collective-permute-start | bytes 1572872 | tf_op jit(solution)/shard_map/ppermute | solution.py:446
  3.2 7.4 %copy-start.1 = (f32[8,512]{1,0:T(8,128)S(1)}, f32[8,512]{1,0:T(8,128)}, u32[]{:S(2)}) copy-start(f32[8,512]{1,0:T(8,128)} %horiz.1) | copy-start | bytes 49156
  4.1 5.3 %collective-permute-start.2 = (f32[18,8,128]{2,1,0:T(8,128)S(1)}, f32[18,8,128]{2,1,0:T(8,128)S(1)}, u32[]{:S(2)}, u32[]{:S(2)}) collective-permute-start(f32[18,8,128]{2,1,0:T(8,128)S(1)} %pad_maximum_fusion.own), channel_id=1, source_target_pairs={{0,2},{1,3},{2,0},{3,1},{4,6},{5,7},{6,4},{7,5},{8,10},{9,11},{10,... | collective-permute-start | bytes 221192 | tf_op jit(solution)/shard_map/ppermute | solution.py:446
  7.0 2.3 %collective-permute-start.1 = (f32[18,8,128]{2,1,0:T(8,128)S(1)}, f32[18,8,128]{2,1,0:T(8,128)S(1)}, u32[]{:S(2)}, u32[]{:S(2)}) collective-permute-start(f32[18,8,128]{2,1,0:T(8,128)S(1)} %pad_maximum_fusion.own), channel_id=1, source_target_pairs={{0,1},{1,0},{2,3},{3,2},{4,5},{5,4},{6,7},{7,6},{8,9},{9,8},{10,11... | collective-permute-start | bytes 221192 | tf_op jit(solution)/shard_map/ppermute | solution.py:446
  9.4 1.3 %collective-permute-start.3 = (f32[18,8,128]{2,1,0:T(8,128)S(1)}, f32[18,8,128]{2,1,0:T(8,128)S(1)}, u32[]{:S(2)}, u32[]{:S(2)}) collective-permute-start(f32[18,8,128]{2,1,0:T(8,128)S(1)} %collective-permute-done.2.cross), channel_id=1, source_target_pairs={{0,1},{1,0},{2,3},{3,2},{4,5},{5,4},{6,7},{7,6},{8,9},{9,8},{10,11... | collective-permute-start | bytes 221192 | tf_op jit(solution)/shard_map/ppermute | solution.py:446
  11.3 9.1 %collective-permute-start.4 = (f32[64,512]{1,0:T(8,128)S(1)}, f32[64,512]{1,0:T(8,128)S(1)}, u32[]{:S(2)}, u32[]{:S(2)}) collective-permute-start(f32[64,512]{1,0:T(8,128)S(1)} %get-tuple-element.19), channel_id=1, source_target_pairs={{0,4},{4,8},{8,12},{12,16},{16,20},{20,24},{24,28},{28,0},{1,5},{5... | collective-permute-start | bytes 393224 | tf_op jit(solution)/shard_map/ppermute | solution.py:449
  13.4 8.1 %collective-permute-start.5 = (f32[64,512]{1,0:T(8,128)S(1)}, f32[64,512]{1,0:T(8,128)S(1)}, u32[]{:S(2)}, u32[]{:S(2)}) collective-permute-start(f32[64,512]{1,0:T(8,128)S(1)} %get-tuple-element.20), channel_id=1, source_target_pairs={{4,0},{8,4},{12,8},{16,12},{20,16},{24,20},{28,24},{0,28},{5,1},{9... | collective-permute-start | bytes 393224 | tf_op jit(solution)/shard_map/ppermute | solution.py:452
  22.8 9.3 %collective-permute-start.7 = (f32[80,512]{1,0:T(8,128)S(1)}, f32[80,512]{1,0:T(8,128)S(1)}, u32[]{:S(2)}, u32[]{:S(2)}) collective-permute-start(f32[80,512]{1,0:T(8,128)S(1)} %get-tuple-element.23), channel_id=1, source_target_pairs={{0,2},{1,3},{2,0},{3,1},{4,6},{5,7},{6,4},{7,5},{8,10},{9,11},{10,... | collective-permute-start | bytes 491528 | tf_op jit(solution)/shard_map/ppermute | solution.py:446
  24.4 7.8 %collective-permute-start.6 = (f32[8,8,512]{2,1,0:T(8,128)S(1)}, f32[8,8,512]{2,1,0:T(8,128)S(1)}, u32[]{:S(2)}, u32[]{:S(2)}) collective-permute-start(f32[8,8,512]{2,1,0:T(8,128)S(1)} %get-tuple-element.22.boundary), channel_id=1, source_target_pairs={{0,2},{1,3},{2,0},{3,1},{4,6},{5,7},{6,4},{7,5},{8,10},{9,11},{10,... | collective-permute-start | bytes 393224 | tf_op jit(solution)/shard_map/ppermute | solution.py:446
  24.9 6.8 %collective-permute-start.8 = (f32[24,512]{1,0:T(8,128)S(1)}, f32[24,512]{1,0:T(8,128)S(1)}, u32[]{:S(2)}, u32[]{:S(2)}) collective-permute-start(f32[24,512]{1,0:T(8,128)S(1)} %get-tuple-element.24), channel_id=1, source_target_pairs={{0,4},{4,8},{8,12},{12,16},{16,20},{20,24},{24,28},{28,0},{1,5},{5... | collective-permute-start | bytes 147464 | tf_op jit(solution)/shard_map/ppermute | solution.py:449
  25.2 6.5 %collective-permute-start.9 = (f32[24,512]{1,0:T(8,128)S(1)}, f32[24,512]{1,0:T(8,128)S(1)}, u32[]{:S(2)}, u32[]{:S(2)}) collective-permute-start(f32[24,512]{1,0:T(8,128)S(1)} %get-tuple-element.25), channel_id=1, source_target_pairs={{4,0},{8,4},{12,8},{16,12},{20,16},{24,20},{28,24},{0,28},{5,1},{9... | collective-permute-start | bytes 147464 | tf_op jit(solution)/shard_map/ppermute | solution.py:452
  34.3 18.6 %copy-start.5 = (f32[4,16,8,512]{3,2,1,0:T(8,128)S(1)}, f32[4,16,8,512]{3,2,1,0:T(8,128)}, u32[]{:S(2)}) copy-start(f32[4,16,8,512]{3,2,1,0:T(8,128)} %get-tuple-element.30) | copy-start | bytes 3145732
  34.3 18.6 %collective-permute-start.10 = (f32[4,8,8,512]{3,2,1,0:T(8,128)S(1)}, f32[4,8,8,512]{3,2,1,0:T(8,128)S(1)}, u32[]{:S(2)}, u32[]{:S(2)}) collective-permute-start(f32[4,8,8,512]{3,2,1,0:T(8,128)S(1)} %get-tuple-element.31), channel_id=1, source_target_pairs={{0,1},{1,0},{2,3},{3,2},{4,5},{5,4},{6,7},{7,6},{8,9},{9,8},{10,11... | collective-permute-start | bytes 1572872 | tf_op jit(solution)/shard_map/ppermute | solution.py:446
  36.6 1.4 %collective-permute-start.11 = (f32[16,512]{1,0:T(8,128)S(1)}, f32[16,512]{1,0:T(8,128)S(1)}, u32[]{:S(2)}, u32[]{:S(2)}) collective-permute-start(f32[16,512]{1,0:T(8,128)S(1)} %shard_map.82), channel_id=1, source_target_pairs={{0,1},{1,0},{2,3},{3,2},{4,5},{5,4},{6,7},{7,6},{8,9},{9,8},{10,11... | collective-permute-start | bytes 98312 | tf_op jit(solution)/shard_map/ppermute | solution.py:446
  38.0 3.3 %collective-permute-start.12 = (f32[16,512]{1,0:T(8,128)S(1)}, f32[16,512]{1,0:T(8,128)S(1)}, u32[]{:S(2)}, u32[]{:S(2)}) collective-permute-start(f32[16,512]{1,0:T(8,128)S(1)} %add.25), channel_id=1, source_target_pairs={{0,3},{1,2},{2,1},{3,0},{4,7},{5,6},{6,5},{7,4},{8,11},{9,10},{10,... | collective-permute-start | bytes 98312 | tf_op jit(solution)/shard_map/ppermute | solution.py:446
  41.4 3.3 %collective-permute-start.13 = (f32[16,512]{1,0:T(8,128)S(1)}, f32[16,512]{1,0:T(8,128)S(1)}, u32[]{:S(2)}, u32[]{:S(2)}) collective-permute-start(f32[16,512]{1,0:T(8,128)S(1)} %add.26), channel_id=1, source_target_pairs={{0,5},{1,4},{2,7},{3,6},{4,1},{5,0},{6,3},{7,2},{8,13},{9,12},{10,... | collective-permute-start | bytes 98312 | tf_op jit(solution)/shard_map/ppermute | solution.py:504
  44.7 3.3 %collective-permute-start.14 = (f32[16,512]{1,0:T(8,128)S(1)}, f32[16,512]{1,0:T(8,128)S(1)}, u32[]{:S(2)}, u32[]{:S(2)}) collective-permute-start(f32[16,512]{1,0:T(8,128)S(1)} %add.27), channel_id=1, source_target_pairs={{0,9},{1,8},{2,11},{3,10},{4,13},{5,12},{6,15},{7,14},{8,1},{9,0},... | collective-permute-start | bytes 98312 | tf_op jit(solution)/shard_map/ppermute | solution.py:504
  48.1 4.2 %collective-permute-start.15 = (f32[16,512]{1,0:T(8,128)S(1)}, f32[16,512]{1,0:T(8,128)S(1)}, u32[]{:S(2)}, u32[]{:S(2)}) collective-permute-start(f32[16,512]{1,0:T(8,128)S(1)} %add.28), channel_id=1, source_target_pairs={{0,17},{1,16},{2,19},{3,18},{4,21},{5,20},{6,23},{7,22},{8,25},{9,... | collective-permute-start | bytes 98312 | tf_op jit(solution)/shard_map/ppermute | solution.py:504
  53.0 1.0 %copy-start.6 = (f32[4,16,8,512]{3,2,1,0:T(8,128)}, f32[4,16,8,512]{3,2,1,0:T(8,128)S(1)}, u32[]{:S(2)}) copy-start(f32[4,16,8,512]{3,2,1,0:T(8,128)S(1)} %constant_dynamic-update-slice_fusion) | copy-start | bytes 3145732

commit v2 on v1

v2 whole, which is shorter than its diff:
```python
import functools

import jax
import jax.numpy as jnp
from jax import lax
from jax.experimental import pallas as pl
from jax.experimental.pallas import tpu as pltpu
from jax.sharding import PartitionSpec as P

GROUPS = 512
LANES = 128
VMEM_BYTES = 32 * 1024 * 1024
UP, DOWN, LEFT, RIGHT = range(4)


def position():
    layer = lax.axis_index("layer")
    return layer // 2, layer % 2


def owned_half():
    side, core = position()
    tile = lax.axis_index("tile")
    total = side + core
    for bit in range((lax.axis_size("tile") - 1).bit_length()):
        total = total + lax.shift_right_logical(tile, bit) % 2
    return total % 2


def edge_flags():
    tile = lax.axis_index("tile")
    last = lax.axis_size("tile") - 1
    return (
        jnp.where(tile > 0, 1.0, 0.0).astype(jnp.float32),
        jnp.where(tile < last, 1.0, 0.0).astype(jnp.float32),
    )


def paired_rows(first, last):
    even = lax.axis_index("tile") % 2 == 0
    return jnp.where(even, last, first), jnp.where(even, first, last)


def halo_rows(near, far):
    even = lax.axis_index("tile") % 2 == 0
    return jnp.where(even, far, near), jnp.where(even, near, far)


def moved(plane, direction, halo=None):
    rows, width = plane.shape
    axis = 0 if direction in (UP, DOWN) else 1
    size = plane.shape[axis]
    first = direction in (UP, LEFT)
    rolled = pltpu.roll(plane, 1 if first else size - 1, axis)
    at_edge = lax.broadcasted_iota(jnp.int32, plane.shape, axis) == (0 if first else size - 1)
    filler = jnp.zeros_like(plane) if halo is None else jnp.broadcast_to(halo, plane.shape)
    return jnp.where(at_edge, filler, rolled)


def chip_factors(planes, side, layers):
    half = layers // 2
    horiz = planes(layers + 2)

    def coupling(j):
        if j == 0:
            return planes(0) * jnp.where(side == 0, 1.0, 0.0)
        return planes(jnp.where(side == 0, j, layers - j))

    multiplier, inverse = [None], []
    below = coupling(0)
    for j in range(half):
        above = coupling(j + 1)
        pivot = below + above + 4.0 * horiz
        if j > 0:
            pivot = pivot - below * multiplier[j]
        inverse.append(1.0 / pivot)
        multiplier.append(above * inverse[j])
        below = above
    return multiplier, inverse, below


def unit_response(multiplier, inverse):
    half = len(inverse)
    response = [None] * half
    response[half - 1] = inverse[half - 1]
    for j in range(half - 2, -1, -1):
        response[j] = multiplier[j + 1] * response[j + 1]
    return response


def chip_solve(values, multiplier, inverse):
    half = len(values)
    swept = [values[0]]
    for j in range(1, half):
        swept.append(values[j] + multiplier[j] * swept[j - 1])
    solved = [None] * half
    solved[half - 1] = swept[half - 1] * inverse[half - 1]
    for j in range(half - 2, -1, -1):
        solved[j] = swept[j] * inverse[j] + multiplier[j + 1] * solved[j + 1]
    return solved


def pack_kernel(
    coupling, velocity, label, mask, forcing, block, sent, kept, velocity_in, label_in, mask_in, sems
):
    mine = owned_half()
    layers = coupling.shape[0]
    functionals = sent.shape[1]
    pairs = [
        (coupling, block.at[pl.ds(0, layers)]),
        (velocity, velocity_in),
        (label, label_in),
        (mask, mask_in),
    ]
    for target, which in ((sent, 1 - mine), (kept, mine)):
        pairs.append((forcing.at[:, pl.ds(which * functionals, functionals)], target))
    copies = [pltpu.make_async_copy(a, b, sems.at[i]) for i, (a, b) in enumerate(pairs)]
    for copy in copies:
        copy.start()
    for copy in copies[:4]:
        copy.wait()
    block[layers] = block[0] * velocity_in[...] * mask_in[...].astype(jnp.float32)
    block[layers + 1] = label_in[...].astype(jnp.float32)
    for copy in copies[4:]:
        copy.wait()


def place_kernel(kept, received, mine_sums, other_sums, out, sums, sems):
    mine = owned_half()
    functionals = kept.shape[1]
    copies = []
    for i, (source, group, which) in enumerate(((received, other_sums, 1 - mine), (kept, mine_sums, mine))):
        at = pl.ds(pl.multiple_of(which * functionals, functionals), functionals)
        copies.append(pltpu.make_async_copy(source, out.at[:, at], sems.at[2 * i]))
        copies.append(pltpu.make_async_copy(group, sums.at[at], sems.at[2 * i + 1]))
    for copy in copies:
        copy.start()
    for copy in copies:
        copy.wait()


def assemble_kernel(own, peer, cross, diag, horiz, planes, row_near, row_far):
    layer = lax.axis_index("layer")
    count, rows = own.shape[0], own.shape[1]
    for k, block in ((0, own), (1, peer), (3, cross), (2, diag)):
        start = pl.multiple_of(jnp.bitwise_xor(layer, k) * LANES, LANES)
        planes[0:count, :, pl.ds(start, LANES)] = block[...]
    planes[count] = horiz[...]
    for k in range(row_near.shape[0]):
        at = min(k, count)
        near, far = paired_rows(planes[at, 0:1, :], planes[at, rows - 1 : rows, :])
        row_near[k : k + 1, :] = near
        row_far[k : k + 1, :] = far


def load_forcing(own, received, gathered, sems):
    _, core = position()
    held = received.shape[0]
    copies = (
        pltpu.make_async_copy(own, gathered.at[pl.ds(core * held, held)], sems.at[0]),
        pltpu.make_async_copy(received, gathered.at[pl.ds((1 - core) * held, held)], sems.at[1]),
    )
    for copy in copies:
        copy.start()
    return copies


def local_kernel(own, received, planes, local, boundary, row_near, row_far, gathered, factors, sems):
    side, _ = position()
    copies = load_forcing(own, received, gathered, sems)
    layers = planes.shape[0] - 3
    half, functionals, rows, _ = local.shape
    multiplier, inverse, _ = chip_factors(lambda k: planes[k], side, layers)
    for j in range(half):
        factors[0, j] = multiplier[j + 1]
        factors[1, j] = inverse[j]
    for copy in copies:
        copy.wait()

    def step(f, carry):
        values = [gathered[side * (half - 1) + (1 - 2 * side) * j, f] for j in range(half)]
        solved = chip_solve(
            values,
            [None] + [factors[0, j] for j in range(half)],
            [factors[1, j] for j in range(half)],
        )
        for j in range(half):
            local[j, f] = solved[j]
            near, far = paired_rows(solved[j][0:1], solved[j][rows - 1 : rows])
            row_near[pl.ds(j * functionals + f, 1), :] = near
            row_far[pl.ds(j * functionals + f, 1), :] = far
        boundary[f] = solved[half - 1]
        return carry

    lax.fori_loop(0, functionals, step, 0)


def full_factors(get, layers):
    multiplier, inverse = [None], []
    horiz = get(layers + 2)
    low = get(0)
    for k in range(layers):
        high = get(k + 1) if k + 1 < layers else jnp.zeros_like(low)
        pivot = low + high + 4.0 * horiz
        if k > 0:
            pivot = pivot - low * multiplier[k]
        inverse.append(1.0 / pivot)
        multiplier.append(high * inverse[k])
        low = high
    return multiplier, inverse


def bed_row(multiplier, inverse):
    layers = len(inverse)
    swept = [jnp.ones_like(inverse[0])]
    for k in range(1, layers):
        swept.append(multiplier[k] * swept[k - 1])
    solved = [None] * layers
    solved[layers - 1] = swept[layers - 1] * inverse[layers - 1]
    for k in range(layers - 2, -1, -1):
        solved[k] = swept[k] * inverse[k] + multiplier[k + 1] * solved[k + 1]
    return solved


def grouped(values, labels):
    label = labels.astype(jnp.int32)
    parts = []
    for b in range(GROUPS // LANES):
        inside = jnp.broadcast_to((label // LANES) == b, values.shape)
        parts.append(jnp.where(inside, values, 0.0))
    left = jnp.concatenate(parts, axis=0)
    high = left.astype(jnp.bfloat16)
    rest = left - high.astype(jnp.float32)
    middle = rest.astype(jnp.bfloat16)
    low = (rest - middle.astype(jnp.float32)).astype(jnp.bfloat16)
    left = jnp.concatenate([high, middle, low], axis=0)
    place = lax.broadcasted_iota(jnp.int32, (LANES, values.shape[1]), 0)
    match = jnp.where(jnp.broadcast_to(label % LANES, place.shape) == place, 1.0, 0.0)
    return lax.dot_general(
        left,
        match.astype(jnp.bfloat16),
        (((1,), (1,)), ((), ())),
        preferred_element_type=jnp.float32,
    )


def add_groups(sums, total, scale, functionals):
    blocks = GROUPS // LANES
    size = blocks * functionals
    total = (total[0:size] + total[size : 2 * size] + total[2 * size :]) * scale
    for b in range(blocks):
        lanes = slice(b * LANES, (b + 1) * LANES)
        sums[:, lanes] = sums[:, lanes] + total[b * functionals : (b + 1) * functionals]


def column_kernel(own, received, planes, sums, gathered, weights, terms, sems, *, scale):
    side, core = position()
    copies = load_forcing(own, received, gathered, sems)
    layers = planes.shape[0] - 3
    half, functionals, rows, _ = gathered.shape
    multiplier, inverse = full_factors(lambda k: planes[k], layers)
    weight = planes[layers]
    spread = weight * planes[layers + 2]
    for k, value in enumerate(bed_row(multiplier, inverse)):
        weights[4, k] = value
    for direction in (UP, DOWN, LEFT, RIGHT):
        source = [moved(weights[4, k] * spread, direction) for k in range(layers)]
        for k, value in enumerate(chip_solve(source, multiplier, inverse)):
            weights[direction, k] = value
    for k in range(layers):
        weights[4, k] = weights[4, k] * weight
    for copy in copies:
        copy.wait()

    def step(f, carry):
        values = [gathered[m, f] for m in range(half)]

        def total(kind):
            out = values[0] * weights[kind, side * half]
            for m in range(1, half):
                out = out + values[m] * weights[kind, side * half + m]
            return out

        here = total(4) + moved(total(UP), DOWN) + moved(total(DOWN), UP)
        terms[f] = here + moved(total(LEFT), RIGHT) + moved(total(RIGHT), LEFT)
        return carry

    lax.fori_loop(0, functionals, step, 0)
    total = grouped(terms[:, 0, :], planes[layers + 1, 0:1, :])
    for y in range(1, rows):
        total = total + grouped(terms[:, y, :], planes[layers + 1, y : y + 1, :])
    sums[...] = jnp.zeros_like(sums)
    add_groups(sums, total, scale, functionals)


def border_kernel(own, received, planes, near, far, inside, sums, halo, *, scale):
    side, core = position()
    layers = planes.shape[0] - 3
    held, functionals, rows, width = received.shape
    top_row = lax.broadcasted_iota(jnp.int32, halo.shape[1:], 0) == 0
    has_above, has_below = edge_flags()

    def pair(above, below):
        return jnp.where(
            top_row, jnp.broadcast_to(above, halo.shape[1:]), jnp.broadcast_to(below, halo.shape[1:])
        )

    for k in range(layers + 3):
        halo[k] = pair(*halo_rows(near[k : k + 1, :], far[k : k + 1, :]))
    outer = bed_row(*full_factors(lambda k: halo[k], layers))
    live = halo[layers] * halo[layers + 2] * jnp.where(top_row, has_above, has_below)
    edge = full_factors(lambda k: pair(planes[k, 0:1, :], planes[k, rows - 1 : rows, :]), layers)
    solved = chip_solve([value * live for value in outer], *edge)
    sums[...] = inside[...]
    total = None
    for which, row in enumerate((0, rows - 1)):
        out = None
        for m in range(2 * held):
            weight = jnp.where(side == 0, solved[m][which : which + 1], solved[2 * held + m][which : which + 1])
            mine, other = own[m % held, :, row, :], received[m % held, :, row, :]
            value = jnp.where(core == m // held, mine, other) * weight
            out = value if out is None else out + value
        part = grouped(out, halo[layers + 1, which : which + 1, :])
        total = part if total is None else total + part
    add_groups(sums, total, scale, functionals)


def fold_kernel(mine, *refs):
    parts, message, out = refs[:-2], refs[-2], refs[-1]
    total = mine[...]
    if parts:
        total = total + parts[0][...]
    if len(parts) == 3:
        total = total + (parts[1][...] + parts[2][...])
    size = mine.shape[0]
    out[out.shape[0] - size :, :] = total


def middle_kernel(local, planes, near, far, base, message, factors):
    side, _ = position()
    layers = planes.shape[0] - 3
    half, functionals, rows, _ = local.shape
    has_above, has_below = edge_flags()
    multiplier, inverse, _ = chip_factors(lambda k: planes[k], side, layers)
    for j in range(half):
        factors[0, j] = multiplier[j + 1]
        factors[1, j] = inverse[j]
    inner = (half - 1) * functionals
    above, below = halo_rows(near[inner : inner + functionals, :], far[inner : inner + functionals, :])
    message[functionals * rows : functionals * (rows + 1), :] = above
    message[functionals * (rows + 1) : functionals * (rows + 2), :] = below

    def step(f, carry):
        horiz = planes[layers + 2]
        residual = []
        for j in range(half):
            here = local[j, f]
            at = pl.ds(j * functionals + f, 1)
            above, below = halo_rows(near[at, :], far[at, :])
            around = moved(here, UP, above * has_above) + moved(here, DOWN, below * has_below)
            around = around + moved(here, LEFT) + moved(here, RIGHT)
            residual.append(horiz * around)
        solved = chip_solve(
            residual,
            [None] + [factors[0, j] for j in range(half)],
            [factors[1, j] for j in range(half)],
        )
        for j in range(half):
            solved[j] = local[j, f] + solved[j]
            base[j, f] = solved[j]
        message[pl.ds(pl.multiple_of(f * rows, rows), rows), :] = solved[half - 1]
        return carry

    lax.fori_loop(0, functionals, step, 0)


def coefficient_kernel(planes, halo, spread, spread_other, response, ends, halo_response):
    side, _ = position()
    layers = planes.shape[0] - 3
    half = layers // 2
    has_above, has_below = edge_flags()
    top_row = lax.broadcasted_iota(jnp.int32, halo.shape[1:], 0) == 0
    halo_live = jnp.where(top_row, has_above, has_below)

    def both(get):
        multiplier, inverse, kappa = chip_factors(get, side, layers)
        unit = unit_response(multiplier, inverse)
        multiplier_other, inverse_other, _ = chip_factors(get, 1 - side, layers)
        unit_other = unit_response(multiplier_other, inverse_other)
        mine, other = kappa * unit[half - 1], kappa * unit_other[half - 1]
        return multiplier, inverse, kappa, unit, unit_other, (mine, other, 1.0 / (1.0 - mine * other))

    _, _, kappa, unit, unit_other, corner = both(lambda k: halo[k])
    rows_halo = halo.shape[1]
    for i in range(3):
        ends[i + 3, 0:rows_halo] = corner[i] * halo_live if i == 2 else corner[i]
    for j in range(half):
        halo_response[0, j] = kappa * unit[j] * halo_live
        halo_response[1, j] = kappa * unit_other[j] * halo_live
    multiplier, inverse, kappa, unit, unit_other, corner = both(lambda k: planes[k])
    for i in range(3):
        ends[i] = corner[i]
    horiz = planes[layers + 2]
    mine = [kappa * unit[j] for j in range(half)]
    other = [kappa * unit_other[j] for j in range(half)]
    for j in range(half):
        response[j] = mine[j]
    for direction in (UP, DOWN, LEFT, RIGHT):
        source, total = [], jnp.zeros_like(horiz)
        for j in range(half):
            edges = (None, None)
            if direction in (UP, DOWN):
                edges = tuple(halo_response[i, j, direction : direction + 1, :] for i in range(2))
            source.append(horiz * moved(mine[j], direction, edges[0]))
            total = total + unit_other[j] * moved(other[j], direction, edges[1])
        spread_other[direction] = horiz * total
        for j, value in enumerate(chip_solve(source, multiplier, inverse)):
            spread[direction, j] = value


def interface_kernel(
    base, boundary, boundary_other, message_mine, message, spread, spread_other, ends, near, diag,
    around_all, second_all, sums, halo_mine, halo_other,
):
    half, functionals, rows, _ = base.shape
    last = functionals * (rows + 2)
    sums[...] = message_mine[last:, :] + message[last:, :]
    if near is not None:
        sums[...] = sums[...] + (near[...] + diag[...])
    for i in range(2):
        start = functionals * (rows + i)
        here = message_mine[start : start + functionals, :]
        mine, other, inverse = (ends[k, i : i + 1, :] for k in (3, 4, 5))
        live = jnp.where(inverse == 0.0, 0.0, 1.0)
        value = (message[start : start + functionals, :] + other * here) * inverse
        halo_other[i] = value
        halo_mine[i] = (here + mine * value) * live

    def step(f, carry):
        here = boundary[f]
        mine, other, inverse = ends[0], ends[1], ends[2]
        value = (boundary_other[f] + other * here) * inverse
        value_mine = here + mine * value

        def around(plane, edges):
            return [
                moved(plane, UP, edges[0, pl.ds(f, 1), :]),
                moved(plane, DOWN, edges[1, pl.ds(f, 1), :]),
                moved(plane, LEFT),
                moved(plane, RIGHT),
            ]

        value_around = around(value, halo_other)
        mine_around = around(value_mine, halo_mine)
        last = base[half - 1, f]
        last_other = message[pl.ds(pl.multiple_of(f * rows, rows), rows), :]
        for d in range(4):
            around_all[d, f] = value_around[d]
            last = last + spread[d, half - 1] * value_around[d]
            last_other = last_other + spread_other[d] * mine_around[d]
        second_all[f] = (last_other + other * last) * inverse
        return carry

    lax.fori_loop(0, functionals, step, 0)


def final_kernel(base, around_all, second_all, spread, response, out, *, other_core):
    side, core = position()
    half, functionals = base.shape[0], base.shape[1]
    held = half // 2
    group = 1 - core if other_core else core

    def step(f, carry):
        second = second_all[f]
        value_around = [around_all[d, f] for d in range(4)]
        for i in range(held):
            m = group * held + i
            j = jnp.where(side == 0, m, half - 1 - m)
            value = base[j, f] + response[j] * second
            for d in range(4):
                value = value + spread[d, j] * value_around[d]
            out[i, f] = value
        return carry

    lax.fori_loop(0, functionals, step, 0)


def call(
    kernel, out_shapes, scratch=(), any_inputs=(), hbm_inputs=(), any_outputs=(), aliases=None
):
    def run(*operands):
        spaces = [
            pltpu.HBM if i in hbm_inputs else pl.ANY if i in any_inputs else pltpu.VMEM
            for i in range(len(operands))
        ]
        in_specs = [pl.BlockSpec(memory_space=space) for space in spaces]
        operands = [
            pltpu.with_memory_space_constraint(x, pltpu.HBM) if space is pltpu.HBM else x
            for x, space in zip(operands, spaces)
        ]
        return pl.pallas_call(
            kernel,
            out_shape=[jax.ShapeDtypeStruct(s, jnp.float32) for s in out_shapes],
            in_specs=in_specs,
            out_specs=[
                pl.BlockSpec(memory_space=pl.ANY if i in any_outputs else pltpu.VMEM)
                for i in range(len(out_shapes))
            ],
            scratch_shapes=list(scratch),
            input_output_aliases=aliases or {},
            compiler_params=pltpu.CompilerParams(vmem_limit_bytes=VMEM_BYTES),
        )(*operands)

    return run


def add_parts(values, parts):
    values = values + parts[0]
    return values + (parts[1] + parts[2]) if len(parts) == 3 else values


def after(value, *earlier):
    return lax.optimization_barrier((value, *earlier))[0]


def shards(forcing, vert_coupling, horiz_coupling, basal_velocity, group_label, ice_mask):
    layers, rows, width_block = vert_coupling.shape
    held, functionals_all, _, width = forcing.shape
    half, functionals = layers // 2, functionals_all // 2
    tiles = lax.axis_size("tile")
    f32 = jnp.float32

    def send(array, target):
        pairs = []
        for t in range(tiles):
            for i in range(4):
                u, k = target(t, i)
                pairs.append((4 * t + i, 4 * u + k))
        return lax.ppermute(array, ("tile", "layer"), pairs)

    def across(array, bits):
        return send(array, lambda t, i: (t, i ^ bits))

    def parity(t):
        return bin(t).count("1") % 2

    def to_near(array, bits=None):
        return to_tile(array, bits, lambda t: t ^ 1)

    def to_far(array, bits=None):
        return to_tile(array, bits, lambda t: t + 1 if t % 2 else t - 1)

    def to_tile(array, bits, partner):
        def target(t, i):
            u = partner(t)
            if not 0 <= u < tiles:
                return t, i ^ 1
            return u, i ^ ((parity(t) + parity(u)) % 2 if bits is None else bits)

        return send(array, target)

    def exchange(values, masks):
        kinds = list(masks)
        if len(masks) == 2:
            kinds.append(masks[0] | masks[1])
        return [send(values, lambda t, i: (t ^ d, i ^ (n < 2))) for n, d in enumerate(kinds)]

    dma = pltpu.SemaphoreType.DMA
    count = layers + 3
    edge_rows = -(-count // 8) * 8
    stack = half * functionals
    flat = (rows, width_block)
    quarter = (held, functionals, rows, width)
    join = lax.optimization_barrier
    block, forcing_sent, forcing_kept = call(
        pack_kernel,
        [(layers + 2, *flat), quarter, quarter],
        [pltpu.VMEM(flat, f32), pltpu.VMEM(flat, jnp.int32), pltpu.VMEM(flat, jnp.int32), dma((6,))],
        hbm_inputs=range(5),
    )(vert_coupling, basal_velocity, group_label, ice_mask, forcing)
    cross, peer, forcing_received = join(
        (across(block, 3), across(block, 1), across(forcing_sent, 1))
    )
    diag = across(cross, 1)
    planes, edge_near, edge_far = call(
        assemble_kernel, [(count, rows, width), (edge_rows, width), (edge_rows, width)]
    )(block, peer, cross, diag, horiz_coupling)
    edge_far = to_far(edge_far, 1)
    edge_near = to_near(edge_near, 1)

    gathered = pltpu.VMEM((half, functionals, rows, width), f32)
    factors = pltpu.VMEM((2, half, rows, width), f32)
    columns_all = tiles * rows * width
    scale = -((columns_all / GROUPS) ** -0.5)
    (sums_inside,) = call(
        functools.partial(column_kernel, scale=scale),
        [(functionals, GROUPS)],
        [
            gathered,
            pltpu.VMEM((5, layers, rows, width), f32),
            pltpu.VMEM((functionals, rows, width), f32),
            dma((2,)),
        ],
        any_inputs=(0, 1),
    )(forcing_kept, forcing_received, planes)
    local, boundary, rows_near, rows_far = call(
        local_kernel,
        [(half, functionals, rows, width), (functionals, rows, width), (stack, width), (stack, width)],
        [gathered, factors, dma((2,))],
        any_inputs=(0, 1),
    )(forcing_kept, forcing_received, planes)
    rows_far, rows_near, boundary, edge_near, edge_far = join(
        (rows_far, rows_near, boundary, edge_near, edge_far)
    )
    rows_far = to_far(rows_far)
    rows_near = to_near(rows_near)
    boundary_other = across(boundary, 3)
    sums, halo = call(
        functools.partial(border_kernel, scale=scale),
        [(functionals, GROUPS), (count, 8, width)],
    )(forcing_kept, forcing_received, planes, edge_near, edge_far, sums_inside)

    spread, spread_other, response, ends = call(
        coefficient_kernel,
        [(4, half, rows, width), (4, rows, width), (half, rows, width), (6, rows, width)],
        [pltpu.VMEM((2, half, 8, width), f32)],
    )(planes, halo)

    masks = [1 << bit for bit in range(1, (tiles - 1).bit_length())]
    while len(masks) > 2:
        sums = add_parts(sums, exchange(sums, masks[:2]))
        masks = masks[2:]
    parts = exchange(sums, masks)
    base, message = call(
        middle_kernel,
        [(half, functionals, rows, width), (functionals * (rows + 3), width)],
        [factors],
    )(after(local, spread), planes, rows_near, rows_far)
    (message,) = call(
        fold_kernel,
        [message.shape],
        aliases={len(parts) + 1: 0},
    )(after(sums, boundary_other), *parts, message)
    message_other = across(message, 3)
    sums = message[functionals * (rows + 2) :]
    near = send(sums, lambda t, i: (t ^ 1, i ^ 1))
    diag = send(sums, lambda t, i: (t ^ 1, i ^ 2))
    message_other, near, diag = join((message_other, near, diag))
    halo_rows_both = pltpu.VMEM((2, functionals, width), f32)
    around, second, sums = call(
        interface_kernel,
        [(4, functionals, rows, width), (functionals, rows, width), (functionals, GROUPS)],
        [halo_rows_both, halo_rows_both],
    )(base, boundary, boundary_other, message, message_other, spread, spread_other, ends, near, diag)
    (sent,) = call(functools.partial(final_kernel, other_core=True), [quarter])(
        base, around, second, spread, response
    )
    (kept,) = call(functools.partial(final_kernel, other_core=False), [quarter])(
        base, around, second, spread, response
    )
    received, other_sums, kept = join((across(sent, 1), across(sums, 1), kept))
    adjoint, sums = call(
        place_kernel,
        [(held, functionals_all, rows, width), (functionals_all, GROUPS)],
        [dma((4,))],
        any_inputs=(0, 1, 2, 3),
        any_outputs=(0, 1),
    )(kept, received, sums, other_sums)
    return (adjoint, sums)


def solution(mesh):
    in_specs = (
        P("layer", None, "tile", None),
        P(None, "tile", "layer"),
        P("tile", None),
        P("tile", "layer"),
        P("tile", "layer"),
        P("tile", "layer"),
    )
    out_specs = (P("layer", None, "tile", None), P())
    return jax.shard_map(shards, mesh=mesh, in_specs=in_specs, out_specs=out_specs, check_vma=False)
```

time: 54.8 us -> 40.8 us (0.74); the launches traced: 54 us -> 40.7 us
  waiting for transfers between devices: 20.6 us -> 12.9 us
  starting transfers between devices: 21.2 us -> 18.1 us
  local copies, waits for them, and re-layouts: 2.36 us -> 0.01 us
  other arithmetic: 2.2 us -> 0 us
  Pallas kernels: 6.78 us -> 8.88 us
    ppermute x16 -> x17, waiting for transfers between devices: 20.6 us -> 12.9 us  [send(): return lax.ppermute(array, ('tile', 'layer'), pairs)]
    ppermute x16 -> x17, starting transfers between devices: 21.2 us -> 18.1 us  [send(): return lax.ppermute(array, ('tile', 'layer'), pairs)]
    pallas_call x6 -> x12, Pallas kernels: 6.78 us -> 8.88 us  [run(): pl.pallas_call(kernel, out_shape=[jax.ShapeDtypeStruct(s, jnp.float32) fo...]
    dynamic_slice x1 -> x0, local copies, waits for them, and re-layouts: 1.17 us -> none  [shards(): lax.dynamic_slice_in_dim(forcing, (1 - core) * functionals, functionals, 1)]
    unnamed x14 -> x2, local copies, waits for them, and re-layouts: 1.15 us -> 0.01 us
    concatenate x1 -> x0, other arithmetic: 0.86 us -> none  [shards(): jnp.concatenate([vert_coupling, weight[None], group_label.astype(f32)[Non...]
    broadcast_in_dim x2 -> x0, other arithmetic: 0.69 us -> none  [the longest x1 0.69 us: shards(): weight[None]]
    add x5 -> x0, other arithmetic: 0.65 us -> none  [the longest x3 0.63 us: shards(): sums = sums + lax.ppermute(sums, ('tile', 'layer'), pairs)]
  transfers between devices with their start and end apart: 16 -> 17, of which waited for: 10 -> 7; matrix products, arithmetic and copies ran while one was open for 4% -> 0% of each run, Pallas kernels for 5% -> 13%
where the time goes in v2:
time: 40.8 us; the launch traced here: 40.7 us
  starting transfers between devices  18.1 us (44%)
  waiting for transfers between devices  12.9 us (32%)
  Pallas kernels  8.88 us (22%)
  between operations  0.78 us (2%)
    ppermute x17, starting transfers between devices, send(): return lax.ppermute(array, ('tile', 'layer'), pairs)  18.1 us
    ppermute x17, waiting for transfers between devices, send(): return lax.ppermute(array, ('tile', 'layer'), pairs)  12.9 us
    pallas_call x12, Pallas kernels, run(): pl.pallas_call(kernel, out_shape=[jax.ShapeDtypeStruct(s, jnp.float32) fo...  8.88 us
  transfers between devices with their start and end apart: 17, of which 7 were waited for; matrix products, arithmetic and copies ran while one was open for 0% of the time, Pallas kernels for 13%

profile of v2, /device:TPU:0, one launch (start us, length us, event | category | flops | bytes accessed | tf_op | source)
XLA Modules:
  0.0 40.7 jit_solution(7769285209922955550)
XLA Ops:
  0.6 0.0 copy-start
  0.6 1.3 %shard_map.77 = (f32[18,8,128]{2,1,0:T(8,128)S(1)}, f32[4,8,8,512]{3,2,1,0:T(8,128)S(1)}, f32[4,8,8,512]{3,2,1,0:T(8,128)S(1)}) custom-call(f32[16,8,128]{2,1,0:T(8,128)} %coupling.1, f32[8,128]{1,0:T(8,128)} %velocity.1, s32[8,128]{1,0:T(8,128)} %label.1, s32[8,128]{1,0:T(8,128)} %mask.1, f32[4,16,8,512]{3,2,1,0:T(8,128)} %forcing.1), custom_call_target="tpu_custom_call" | custom-call | tf_op jit(solution)/shard_map/pallas_call | solution.py:501
  2.0 0.5 %collective-permute-start.2 = (f32[4,8,8,512]{3,2,1,0:T(8,128)S(1)}, f32[4,8,8,512]{3,2,1,0:T(8,128)S(1)}, u32[]{:S(2)}, u32[]{:S(2)}) collective-permute-start(f32[4,8,8,512]{3,2,1,0:T(8,128)S(1)} %get-tuple-element.41), channel_id=1, source_target_pairs={{0,1},{1,0},{2,3},{3,2},{4,5},{5,4},{6,7},{7,6},{8,9},{9,8},{10,11... | collective-permute-start | bytes 1572872 | tf_op jit(solution)/shard_map/ppermute | solution.py:539
  2.5 2.6 %collective-permute-start = (f32[18,8,128]{2,1,0:T(8,128)S(1)}, f32[18,8,128]{2,1,0:T(8,128)S(1)}, u32[]{:S(2)}, u32[]{:S(2)}) collective-permute-start(f32[18,8,128]{2,1,0:T(8,128)S(1)} %get-tuple-element.40.own), channel_id=1, source_target_pairs={{0,3},{1,2},{2,1},{3,0},{4,7},{5,6},{6,5},{7,4},{8,11},{9,10},{10,... | collective-permute-start | bytes 221192 | tf_op jit(solution)/shard_map/ppermute | solution.py:539
  5.1 0.1 collective-permute-start.1
  5.2 2.5 %collective-permute-done.cross = f32[18,8,128]{2,1,0:T(8,128)S(1)} collective-permute-done((f32[18,8,128]{2,1,0:T(8,128)S(1)}, f32[18,8,128]{2,1,0:T(8,128)S(1)}, u32[]{:S(2)}, u32[]{:S(2)}) %collective-permute-start) | collective-permute-done | bytes 73760 | tf_op jit(solution)/shard_map/ppermute | solution.py:539
  7.7 0.0 collective-permute-done.1.peer
  7.7 0.0 collective-permute-done.2.received
  7.7 0.1 collective-permute-start.3
  7.8 1.2 %collective-permute-done.3.diag = f32[18,8,128]{2,1,0:T(8,128)S(1)} collective-permute-done((f32[18,8,128]{2,1,0:T(8,128)S(1)}, f32[18,8,128]{2,1,0:T(8,128)S(1)}, u32[]{:S(2)}, u32[]{:S(2)}) %collective-permute-start.3) | collective-permute-done | bytes 73760 | tf_op jit(solution)/shard_map/ppermute | solution.py:539
  9.0 0.0 copy-done
  9.0 0.1 shard_map.78
  9.0 1.5 %collective-permute-start.4 = (f32[24,512]{1,0:T(8,128)S(1)}, f32[24,512]{1,0:T(8,128)S(1)}, u32[]{:S(2)}, u32[]{:S(2)}) collective-permute-start(f32[24,512]{1,0:T(8,128)S(1)} %get-tuple-element.50), channel_id=1, source_target_pairs={{0,5},{1,4},{2,7},{3,6},{4,1},{5,0},{6,3},{7,2},{8,13},{9,12},{10,... | collective-permute-start | bytes 147464 | tf_op jit(solution)/shard_map/ppermute | solution.py:539
  10.5 0.2 collective-permute-start.5
  10.7 0.7 %shard_map.79 = (f32[8,8,8,512]{3,2,1,0:T(8,128)S(1)}, f32[8,8,512]{2,1,0:T(8,128)S(1)}, f32[64,512]{1,0:T(8,128)S(1)}, f32[64,512]{1,0:T(8,128)S(1)}) custom-call(f32[4,8,8,512]{3,2,1,0:T(8,128)S(1)} %get-tuple-element.39.own, f32[4,8,8,512]{3,2,1,0:T(8,128)S(1)} %collective-permute-done.2.received, f32[19,8,512]{2,1,0:T(8,128)S(1)} %get-tuple-element.45.planes), custom_call_target="tpu_custom_call" | custom-call | tf_op jit(solution)/shard_map/pallas_call | solution.py:501
  11.4 1.4 %collective-permute-done.4.near = f32[24,512]{1,0:T(8,128)S(1)} collective-permute-done((f32[24,512]{1,0:T(8,128)S(1)}, f32[24,512]{1,0:T(8,128)S(1)}, u32[]{:S(2)}, u32[]{:S(2)}) %collective-permute-start.4) | collective-permute-done | bytes 49184 | tf_op jit(solution)/shard_map/ppermute | solution.py:539
  12.8 0.0 collective-permute-done.5.far
  12.8 1.2 %collective-permute-start.8 = (f32[8,8,512]{2,1,0:T(8,128)S(1)}, f32[8,8,512]{2,1,0:T(8,128)S(1)}, u32[]{:S(2)}, u32[]{:S(2)}) collective-permute-start(f32[8,8,512]{2,1,0:T(8,128)S(1)} %get-tuple-element.60.boundary), channel_id=1, source_target_pairs={{0,3},{1,2},{2,1},{3,0},{4,7},{5,6},{6,5},{7,4},{8,11},{9,10},{10,... | collective-permute-start | bytes 393224 | tf_op jit(solution)/shard_map/ppermute | solution.py:539
  14.0 2.8 %collective-permute-start.6 = (f32[64,512]{1,0:T(8,128)S(1)}, f32[64,512]{1,0:T(8,128)S(1)}, u32[]{:S(2)}, u32[]{:S(2)}) collective-permute-start(f32[64,512]{1,0:T(8,128)S(1)} %get-tuple-element.57), channel_id=1, source_target_pairs={{0,5},{1,4},{2,7},{3,6},{4,1},{5,0},{6,3},{7,2},{8,13},{9,12},{10,... | collective-permute-start | bytes 393224 | tf_op jit(solution)/shard_map/ppermute | solution.py:539
  16.8 0.2 collective-permute-start.7
  17.0 2.0 %shard_map.80.inside = f32[8,512]{1,0:T(8,128)S(1)} custom-call(f32[4,8,8,512]{3,2,1,0:T(8,128)S(1)} %get-tuple-element.39.own, f32[4,8,8,512]{3,2,1,0:T(8,128)S(1)} %collective-permute-done.2.received, f32[19,8,512]{2,1,0:T(8,128)S(1)} %get-tuple-element.45.planes), custom_call_target="tpu_custom_call" | custom-call | tf_op jit(solution)/shard_map/pallas_call | solution.py:501
  19.0 0.8 %shard_map.81 = (f32[8,512]{1,0:T(8,128)S(1)}, f32[19,8,512]{2,1,0:T(8,128)S(1)}) custom-call(f32[4,8,8,512]{3,2,1,0:T(8,128)S(1)} %get-tuple-element.39.own, f32[4,8,8,512]{3,2,1,0:T(8,128)S(1)} %collective-permute-done.2.received, f32[19,8,512]{2,1,0:T(8,128)S(1)} %get-tuple-element.45.planes, f32[24,512]{1,0:T(8,128)S(1)} %collective-permute-done.4.near, ...), custom_call_target="tpu_custom_call" | custom-call | tf_op jit(solution)/shard_map/pallas_call | solution.py:501
  19.8 1.2 %collective-permute-start.9 = (f32[8,512]{1,0:T(8,128)S(1)}, f32[8,512]{1,0:T(8,128)S(1)}, u32[]{:S(2)}, u32[]{:S(2)}) collective-permute-start(f32[8,512]{1,0:T(8,128)S(1)} %get-tuple-element.62.mine), channel_id=1, source_target_pairs={{0,9},{1,8},{2,11},{3,10},{4,13},{5,12},{6,15},{7,14},{8,1},{9,0},... | collective-permute-start | bytes 49160 | tf_op jit(solution)/shard_map/ppermute | solution.py:539
  21.0 3.9 %collective-permute-start.10 = (f32[8,512]{1,0:T(8,128)S(1)}, f32[8,512]{1,0:T(8,128)S(1)}, u32[]{:S(2)}, u32[]{:S(2)}) collective-permute-start(f32[8,512]{1,0:T(8,128)S(1)} %get-tuple-element.62.mine), channel_id=1, source_target_pairs={{0,17},{1,16},{2,19},{3,18},{4,21},{5,20},{6,23},{7,22},{8,25},{9,... | collective-permute-start | bytes 49160 | tf_op jit(solution)/shard_map/ppermute | solution.py:539
  24.9 0.0 collective-permute-done.8.boundary_other
  24.9 0.0 collective-permute-start.11
  24.9 0.4 shard_map.82
  25.3 0.0 collective-permute-done.6.near
  25.3 0.0 collective-permute-done.7.far
  25.4 1.3 %shard_map.83 = (f32[8,8,8,512]{3,2,1,0:T(8,128)S(1)}, f32[88,512]{1,0:T(8,128)S(1)}) custom-call(f32[8,8,8,512]{3,2,1,0:T(8,128)S(1)} %get-tuple-element.56.local, f32[19,8,512]{2,1,0:T(8,128)S(1)} %get-tuple-element.45.planes, f32[64,512]{1,0:T(8,128)S(1)} %collective-permute-done.6.near, f32[64,512]{1,0:T(8,128)S(1)} %collective-permute-done.7.far), custom_call_target="tpu_custom_call" | custom-call | tf_op jit(solution)/shard_map/pallas_call | solution.py:501
  26.7 0.0 collective-permute-done.9.refs_0_
  26.7 0.0 collective-permute-done.10.refs_1_
  26.7 3.7 %collective-permute-done.11.refs_2_ = f32[8,512]{1,0:T(8,128)S(1)} collective-permute-done((f32[8,512]{1,0:T(8,128)S(1)}, f32[8,512]{1,0:T(8,128)S(1)}, u32[]{:S(2)}, u32[]{:S(2)}) %collective-permute-start.11) | collective-permute-done | bytes 16416 | tf_op jit(solution)/shard_map/ppermute | solution.py:539
  30.5 0.1 collective-permute-start.12
  30.6 0.5 %collective-permute-start.13 = (f32[8,512]{1,0:T(8,128)S(1)}, f32[8,512]{1,0:T(8,128)S(1)}, u32[]{:S(2)}, u32[]{:S(2)}) collective-permute-start(f32[8,512]{1,0:T(8,128)S(1)} %slice.4), channel_id=1, source_target_pairs={{0,5},{1,4},{2,7},{3,6},{4,1},{5,0},{6,3},{7,2},{8,13},{9,12},{10,... | collective-permute-start | bytes 49160 | tf_op jit(solution)/shard_map/ppermute | solution.py:539
  31.1 2.7 %collective-permute-start.14 = (f32[8,512]{1,0:T(8,128)S(1)}, f32[8,512]{1,0:T(8,128)S(1)}, u32[]{:S(2)}, u32[]{:S(2)}) collective-permute-start(f32[8,512]{1,0:T(8,128)S(1)} %slice.4), channel_id=1, source_target_pairs={{0,6},{1,7},{2,4},{3,5},{4,2},{5,3},{6,0},{7,1},{8,14},{9,15},{10,... | collective-permute-start | bytes 49160 | tf_op jit(solution)/shard_map/ppermute | solution.py:539
  33.8 0.0 collective-permute-done.13.near
  33.8 2.5 %collective-permute-done.14.diag = f32[8,512]{1,0:T(8,128)S(1)} collective-permute-done((f32[8,512]{1,0:T(8,128)S(1)}, f32[8,512]{1,0:T(8,128)S(1)}, u32[]{:S(2)}, u32[]{:S(2)}) %collective-permute-start.14) | collective-permute-done | bytes 16416 | tf_op jit(solution)/shard_map/ppermute | solution.py:539
  36.3 0.4 collective-permute-done.12.message
  36.6 0.8 %shard_map.85 = (f32[4,8,8,512]{3,2,1,0:T(8,128)S(1)}, f32[8,8,512]{2,1,0:T(8,128)S(1)}, f32[8,512]{1,0:T(8,128)S(1)}) custom-call(f32[8,8,8,512]{3,2,1,0:T(8,128)S(1)} %get-tuple-element.59.base, f32[8,8,512]{2,1,0:T(8,128)S(1)} %get-tuple-element.60.boundary, f32[8,8,512]{2,1,0:T(8,128)S(1)} %collective-permute-done.8.boundary_other, ...), custom_call_target="tpu_custom_call" | custom-call | tf_op jit(solution)/shard_map/pallas_call | solution.py:501
  37.4 0.3 shard_map.86
  37.7 0.1 collective-permute-start.15
  37.8 0.5 %collective-permute-start.16 = (f32[8,512]{1,0:T(8,128)S(1)}, f32[8,512]{1,0:T(8,128)S(1)}, u32[]{:S(2)}, u32[]{:S(2)}) collective-permute-start(f32[8,512]{1,0:T(8,128)S(1)} %get-tuple-element.72.mine_sums), channel_id=1, source_target_pairs={{0,1},{1,0},{2,3},{3,2},{4,5},{5,4},{6,7},{7,6},{8,9},{9,8},{10,11... | collective-permute-start | bytes 49160 | tf_op jit(solution)/shard_map/ppermute | solution.py:539
  38.3 0.2 shard_map.87.kept
  38.5 1.2 %collective-permute-done.16.other_sums = f32[8,512]{1,0:T(8,128)S(1)} collective-permute-done((f32[8,512]{1,0:T(8,128)S(1)}, f32[8,512]{1,0:T(8,128)S(1)}, u32[]{:S(2)}, u32[]{:S(2)}) %collective-permute-start.16) | collective-permute-done | bytes 16416 | tf_op jit(solution)/shard_map/ppermute | solution.py:539
  39.7 0.0 collective-permute-done.15.received
  39.7 1.0 %shard_map.88 = (f32[4,16,8,512]{3,2,1,0:T(8,128)}, f32[16,512]{1,0:T(8,128)}) custom-call(f32[4,8,8,512]{3,2,1,0:T(8,128)S(1)} %shard_map.87.kept, f32[4,8,8,512]{3,2,1,0:T(8,128)S(1)} %collective-permute-done.15.received, f32[8,512]{1,0:T(8,128)S(1)} %get-tuple-element.72.mine_sums, f32[8,512]{1,0:T(8,128)S(1)} %collective-permute-done.16.other_sums), custom_call_target="tpu_custom_call" | custom-call | tf_op jit(solution)/shard_map/pallas_call | solution.py:501
  (2 shorter events, 0.0 us)
Async XLA Ops:
  0.6 8.3 %copy-start = (f32[8,512]{1,0:T(8,128)S(1)}, f32[8,512]{1,0:T(8,128)}, u32[]{:S(2)}) copy-start(f32[8,512]{1,0:T(8,128)} %horiz.1) | copy-start | bytes 49156
  2.0 5.7 %collective-permute-start.2 = (f32[4,8,8,512]{3,2,1,0:T(8,128)S(1)}, f32[4,8,8,512]{3,2,1,0:T(8,128)S(1)}, u32[]{:S(2)}, u32[]{:S(2)}) collective-permute-start(f32[4,8,8,512]{3,2,1,0:T(8,128)S(1)} %get-tuple-element.41), channel_id=1, source_target_pairs={{0,1},{1,0},{2,3},{3,2},{4,5},{5,4},{6,7},{7,6},{8,9},{9,8},{10,11... | collective-permute-start | bytes 1572872 | tf_op jit(solution)/shard_map/ppermute | solution.py:539
  2.5 5.2 %collective-permute-start = (f32[18,8,128]{2,1,0:T(8,128)S(1)}, f32[18,8,128]{2,1,0:T(8,128)S(1)}, u32[]{:S(2)}, u32[]{:S(2)}) collective-permute-start(f32[18,8,128]{2,1,0:T(8,128)S(1)} %get-tuple-element.40.own), channel_id=1, source_target_pairs={{0,3},{1,2},{2,1},{3,0},{4,7},{5,6},{6,5},{7,4},{8,11},{9,10},{10,... | collective-permute-start | bytes 221192 | tf_op jit(solution)/shard_map/ppermute | solution.py:539
  5.1 2.6 %collective-permute-start.1 = (f32[18,8,128]{2,1,0:T(8,128)S(1)}, f32[18,8,128]{2,1,0:T(8,128)S(1)}, u32[]{:S(2)}, u32[]{:S(2)}) collective-permute-start(f32[18,8,128]{2,1,0:T(8,128)S(1)} %get-tuple-element.40.own), channel_id=1, source_target_pairs={{0,1},{1,0},{2,3},{3,2},{4,5},{5,4},{6,7},{7,6},{8,9},{9,8},{10,11... | collective-permute-start | bytes 221192 | tf_op jit(solution)/shard_map/ppermute | solution.py:539
  7.7 1.3 %collective-permute-start.3 = (f32[18,8,128]{2,1,0:T(8,128)S(1)}, f32[18,8,128]{2,1,0:T(8,128)S(1)}, u32[]{:S(2)}, u32[]{:S(2)}) collective-permute-start(f32[18,8,128]{2,1,0:T(8,128)S(1)} %collective-permute-done.cross), channel_id=1, source_target_pairs={{0,1},{1,0},{2,3},{3,2},{4,5},{5,4},{6,7},{7,6},{8,9},{9,8},{10,11... | collective-permute-start | bytes 221192 | tf_op jit(solution)/shard_map/ppermute | solution.py:539
  9.0 3.8 %collective-permute-start.4 = (f32[24,512]{1,0:T(8,128)S(1)}, f32[24,512]{1,0:T(8,128)S(1)}, u32[]{:S(2)}, u32[]{:S(2)}) collective-permute-start(f32[24,512]{1,0:T(8,128)S(1)} %get-tuple-element.50), channel_id=1, source_target_pairs={{0,5},{1,4},{2,7},{3,6},{4,1},{5,0},{6,3},{7,2},{8,13},{9,12},{10,... | collective-permute-start | bytes 147464 | tf_op jit(solution)/shard_map/ppermute | solution.py:539
  10.5 2.3 %collective-permute-start.5 = (f32[24,512]{1,0:T(8,128)S(1)}, f32[24,512]{1,0:T(8,128)S(1)}, u32[]{:S(2)}, u32[]{:S(2)}) collective-permute-start(f32[24,512]{1,0:T(8,128)S(1)} %get-tuple-element.51), channel_id=1, source_target_pairs={{0,1},{1,0},{2,3},{3,2},{4,9},{5,8},{6,11},{7,10},{8,5},{9,4},{10,... | collective-permute-start | bytes 147464 | tf_op jit(solution)/shard_map/ppermute | solution.py:539
  12.8 12.1 %collective-permute-start.8 = (f32[8,8,512]{2,1,0:T(8,128)S(1)}, f32[8,8,512]{2,1,0:T(8,128)S(1)}, u32[]{:S(2)}, u32[]{:S(2)}) collective-permute-start(f32[8,8,512]{2,1,0:T(8,128)S(1)} %get-tuple-element.60.boundary), channel_id=1, source_target_pairs={{0,3},{1,2},{2,1},{3,0},{4,7},{5,6},{6,5},{7,4},{8,11},{9,10},{10,... | collective-permute-start | bytes 393224 | tf_op jit(solution)/shard_map/ppermute | solution.py:539
  14.0 11.3 %collective-permute-start.6 = (f32[64,512]{1,0:T(8,128)S(1)}, f32[64,512]{1,0:T(8,128)S(1)}, u32[]{:S(2)}, u32[]{:S(2)}) collective-permute-start(f32[64,512]{1,0:T(8,128)S(1)} %get-tuple-element.57), channel_id=1, source_target_pairs={{0,5},{1,4},{2,7},{3,6},{4,1},{5,0},{6,3},{7,2},{8,13},{9,12},{10,... | collective-permute-start | bytes 393224 | tf_op jit(solution)/shard_map/ppermute | solution.py:539
  16.8 8.5 %collective-permute-start.7 = (f32[64,512]{1,0:T(8,128)S(1)}, f32[64,512]{1,0:T(8,128)S(1)}, u32[]{:S(2)}, u32[]{:S(2)}) collective-permute-start(f32[64,512]{1,0:T(8,128)S(1)} %get-tuple-element.58), channel_id=1, source_target_pairs={{0,1},{1,0},{2,3},{3,2},{4,8},{5,9},{6,10},{7,11},{8,4},{9,5},{10,... | collective-permute-start | bytes 393224 | tf_op jit(solution)/shard_map/ppermute | solution.py:539
  19.8 6.9 %collective-permute-start.9 = (f32[8,512]{1,0:T(8,128)S(1)}, f32[8,512]{1,0:T(8,128)S(1)}, u32[]{:S(2)}, u32[]{:S(2)}) collective-permute-start(f32[8,512]{1,0:T(8,128)S(1)} %get-tuple-element.62.mine), channel_id=1, source_target_pairs={{0,9},{1,8},{2,11},{3,10},{4,13},{5,12},{6,15},{7,14},{8,1},{9,0},... | collective-permute-start | bytes 49160 | tf_op jit(solution)/shard_map/ppermute | solution.py:539
  21.0 5.7 %collective-permute-start.10 = (f32[8,512]{1,0:T(8,128)S(1)}, f32[8,512]{1,0:T(8,128)S(1)}, u32[]{:S(2)}, u32[]{:S(2)}) collective-permute-start(f32[8,512]{1,0:T(8,128)S(1)} %get-tuple-element.62.mine), channel_id=1, source_target_pairs={{0,17},{1,16},{2,19},{3,18},{4,21},{5,20},{6,23},{7,22},{8,25},{9,... | collective-permute-start | bytes 49160 | tf_op jit(solution)/shard_map/ppermute | solution.py:539
  24.9 5.5 %collective-permute-start.11 = (f32[8,512]{1,0:T(8,128)S(1)}, f32[8,512]{1,0:T(8,128)S(1)}, u32[]{:S(2)}, u32[]{:S(2)}) collective-permute-start(f32[8,512]{1,0:T(8,128)S(1)} %get-tuple-element.62.mine), channel_id=1, source_target_pairs={{0,24},{1,25},{2,26},{3,27},{4,28},{5,29},{6,30},{7,31},{8,16},{9,... | collective-permute-start | bytes 49160 | tf_op jit(solution)/shard_map/ppermute | solution.py:539
  30.5 6.2 %collective-permute-start.12 = (f32[88,512]{1,0:T(8,128)S(1)}, f32[88,512]{1,0:T(8,128)S(1)}, u32[]{:S(2)}, u32[]{:S(2)}) collective-permute-start(f32[88,512]{1,0:T(8,128)S(1)} %shard_map.84.message_mine), channel_id=1, source_target_pairs={{0,3},{1,2},{2,1},{3,0},{4,7},{5,6},{6,5},{7,4},{8,11},{9,10},{10,... | collective-permute-start | bytes 540680 | tf_op jit(solution)/shard_map/ppermute | solution.py:539
  30.6 3.2 %collective-permute-start.13 = (f32[8,512]{1,0:T(8,128)S(1)}, f32[8,512]{1,0:T(8,128)S(1)}, u32[]{:S(2)}, u32[]{:S(2)}) collective-permute-start(f32[8,512]{1,0:T(8,128)S(1)} %slice.4), channel_id=1, source_target_pairs={{0,5},{1,4},{2,7},{3,6},{4,1},{5,0},{6,3},{7,2},{8,13},{9,12},{10,... | collective-permute-start | bytes 49160 | tf_op jit(solution)/shard_map/ppermute | solution.py:539
  31.1 5.2 %collective-permute-start.14 = (f32[8,512]{1,0:T(8,128)S(1)}, f32[8,512]{1,0:T(8,128)S(1)}, u32[]{:S(2)}, u32[]{:S(2)}) collective-permute-start(f32[8,512]{1,0:T(8,128)S(1)} %slice.4), channel_id=1, source_target_pairs={{0,6},{1,7},{2,4},{3,5},{4,2},{5,3},{6,0},{7,1},{8,14},{9,15},{10,... | collective-permute-start | bytes 49160 | tf_op jit(solution)/shard_map/ppermute | solution.py:539
  37.7 2.0 %collective-permute-start.15 = (f32[4,8,8,512]{3,2,1,0:T(8,128)S(1)}, f32[4,8,8,512]{3,2,1,0:T(8,128)S(1)}, u32[]{:S(2)}, u32[]{:S(2)}) collective-permute-start(f32[4,8,8,512]{3,2,1,0:T(8,128)S(1)} %shard_map.86), channel_id=1, source_target_pairs={{0,1},{1,0},{2,3},{3,2},{4,5},{5,4},{6,7},{7,6},{8,9},{9,8},{10,11... | collective-permute-start | bytes 1572872 | tf_op jit(solution)/shard_map/ppermute | solution.py:539
  37.8 1.9 %collective-permute-start.16 = (f32[8,512]{1,0:T(8,128)S(1)}, f32[8,512]{1,0:T(8,128)S(1)}, u32[]{:S(2)}, u32[]{:S(2)}) collective-permute-start(f32[8,512]{1,0:T(8,128)S(1)} %get-tuple-element.72.mine_sums), channel_id=1, source_target_pairs={{0,1},{1,0},{2,3},{3,2},{4,5},{5,4},{6,7},{7,6},{8,9},{9,8},{10,11... | collective-permute-start | bytes 49160 | tf_op jit(solution)/shard_map/ppermute | solution.py:539

commit v3 on v2

--- a/solution.py
+++ b/solution.py
@@ -125,6 +125,17 @@
         copy.wait()
 
 
+def rows_kernel(kept, received, row_near, row_far):
+    _, core = position()
+    held, functionals, rows, _ = kept.shape
+    for source, first in ((kept, core * held), (received, (1 - core) * held)):
+        for i in range(held):
+            near, far = paired_rows(source[i, :, 0, :], source[i, :, rows - 1, :])
+            at = pl.ds(pl.multiple_of((first + i) * functionals, functionals), functionals)
+            row_near[at, :] = near
+            row_far[at, :] = far
+
+
 def place_kernel(kept, received, mine_sums, other_sums, out, sums, sems):
     mine = owned_half()
     functionals = kept.shape[1]
@@ -165,7 +176,7 @@
     return copies
 
 
-def local_kernel(own, received, planes, local, boundary, row_near, row_far, gathered, factors, sems):
+def local_kernel(own, received, planes, local, boundary, gathered, factors, sems):
     side, _ = position()
     copies = load_forcing(own, received, gathered, sems)
     layers = planes.shape[0] - 3
@@ -186,9 +197,6 @@
         )
         for j in range(half):
             local[j, f] = solved[j]
-            near, far = paired_rows(solved[j][0:1], solved[j][rows - 1 : rows])
-            row_near[pl.ds(j * functionals + f, 1), :] = near
-            row_far[pl.ds(j * functionals + f, 1), :] = far
         boundary[f] = solved[half - 1]
         return carry
 
@@ -336,28 +344,40 @@
     out[out.shape[0] - size :, :] = total
 
 
-def middle_kernel(local, planes, near, far, base, message, factors):
+def middle_kernel(local, planes, halo, near, far, base, message, factors, outside):
     side, _ = position()
     layers = planes.shape[0] - 3
     half, functionals, rows, _ = local.shape
-    has_above, has_below = edge_flags()
+    multiplier, inverse, _ = chip_factors(lambda k: halo[k], side, layers)
+    around = []
+    for m in range(half):
+        at = slice(m * functionals, (m + 1) * functionals)
+        around.append(halo_rows(near[at, :], far[at, :]))
+    for which, live in enumerate(edge_flags()):
+        values = [
+            jnp.where(side == 0, around[j][which], around[half - 1 - j][which]) for j in range(half)
+        ]
+        solved = chip_solve(
+            values,
+            [None] + [m[which : which + 1] for m in multiplier[1:]],
+            [v[which : which + 1] for v in inverse],
+        )
+        for j in range(half):
+            outside[which, j] = solved[j] * live
+        start = functionals * (rows + which)
+        message[start : start + functionals, :] = solved[half - 1]
     multiplier, inverse, _ = chip_factors(lambda k: planes[k], side, layers)
     for j in range(half):
         factors[0, j] = multiplier[j + 1]
         factors[1, j] = inverse[j]
-    inner = (half - 1) * functionals
-    above, below = halo_rows(near[inner : inner + functionals, :], far[inner : inner + functionals, :])
-    message[functionals * rows : functionals * (rows + 1), :] = above
-    message[functionals * (rows + 1) : functionals * (rows + 2), :] = below
 
     def step(f, carry):
         horiz = planes[layers + 2]
         residual = []
         for j in range(half):
             here = local[j, f]
-            at = pl.ds(j * functionals + f, 1)
-            above, below = halo_rows(near[at, :], far[at, :])
-            around = moved(here, UP, above * has_above) + moved(here, DOWN, below * has_below)
+            at = pl.ds(f, 1)
+            around = moved(here, UP, outside[0, j, at, :]) + moved(here, DOWN, outside[1, j, at, :])
             around = around + moved(here, LEFT) + moved(here, RIGHT)
             residual.append(horiz * around)
         solved = chip_solve(
@@ -581,6 +601,11 @@
     cross, peer, forcing_received = join(
         (across(block, 3), across(block, 1), across(forcing_sent, 1))
     )
+    rows_near, rows_far = call(rows_kernel, [(stack, width), (stack, width)])(
+        forcing_kept, forcing_received
+    )
+    rows_far = to_far(rows_far)
+    rows_near = to_near(rows_near)
     diag = across(cross, 1)
     planes, edge_near, edge_far = call(
         assemble_kernel, [(count, rows, width), (edge_rows, width), (edge_rows, width)]
@@ -603,23 +628,19 @@
         ],
         any_inputs=(0, 1),
     )(forcing_kept, forcing_received, planes)
-    local, boundary, rows_near, rows_far = call(
+    planes_later, edge_near, edge_far, sums_inside = join((planes, edge_near, edge_far, sums_inside))
+    local, boundary = call(
         local_kernel,
-        [(half, functionals, rows, width), (functionals, rows, width), (stack, width), (stack, width)],
+        [(half, functionals, rows, width), (functionals, rows, width)],
         [gathered, factors, dma((2,))],
         any_inputs=(0, 1),
-    )(forcing_kept, forcing_received, planes)
-    rows_far, rows_near, boundary, edge_near, edge_far = join(
-        (rows_far, rows_near, boundary, edge_near, edge_far)
-    )
-    rows_far = to_far(rows_far)
-    rows_near = to_near(rows_near)
-    boundary_other = across(boundary, 3)
+    )(forcing_kept, forcing_received, planes_later)
     sums, halo = call(
         functools.partial(border_kernel, scale=scale),
         [(functionals, GROUPS), (count, 8, width)],
     )(forcing_kept, forcing_received, planes, edge_near, edge_far, sums_inside)
 
+    boundary_other = across(after(boundary, sums), 3)
     spread, spread_other, response, ends = call(
         coefficient_kernel,
         [(4, half, rows, width), (4, rows, width), (half, rows, width), (6, rows, width)],
@@ -634,8 +655,8 @@
     base, message = call(
         middle_kernel,
         [(half, functionals, rows, width), (functionals * (rows + 3), width)],
-        [factors],
-    )(after(local, spread), planes, rows_near, rows_far)
+        [factors, pltpu.VMEM((2, half, functionals, width), f32)],
+    )(after(local, spread), planes, halo, rows_near, rows_far)
     (message,) = call(
         fold_kernel,
         [message.shape],

time: 40.8 us -> 38.1 us (0.934)
  waiting for transfers between devices: 12.9 us -> 9.98 us
    ppermute x17, waiting for transfers between devices: 12.9 us -> 9.98 us  [send(): return lax.ppermute(array, ('tile', 'layer'), pairs)]
    pallas_call x12 -> x13, Pallas kernels: 8.88 us -> 8.89 us  [run(): pl.pallas_call(kernel, out_shape=[jax.ShapeDtypeStruct(s, jnp.float32) fo...]
  transfers between devices with their start and end apart: 17 -> 17, of which waited for: 7 -> 6; matrix products, arithmetic and copies ran while one was open for 0% -> 0% of each run, Pallas kernels for 13% -> 14%
where the time goes in v3:
time: 38.1 us; the launch traced here: 38 us
  starting transfers between devices  18.3 us (48%)
  waiting for transfers between devices  9.98 us (26%)
  Pallas kernels  8.89 us (23%)
  between operations  0.8 us (2%)
    ppermute x17, starting transfers between devices, send(): return lax.ppermute(array, ('tile', 'layer'), pairs)  18.3 us
    ppermute x17, waiting for transfers between devices, send(): return lax.ppermute(array, ('tile', 'layer'), pairs)  9.98 us
    pallas_call x13, Pallas kernels, run(): pl.pallas_call(kernel, out_shape=[jax.ShapeDtypeStruct(s, jnp.float32) fo...  8.89 us
  transfers between devices with their start and end apart: 17, of which 6 were waited for; matrix products, arithmetic and copies ran while one was open for 0% of the time, Pallas kernels for 14%

profile of v3, /device:TPU:0, one launch (start us, length us, event | category | flops | bytes accessed | tf_op | source)
XLA Modules:
  0.0 38.0 jit_solution(6482760103125789413)
XLA Ops:
  0.6 0.0 copy-start
  0.6 1.3 %shard_map.77 = (f32[18,8,128]{2,1,0:T(8,128)S(1)}, f32[4,8,8,512]{3,2,1,0:T(8,128)S(1)}, f32[4,8,8,512]{3,2,1,0:T(8,128)S(1)}) custom-call(f32[16,8,128]{2,1,0:T(8,128)} %coupling.1, f32[8,128]{1,0:T(8,128)} %velocity.1, s32[8,128]{1,0:T(8,128)} %label.1, s32[8,128]{1,0:T(8,128)} %mask.1, f32[4,16,8,512]{3,2,1,0:T(8,128)} %forcing.1), custom_call_target="tpu_custom_call" | custom-call | tf_op jit(solution)/shard_map/pallas_call | solution.py:521
  2.0 0.5 %collective-permute-start.2 = (f32[4,8,8,512]{3,2,1,0:T(8,128)S(1)}, f32[4,8,8,512]{3,2,1,0:T(8,128)S(1)}, u32[]{:S(2)}, u32[]{:S(2)}) collective-permute-start(f32[4,8,8,512]{3,2,1,0:T(8,128)S(1)} %get-tuple-element.41), channel_id=1, source_target_pairs={{0,1},{1,0},{2,3},{3,2},{4,5},{5,4},{6,7},{7,6},{8,9},{9,8},{10,11... | collective-permute-start | bytes 1572872 | tf_op jit(solution)/shard_map/ppermute | solution.py:559
  2.5 2.6 %collective-permute-start = (f32[18,8,128]{2,1,0:T(8,128)S(1)}, f32[18,8,128]{2,1,0:T(8,128)S(1)}, u32[]{:S(2)}, u32[]{:S(2)}) collective-permute-start(f32[18,8,128]{2,1,0:T(8,128)S(1)} %get-tuple-element.40.own), channel_id=1, source_target_pairs={{0,3},{1,2},{2,1},{3,0},{4,7},{5,6},{6,5},{7,4},{8,11},{9,10},{10,... | collective-permute-start | bytes 221192 | tf_op jit(solution)/shard_map/ppermute | solution.py:559
  5.1 0.1 collective-permute-start.1
  5.2 2.5 %collective-permute-done.cross = f32[18,8,128]{2,1,0:T(8,128)S(1)} collective-permute-done((f32[18,8,128]{2,1,0:T(8,128)S(1)}, f32[18,8,128]{2,1,0:T(8,128)S(1)}, u32[]{:S(2)}, u32[]{:S(2)}) %collective-permute-start) | collective-permute-done | bytes 73760 | tf_op jit(solution)/shard_map/ppermute | solution.py:559
  7.7 0.0 collective-permute-done.1.peer
  7.7 0.0 collective-permute-done.2.received
  7.7 0.1 collective-permute-start.3
  7.8 1.2 %collective-permute-done.3.diag = f32[18,8,128]{2,1,0:T(8,128)S(1)} collective-permute-done((f32[18,8,128]{2,1,0:T(8,128)S(1)}, f32[18,8,128]{2,1,0:T(8,128)S(1)}, u32[]{:S(2)}, u32[]{:S(2)}) %collective-permute-start.3) | collective-permute-done | bytes 73760 | tf_op jit(solution)/shard_map/ppermute | solution.py:559
  9.0 0.0 copy-done
  9.0 0.1 shard_map.78
  9.0 1.5 %collective-permute-start.4 = (f32[24,512]{1,0:T(8,128)S(1)}, f32[24,512]{1,0:T(8,128)S(1)}, u32[]{:S(2)}, u32[]{:S(2)}) collective-permute-start(f32[24,512]{1,0:T(8,128)S(1)} %get-tuple-element.46), channel_id=1, source_target_pairs={{0,5},{1,4},{2,7},{3,6},{4,1},{5,0},{6,3},{7,2},{8,13},{9,12},{10,... | collective-permute-start | bytes 147464 | tf_op jit(solution)/shard_map/ppermute | solution.py:559
  10.5 0.2 collective-permute-start.5
  10.7 0.1 shard_map.83
  10.8 2.7 %collective-permute-start.6 = (f32[64,512]{1,0:T(8,128)S(1)}, f32[64,512]{1,0:T(8,128)S(1)}, u32[]{:S(2)}, u32[]{:S(2)}) collective-permute-start(f32[64,512]{1,0:T(8,128)S(1)} %get-tuple-element.56), channel_id=1, source_target_pairs={{0,5},{1,4},{2,7},{3,6},{4,1},{5,0},{6,3},{7,2},{8,13},{9,12},{10,... | collective-permute-start | bytes 393224 | tf_op jit(solution)/shard_map/ppermute | solution.py:559
  13.4 0.2 collective-permute-start.7
  13.6 2.0 %shard_map.79.inside = f32[8,512]{1,0:T(8,128)S(1)} custom-call(f32[4,8,8,512]{3,2,1,0:T(8,128)S(1)} %get-tuple-element.39.own.kept, f32[4,8,8,512]{3,2,1,0:T(8,128)S(1)} %collective-permute-done.2.received, f32[19,8,512]{2,1,0:T(8,128)S(1)} %get-tuple-element.48.planes), custom_call_target="tpu_custom_call" | custom-call | tf_op jit(solution)/shard_map/pallas_call | solution.py:521
  15.6 0.0 collective-permute-done.4.near
  15.6 0.0 collective-permute-done.5.far
  15.6 0.5 %shard_map.80 = (f32[8,8,8,512]{3,2,1,0:T(8,128)S(1)}, f32[8,8,512]{2,1,0:T(8,128)S(1)}) custom-call(f32[4,8,8,512]{3,2,1,0:T(8,128)S(1)} %get-tuple-element.39.own.kept, f32[4,8,8,512]{3,2,1,0:T(8,128)S(1)} %collective-permute-done.2.received, f32[19,8,512]{2,1,0:T(8,128)S(1)} %get-tuple-element.48.planes), custom_call_target="tpu_custom_call" | custom-call | tf_op jit(solution)/shard_map/pallas_call | solution.py:521
  16.1 0.8 %shard_map.81 = (f32[8,512]{1,0:T(8,128)S(1)}, f32[19,8,512]{2,1,0:T(8,128)S(1)}) custom-call(f32[4,8,8,512]{3,2,1,0:T(8,128)S(1)} %get-tuple-element.39.own.kept, f32[4,8,8,512]{3,2,1,0:T(8,128)S(1)} %collective-permute-done.2.received, f32[19,8,512]{2,1,0:T(8,128)S(1)} %get-tuple-element.48.planes, f32[24,512]{1,0:T(8,128)S(1)} %collective-permute-done.4.near, ...), custom_call_target="tpu_custom_call" | custom-call | tf_op jit(solution)/shard_map/pallas_call | solution.py:521
  16.9 1.5 %collective-permute-start.8 = (f32[8,8,512]{2,1,0:T(8,128)S(1)}, f32[8,8,512]{2,1,0:T(8,128)S(1)}, u32[]{:S(2)}, u32[]{:S(2)}) collective-permute-start(f32[8,8,512]{2,1,0:T(8,128)S(1)} %get-tuple-element.61.boundary), channel_id=1, source_target_pairs={{0,3},{1,2},{2,1},{3,0},{4,7},{5,6},{6,5},{7,4},{8,11},{9,10},{10,... | collective-permute-start | bytes 393224 | tf_op jit(solution)/shard_map/ppermute | solution.py:559
  18.4 1.2 %collective-permute-start.9 = (f32[8,512]{1,0:T(8,128)S(1)}, f32[8,512]{1,0:T(8,128)S(1)}, u32[]{:S(2)}, u32[]{:S(2)}) collective-permute-start(f32[8,512]{1,0:T(8,128)S(1)} %get-tuple-element.62.mine), channel_id=1, source_target_pairs={{0,9},{1,8},{2,11},{3,10},{4,13},{5,12},{6,15},{7,14},{8,1},{9,0},... | collective-permute-start | bytes 49160 | tf_op jit(solution)/shard_map/ppermute | solution.py:559
  19.6 2.4 %collective-permute-start.10 = (f32[8,512]{1,0:T(8,128)S(1)}, f32[8,512]{1,0:T(8,128)S(1)}, u32[]{:S(2)}, u32[]{:S(2)}) collective-permute-start(f32[8,512]{1,0:T(8,128)S(1)} %get-tuple-element.62.mine), channel_id=1, source_target_pairs={{0,17},{1,16},{2,19},{3,18},{4,21},{5,20},{6,23},{7,22},{8,25},{9,... | collective-permute-start | bytes 49160 | tf_op jit(solution)/shard_map/ppermute | solution.py:559
  22.0 0.0 collective-permute-done.6.near
  22.0 1.6 %collective-permute-start.11 = (f32[8,512]{1,0:T(8,128)S(1)}, f32[8,512]{1,0:T(8,128)S(1)}, u32[]{:S(2)}, u32[]{:S(2)}) collective-permute-start(f32[8,512]{1,0:T(8,128)S(1)} %get-tuple-element.62.mine), channel_id=1, source_target_pairs={{0,24},{1,25},{2,26},{3,27},{4,28},{5,29},{6,30},{7,31},{8,16},{9,... | collective-permute-start | bytes 49160 | tf_op jit(solution)/shard_map/ppermute | solution.py:559
  23.6 0.4 %shard_map.82 = (f32[4,8,8,512]{3,2,1,0:T(8,128)S(1)}, f32[4,8,512]{2,1,0:T(8,128)S(1)}, f32[8,8,512]{2,1,0:T(8,128)S(1)}, f32[6,8,512]{2,1,0:T(8,128)S(1)}) custom-call(f32[19,8,512]{2,1,0:T(8,128)S(1)} %get-tuple-element.48.planes, f32[19,8,512]{2,1,0:T(8,128)S(1)} %get-tuple-element.53.halo), custom_call_target="tpu_custom_call" | custom-call | tf_op jit(solution)/shard_map/pallas_call | solution.py:521
  24.0 0.0 collective-permute-done.7.far
  24.0 1.5 %shard_map.84 = (f32[8,8,8,512]{3,2,1,0:T(8,128)S(1)}, f32[88,512]{1,0:T(8,128)S(1)}) custom-call(f32[8,8,8,512]{3,2,1,0:T(8,128)S(1)} %get-tuple-element.55.local, f32[19,8,512]{2,1,0:T(8,128)S(1)} %get-tuple-element.48.planes, f32[19,8,512]{2,1,0:T(8,128)S(1)} %get-tuple-element.53.halo, f32[64,512]{1,0:T(8,128)S(1)} %collective-permute-done.6.near, ...), custom_call_target="tpu_custom_call" | custom-call | tf_op jit(solution)/shard_map/pallas_call | solution.py:521
  25.5 0.0 collective-permute-done.8.boundary_other
  25.5 0.0 collective-permute-done.9.refs_0_
  25.5 0.0 collective-permute-done.10.refs_1_
  25.5 2.0 %collective-permute-done.11.refs_2_ = f32[8,512]{1,0:T(8,128)S(1)} collective-permute-done((f32[8,512]{1,0:T(8,128)S(1)}, f32[8,512]{1,0:T(8,128)S(1)}, u32[]{:S(2)}, u32[]{:S(2)}) %collective-permute-start.11) | collective-permute-done | bytes 16416 | tf_op jit(solution)/shard_map/ppermute | solution.py:559
  27.6 0.1 collective-permute-start.12
  27.6 0.8 %collective-permute-start.13 = (f32[8,512]{1,0:T(8,128)S(1)}, f32[8,512]{1,0:T(8,128)S(1)}, u32[]{:S(2)}, u32[]{:S(2)}) collective-permute-start(f32[8,512]{1,0:T(8,128)S(1)} %slice.4), channel_id=1, source_target_pairs={{0,5},{1,4},{2,7},{3,6},{4,1},{5,0},{6,3},{7,2},{8,13},{9,12},{10,... | collective-permute-start | bytes 49160 | tf_op jit(solution)/shard_map/ppermute | solution.py:559
  28.4 2.4 %collective-permute-start.14 = (f32[8,512]{1,0:T(8,128)S(1)}, f32[8,512]{1,0:T(8,128)S(1)}, u32[]{:S(2)}, u32[]{:S(2)}) collective-permute-start(f32[8,512]{1,0:T(8,128)S(1)} %slice.4), channel_id=1, source_target_pairs={{0,6},{1,7},{2,4},{3,5},{4,2},{5,3},{6,0},{7,1},{8,14},{9,15},{10,... | collective-permute-start | bytes 49160 | tf_op jit(solution)/shard_map/ppermute | solution.py:559
  30.8 0.0 collective-permute-done.13.near
  30.9 2.7 %collective-permute-done.14.diag = f32[8,512]{1,0:T(8,128)S(1)} collective-permute-done((f32[8,512]{1,0:T(8,128)S(1)}, f32[8,512]{1,0:T(8,128)S(1)}, u32[]{:S(2)}, u32[]{:S(2)}) %collective-permute-start.14) | collective-permute-done | bytes 16416 | tf_op jit(solution)/shard_map/ppermute | solution.py:559
  33.6 0.4 collective-permute-done.12.message
  33.9 0.8 %shard_map.86 = (f32[4,8,8,512]{3,2,1,0:T(8,128)S(1)}, f32[8,8,512]{2,1,0:T(8,128)S(1)}, f32[8,512]{1,0:T(8,128)S(1)}) custom-call(f32[8,8,8,512]{3,2,1,0:T(8,128)S(1)} %get-tuple-element.58.base, f32[8,8,512]{2,1,0:T(8,128)S(1)} %get-tuple-element.61.boundary, f32[8,8,512]{2,1,0:T(8,128)S(1)} %collective-permute-done.8.boundary_other, ...), custom_call_target="tpu_custom_call" | custom-call | tf_op jit(solution)/shard_map/pallas_call | solution.py:521
  34.7 0.3 shard_map.87
  35.0 0.1 collective-permute-start.15
  35.1 0.5 %collective-permute-start.16 = (f32[8,512]{1,0:T(8,128)S(1)}, f32[8,512]{1,0:T(8,128)S(1)}, u32[]{:S(2)}, u32[]{:S(2)}) collective-permute-start(f32[8,512]{1,0:T(8,128)S(1)} %get-tuple-element.72.mine_sums), channel_id=1, source_target_pairs={{0,1},{1,0},{2,3},{3,2},{4,5},{5,4},{6,7},{7,6},{8,9},{9,8},{10,11... | collective-permute-start | bytes 49160 | tf_op jit(solution)/shard_map/ppermute | solution.py:559
  35.6 0.2 shard_map.88.kept
  35.8 1.2 %collective-permute-done.16.other_sums = f32[8,512]{1,0:T(8,128)S(1)} collective-permute-done((f32[8,512]{1,0:T(8,128)S(1)}, f32[8,512]{1,0:T(8,128)S(1)}, u32[]{:S(2)}, u32[]{:S(2)}) %collective-permute-start.16) | collective-permute-done | bytes 16416 | tf_op jit(solution)/shard_map/ppermute | solution.py:559
  37.0 0.0 collective-permute-done.15.received
  37.0 1.0 %shard_map.89 = (f32[4,16,8,512]{3,2,1,0:T(8,128)}, f32[16,512]{1,0:T(8,128)}) custom-call(f32[4,8,8,512]{3,2,1,0:T(8,128)S(1)} %shard_map.88.kept, f32[4,8,8,512]{3,2,1,0:T(8,128)S(1)} %collective-permute-done.15.received, f32[8,512]{1,0:T(8,128)S(1)} %get-tuple-element.72.mine_sums, f32[8,512]{1,0:T(8,128)S(1)} %collective-permute-done.16.other_sums), custom_call_target="tpu_custom_call" | custom-call | tf_op jit(solution)/shard_map/pallas_call | solution.py:521
  (2 shorter events, 0.0 us)
Async XLA Ops:
  0.6 8.3 %copy-start = (f32[8,512]{1,0:T(8,128)S(1)}, f32[8,512]{1,0:T(8,128)}, u32[]{:S(2)}) copy-start(f32[8,512]{1,0:T(8,128)} %horiz.1) | copy-start | bytes 49156
  2.0 5.7 %collective-permute-start.2 = (f32[4,8,8,512]{3,2,1,0:T(8,128)S(1)}, f32[4,8,8,512]{3,2,1,0:T(8,128)S(1)}, u32[]{:S(2)}, u32[]{:S(2)}) collective-permute-start(f32[4,8,8,512]{3,2,1,0:T(8,128)S(1)} %get-tuple-element.41), channel_id=1, source_target_pairs={{0,1},{1,0},{2,3},{3,2},{4,5},{5,4},{6,7},{7,6},{8,9},{9,8},{10,11... | collective-permute-start | bytes 1572872 | tf_op jit(solution)/shard_map/ppermute | solution.py:559
  2.5 5.2 %collective-permute-start = (f32[18,8,128]{2,1,0:T(8,128)S(1)}, f32[18,8,128]{2,1,0:T(8,128)S(1)}, u32[]{:S(2)}, u32[]{:S(2)}) collective-permute-start(f32[18,8,128]{2,1,0:T(8,128)S(1)} %get-tuple-element.40.own), channel_id=1, source_target_pairs={{0,3},{1,2},{2,1},{3,0},{4,7},{5,6},{6,5},{7,4},{8,11},{9,10},{10,... | collective-permute-start | bytes 221192 | tf_op jit(solution)/shard_map/ppermute | solution.py:559
  5.1 2.6 %collective-permute-start.1 = (f32[18,8,128]{2,1,0:T(8,128)S(1)}, f32[18,8,128]{2,1,0:T(8,128)S(1)}, u32[]{:S(2)}, u32[]{:S(2)}) collective-permute-start(f32[18,8,128]{2,1,0:T(8,128)S(1)} %get-tuple-element.40.own), channel_id=1, source_target_pairs={{0,1},{1,0},{2,3},{3,2},{4,5},{5,4},{6,7},{7,6},{8,9},{9,8},{10,11... | collective-permute-start | bytes 221192 | tf_op jit(solution)/shard_map/ppermute | solution.py:559
  7.7 1.3 %collective-permute-start.3 = (f32[18,8,128]{2,1,0:T(8,128)S(1)}, f32[18,8,128]{2,1,0:T(8,128)S(1)}, u32[]{:S(2)}, u32[]{:S(2)}) collective-permute-start(f32[18,8,128]{2,1,0:T(8,128)S(1)} %collective-permute-done.cross), channel_id=1, source_target_pairs={{0,1},{1,0},{2,3},{3,2},{4,5},{5,4},{6,7},{7,6},{8,9},{9,8},{10,11... | collective-permute-start | bytes 221192 | tf_op jit(solution)/shard_map/ppermute | solution.py:559
  9.0 6.6 %collective-permute-start.4 = (f32[24,512]{1,0:T(8,128)S(1)}, f32[24,512]{1,0:T(8,128)S(1)}, u32[]{:S(2)}, u32[]{:S(2)}) collective-permute-start(f32[24,512]{1,0:T(8,128)S(1)} %get-tuple-element.46), channel_id=1, source_target_pairs={{0,5},{1,4},{2,7},{3,6},{4,1},{5,0},{6,3},{7,2},{8,13},{9,12},{10,... | collective-permute-start | bytes 147464 | tf_op jit(solution)/shard_map/ppermute | solution.py:559
  10.5 5.1 %collective-permute-start.5 = (f32[24,512]{1,0:T(8,128)S(1)}, f32[24,512]{1,0:T(8,128)S(1)}, u32[]{:S(2)}, u32[]{:S(2)}) collective-permute-start(f32[24,512]{1,0:T(8,128)S(1)} %get-tuple-element.47), channel_id=1, source_target_pairs={{0,1},{1,0},{2,3},{3,2},{4,9},{5,8},{6,11},{7,10},{8,5},{9,4},{10,... | collective-permute-start | bytes 147464 | tf_op jit(solution)/shard_map/ppermute | solution.py:559
  10.8 11.3 %collective-permute-start.6 = (f32[64,512]{1,0:T(8,128)S(1)}, f32[64,512]{1,0:T(8,128)S(1)}, u32[]{:S(2)}, u32[]{:S(2)}) collective-permute-start(f32[64,512]{1,0:T(8,128)S(1)} %get-tuple-element.56), channel_id=1, source_target_pairs={{0,5},{1,4},{2,7},{3,6},{4,1},{5,0},{6,3},{7,2},{8,13},{9,12},{10,... | collective-permute-start | bytes 393224 | tf_op jit(solution)/shard_map/ppermute | solution.py:559
  13.4 10.6 %collective-permute-start.7 = (f32[64,512]{1,0:T(8,128)S(1)}, f32[64,512]{1,0:T(8,128)S(1)}, u32[]{:S(2)}, u32[]{:S(2)}) collective-permute-start(f32[64,512]{1,0:T(8,128)S(1)} %get-tuple-element.57), channel_id=1, source_target_pairs={{0,1},{1,0},{2,3},{3,2},{4,8},{5,9},{6,10},{7,11},{8,4},{9,5},{10,... | collective-permute-start | bytes 393224 | tf_op jit(solution)/shard_map/ppermute | solution.py:559
  16.9 8.6 %collective-permute-start.8 = (f32[8,8,512]{2,1,0:T(8,128)S(1)}, f32[8,8,512]{2,1,0:T(8,128)S(1)}, u32[]{:S(2)}, u32[]{:S(2)}) collective-permute-start(f32[8,8,512]{2,1,0:T(8,128)S(1)} %get-tuple-element.61.boundary), channel_id=1, source_target_pairs={{0,3},{1,2},{2,1},{3,0},{4,7},{5,6},{6,5},{7,4},{8,11},{9,10},{10,... | collective-permute-start | bytes 393224 | tf_op jit(solution)/shard_map/ppermute | solution.py:559
  18.4 7.1 %collective-permute-start.9 = (f32[8,512]{1,0:T(8,128)S(1)}, f32[8,512]{1,0:T(8,128)S(1)}, u32[]{:S(2)}, u32[]{:S(2)}) collective-permute-start(f32[8,512]{1,0:T(8,128)S(1)} %get-tuple-element.62.mine), channel_id=1, source_target_pairs={{0,9},{1,8},{2,11},{3,10},{4,13},{5,12},{6,15},{7,14},{8,1},{9,0},... | collective-permute-start | bytes 49160 | tf_op jit(solution)/shard_map/ppermute | solution.py:559
  19.6 5.9 %collective-permute-start.10 = (f32[8,512]{1,0:T(8,128)S(1)}, f32[8,512]{1,0:T(8,128)S(1)}, u32[]{:S(2)}, u32[]{:S(2)}) collective-permute-start(f32[8,512]{1,0:T(8,128)S(1)} %get-tuple-element.62.mine), channel_id=1, source_target_pairs={{0,17},{1,16},{2,19},{3,18},{4,21},{5,20},{6,23},{7,22},{8,25},{9,... | collective-permute-start | bytes 49160 | tf_op jit(solution)/shard_map/ppermute | solution.py:559
  22.0 5.5 %collective-permute-start.11 = (f32[8,512]{1,0:T(8,128)S(1)}, f32[8,512]{1,0:T(8,128)S(1)}, u32[]{:S(2)}, u32[]{:S(2)}) collective-permute-start(f32[8,512]{1,0:T(8,128)S(1)} %get-tuple-element.62.mine), channel_id=1, source_target_pairs={{0,24},{1,25},{2,26},{3,27},{4,28},{5,29},{6,30},{7,31},{8,16},{9,... | collective-permute-start | bytes 49160 | tf_op jit(solution)/shard_map/ppermute | solution.py:559
  27.6 6.4 %collective-permute-start.12 = (f32[88,512]{1,0:T(8,128)S(1)}, f32[88,512]{1,0:T(8,128)S(1)}, u32[]{:S(2)}, u32[]{:S(2)}) collective-permute-start(f32[88,512]{1,0:T(8,128)S(1)} %shard_map.85.message_mine), channel_id=1, source_target_pairs={{0,3},{1,2},{2,1},{3,0},{4,7},{5,6},{6,5},{7,4},{8,11},{9,10},{10,... | collective-permute-start | bytes 540680 | tf_op jit(solution)/shard_map/ppermute | solution.py:559
  27.6 3.2 %collective-permute-start.13 = (f32[8,512]{1,0:T(8,128)S(1)}, f32[8,512]{1,0:T(8,128)S(1)}, u32[]{:S(2)}, u32[]{:S(2)}) collective-permute-start(f32[8,512]{1,0:T(8,128)S(1)} %slice.4), channel_id=1, source_target_pairs={{0,5},{1,4},{2,7},{3,6},{4,1},{5,0},{6,3},{7,2},{8,13},{9,12},{10,... | collective-permute-start | bytes 49160 | tf_op jit(solution)/shard_map/ppermute | solution.py:559
  28.4 5.1 %collective-permute-start.14 = (f32[8,512]{1,0:T(8,128)S(1)}, f32[8,512]{1,0:T(8,128)S(1)}, u32[]{:S(2)}, u32[]{:S(2)}) collective-permute-start(f32[8,512]{1,0:T(8,128)S(1)} %slice.4), channel_id=1, source_target_pairs={{0,6},{1,7},{2,4},{3,5},{4,2},{5,3},{6,0},{7,1},{8,14},{9,15},{10,... | collective-permute-start | bytes 49160 | tf_op jit(solution)/shard_map/ppermute | solution.py:559
  35.0 2.0 %collective-permute-start.15 = (f32[4,8,8,512]{3,2,1,0:T(8,128)S(1)}, f32[4,8,8,512]{3,2,1,0:T(8,128)S(1)}, u32[]{:S(2)}, u32[]{:S(2)}) collective-permute-start(f32[4,8,8,512]{3,2,1,0:T(8,128)S(1)} %shard_map.87), channel_id=1, source_target_pairs={{0,1},{1,0},{2,3},{3,2},{4,5},{5,4},{6,7},{7,6},{8,9},{9,8},{10,11... | collective-permute-start | bytes 1572872 | tf_op jit(solution)/shard_map/ppermute | solution.py:559
  35.1 1.9 %collective-permute-start.16 = (f32[8,512]{1,0:T(8,128)S(1)}, f32[8,512]{1,0:T(8,128)S(1)}, u32[]{:S(2)}, u32[]{:S(2)}) collective-permute-start(f32[8,512]{1,0:T(8,128)S(1)} %get-tuple-element.72.mine_sums), channel_id=1, source_target_pairs={{0,1},{1,0},{2,3},{3,2},{4,5},{5,4},{6,7},{7,6},{8,9},{9,8},{10,11... | collective-permute-start | bytes 49160 | tf_op jit(solution)/shard_map/ppermute | solution.py:559

commit v4 on v3

--- a/solution.py
+++ b/solution.py
@@ -164,43 +164,38 @@
         row_far[k : k + 1, :] = far
 
 
-def load_forcing(own, received, gathered, sems):
-    _, core = position()
-    held = received.shape[0]
-    copies = (
-        pltpu.make_async_copy(own, gathered.at[pl.ds(core * held, held)], sems.at[0]),
-        pltpu.make_async_copy(received, gathered.at[pl.ds((1 - core) * held, held)], sems.at[1]),
-    )
-    for copy in copies:
-        copy.start()
-    return copies
-
-
-def local_kernel(own, received, planes, local, boundary, gathered, factors, sems):
-    side, _ = position()
-    copies = load_forcing(own, received, gathered, sems)
+def local_kernel(own, received, planes, local, boundary, factors):
+    side, core = position()
     layers = planes.shape[0] - 3
     half, functionals, rows, _ = local.shape
+    held = half // 2
     multiplier, inverse, _ = chip_factors(lambda k: planes[k], side, layers)
     for j in range(half):
         factors[0, j] = multiplier[j + 1]
         factors[1, j] = inverse[j]
-    for copy in copies:
-        copy.wait()
-
-    def step(f, carry):
-        values = [gathered[side * (half - 1) + (1 - 2 * side) * j, f] for j in range(half)]
-        solved = chip_solve(
-            values,
-            [None] + [factors[0, j] for j in range(half)],
-            [factors[1, j] for j in range(half)],
-        )
-        for j in range(half):
-            local[j, f] = solved[j]
-        boundary[f] = solved[half - 1]
-        return carry
-
-    lax.fori_loop(0, functionals, step, 0)
+
+    def sweep(at_side, at_core):
+        order = range(half) if at_side == 0 else range(half - 1, -1, -1)
+
+        def step(f, carry):
+            values = [(own if m // held == at_core else received)[m % held, f] for m in order]
+            solved = chip_solve(
+                values,
+                [None] + [factors[0, j] for j in range(half)],
+                [factors[1, j] for j in range(half)],
+            )
+            for j in range(half):
+                local[j, f] = solved[j]
+            boundary[f] = solved[half - 1]
+            return carry
+
+        lax.fori_loop(0, functionals, step, 0, unroll=8)
+
+    for at_side in range(2):
+        for at_core in range(2):
+            pl.when((side == at_side) & (core == at_core))(
+                functools.partial(sweep, at_side, at_core)
+            )
 
 
 def full_factors(get, layers):
@@ -261,11 +256,11 @@
         sums[:, lanes] = sums[:, lanes] + total[b * functionals : (b + 1) * functionals]
 
 
-def column_kernel(own, received, planes, sums, gathered, weights, terms, sems, *, scale):
+def column_kernel(own, received, planes, sums, weights, parts, terms, *, scale):
     side, core = position()
-    copies = load_forcing(own, received, gathered, sems)
     layers = planes.shape[0] - 3
-    half, functionals, rows, _ = gathered.shape
+    held, functionals, rows, width = own.shape
+    half = 2 * held
     multiplier, inverse = full_factors(lambda k: planes[k], layers)
     weight = planes[layers]
     spread = weight * planes[layers + 2]
@@ -277,23 +272,32 @@
             weights[direction, k] = value
     for k in range(layers):
         weights[4, k] = weights[4, k] * weight
-    for copy in copies:
-        copy.wait()
+
+    def chunk(n, carry):
+        lanes = pl.ds(pl.multiple_of(n * LANES, LANES), LANES)
+        totals = [[None] * functionals for _ in range(5)]
+        for source, first in ((own, core * held), (received, (1 - core) * held)):
+            for i in range(held):
+                factor = [weights[kind, side * half + first + i, :, lanes] for kind in range(5)]
+                for f in range(functionals):
+                    value = source[i, f, :, lanes]
+                    for kind in range(5):
+                        term = value * factor[kind]
+                        old = totals[kind][f]
+                        totals[kind][f] = term if old is None else old + term
+        for kind in range(5):
+            for f in range(functionals):
+                parts[kind, f, :, lanes] = totals[kind][f]
+        return carry
+
+    lax.fori_loop(0, width // LANES, chunk, 0, unroll=4)
 
     def step(f, carry):
-        values = [gathered[m, f] for m in range(half)]
-
-        def total(kind):
-            out = values[0] * weights[kind, side * half]
-            for m in range(1, half):
-                out = out + values[m] * weights[kind, side * half + m]
-            return out
-
-        here = total(4) + moved(total(UP), DOWN) + moved(total(DOWN), UP)
-        terms[f] = here + moved(total(LEFT), RIGHT) + moved(total(RIGHT), LEFT)
+        here = parts[4, f] + moved(parts[UP, f], DOWN) + moved(parts[DOWN, f], UP)
+        terms[f] = here + moved(parts[LEFT, f], RIGHT) + moved(parts[RIGHT, f], LEFT)
         return carry
 
-    lax.fori_loop(0, functionals, step, 0)
+    lax.fori_loop(0, functionals, step, 0, unroll=8)
     total = grouped(terms[:, 0, :], planes[layers + 1, 0:1, :])
     for y in range(1, rows):
         total = total + grouped(terms[:, y, :], planes[layers + 1, y : y + 1, :])
@@ -301,10 +305,10 @@
     add_groups(sums, total, scale, functionals)
 
 
-def border_kernel(own, received, planes, near, far, inside, sums, halo, *, scale):
-    side, core = position()
+def border_kernel(local, planes, near, far, inside, sums, halo, *, scale):
+    side, _ = position()
     layers = planes.shape[0] - 3
-    held, functionals, rows, width = received.shape
+    half, functionals, rows, _ = local.shape
     top_row = lax.broadcasted_iota(jnp.int32, halo.shape[1:], 0) == 0
     has_above, has_below = edge_flags()
 
@@ -315,19 +319,39 @@
 
     for k in range(layers + 3):
         halo[k] = pair(*halo_rows(near[k : k + 1, :], far[k : k + 1, :]))
-    outer = bed_row(*full_factors(lambda k: halo[k], layers))
     live = halo[layers] * halo[layers + 2] * jnp.where(top_row, has_above, has_below)
-    edge = full_factors(lambda k: pair(planes[k, 0:1, :], planes[k, rows - 1 : rows, :]), layers)
-    solved = chip_solve([value * live for value in outer], *edge)
+    lower, lower_inverse, kappa = chip_factors(lambda k: halo[k], 0, layers)
+    upper, upper_inverse, _ = chip_factors(lambda k: halo[k], 1, layers)
+    lower_unit, upper_unit = unit_response(lower, lower_inverse), unit_response(upper, upper_inverse)
+    bed = chip_solve(
+        [jnp.ones_like(kappa)] + [jnp.zeros_like(kappa)] * (half - 1), lower, lower_inverse
+    )
+    below_top = kappa * bed[half - 1] / (1.0 - kappa * lower_unit[half - 1] * kappa * upper_unit[half - 1])
+    above_top = kappa * upper_unit[half - 1] * below_top
+    lower_row = [live * (bed[j] + lower_unit[j] * above_top) for j in range(half)]
+    upper_row = [live * (upper_unit[j] * below_top) for j in range(half)]
+    mine = [jnp.where(side == 0, a, b) for a, b in zip(lower_row, upper_row)]
+    other = [jnp.where(side == 0, b, a) for a, b in zip(lower_row, upper_row)]
+
+    def edge(k):
+        return pair(planes[k, 0:1, :], planes[k, rows - 1 : rows, :])
+
+    multiplier, inverse, kappa = chip_factors(edge, side, layers)
+    unit = unit_response(multiplier, inverse)
+    unit_other = unit_response(*chip_factors(edge, 1 - side, layers)[:2])
+    reach, reach_other = unit[0] * mine[0], unit_other[0] * other[0]
+    for j in range(1, half):
+        reach = reach + unit[j] * mine[j]
+        reach_other = reach_other + unit_other[j] * other[j]
+    far_side = kappa * unit_other[half - 1]
+    across = (reach_other + far_side * reach) / (1.0 - kappa * unit[half - 1] * far_side)
+    mine[half - 1] = mine[half - 1] + kappa * across
     sums[...] = inside[...]
     total = None
     for which, row in enumerate((0, rows - 1)):
-        out = None
-        for m in range(2 * held):
-            weight = jnp.where(side == 0, solved[m][which : which + 1], solved[2 * held + m][which : which + 1])
-            mine, other = own[m % held, :, row, :], received[m % held, :, row, :]
-            value = jnp.where(core == m // held, mine, other) * weight
-            out = value if out is None else out + value
+        out = local[0, :, row, :] * mine[0][which : which + 1]
+        for j in range(1, half):
+            out = out + local[j, :, row, :] * mine[j][which : which + 1]
         part = grouped(out, halo[layers + 1, which : which + 1, :])
         total = part if total is None else total + part
     add_groups(sums, total, scale, functionals)
@@ -391,7 +415,7 @@
         message[pl.ds(pl.multiple_of(f * rows, rows), rows), :] = solved[half - 1]
         return carry
 
-    lax.fori_loop(0, functionals, step, 0)
+    lax.fori_loop(0, functionals, step, 0, unroll=8)
 
 
 def coefficient_kernel(planes, halo, spread, spread_other, response, ends, halo_response):
@@ -481,7 +505,7 @@
         second_all[f] = (last_other + other * last) * inverse
         return carry
 
-    lax.fori_loop(0, functionals, step, 0)
+    lax.fori_loop(0, functionals, step, 0, unroll=8)
 
 
 def final_kernel(base, around_all, second_all, spread, response, out, *, other_core):
@@ -502,7 +526,7 @@
             out[i, f] = value
         return carry
 
-    lax.fori_loop(0, functionals, step, 0)
+    lax.fori_loop(0, functionals, step, 0, unroll=8)
 
 
 def call(
@@ -613,7 +637,6 @@
     edge_far = to_far(edge_far, 1)
     edge_near = to_near(edge_near, 1)
 
-    gathered = pltpu.VMEM((half, functionals, rows, width), f32)
     factors = pltpu.VMEM((2, half, rows, width), f32)
     columns_all = tiles * rows * width
     scale = -((columns_all / GROUPS) ** -0.5)
@@ -621,26 +644,23 @@
         functools.partial(column_kernel, scale=scale),
         [(functionals, GROUPS)],
         [
-            gathered,
             pltpu.VMEM((5, layers, rows, width), f32),
+            pltpu.VMEM((5, functionals, rows, width), f32),
             pltpu.VMEM((functionals, rows, width), f32),
-            dma((2,)),
         ],
-        any_inputs=(0, 1),
     )(forcing_kept, forcing_received, planes)
     planes_later, edge_near, edge_far, sums_inside = join((planes, edge_near, edge_far, sums_inside))
     local, boundary = call(
         local_kernel,
         [(half, functionals, rows, width), (functionals, rows, width)],
-        [gathered, factors, dma((2,))],
-        any_inputs=(0, 1),
-    )(forcing_kept, forcing_received, planes_later)
+        [factors],
+    )(forcing_kept, forcing_received, planes)
     sums, halo = call(
         functools.partial(border_kernel, scale=scale),
         [(functionals, GROUPS), (count, 8, width)],
-    )(forcing_kept, forcing_received, planes, edge_near, edge_far, sums_inside)
-
-    boundary_other = across(after(boundary, sums), 3)
+    )(local, planes, edge_near, edge_far, sums_inside)
+
+    boundary_other = across(after(boundary, sums_inside), 3)
     spread, spread_other, response, ends = call(
         coefficient_kernel,
         [(4, half, rows, width), (4, rows, width), (half, rows, width), (6, rows, width)],

time: 38.1 us -> 37.4 us (0.982)
  Pallas kernels: 8.89 us -> 6.74 us
  starting transfers between devices: 18.3 us -> 19.2 us
  waiting for transfers between devices: 9.98 us -> 10.6 us
    pallas_call x13, Pallas kernels: 8.89 us -> 6.74 us  [run(): pl.pallas_call(kernel, out_shape=[jax.ShapeDtypeStruct(s, jnp.float32) fo...]
    ppermute x17, starting transfers between devices: 18.3 us -> 19.2 us  [send(): return lax.ppermute(array, ('tile', 'layer'), pairs)]
    ppermute x17, waiting for transfers between devices: 9.98 us -> 10.6 us  [send(): return lax.ppermute(array, ('tile', 'layer'), pairs)]
  transfers between devices with their start and end apart: 17 -> 17, of which waited for: 6 -> 5; matrix products, arithmetic and copies ran while one was open for 0% -> 0% of each run, Pallas kernels for 14% -> 10%
where the time goes in v4:
time: 37.4 us; the launch traced here: 37.3 us
  starting transfers between devices  19.2 us (51%)
  waiting for transfers between devices  10.6 us (28%)
  Pallas kernels  6.74 us (18%)
  between operations  0.78 us (2%)
    ppermute x17, starting transfers between devices, send(): return lax.ppermute(array, ('tile', 'layer'), pairs)  19.2 us
    ppermute x17, waiting for transfers between devices, send(): return lax.ppermute(array, ('tile', 'layer'), pairs)  10.6 us
    pallas_call x13, Pallas kernels, run(): pl.pallas_call(kernel, out_shape=[jax.ShapeDtypeStruct(s, jnp.float32) fo...  6.74 us
  transfers between devices with their start and end apart: 17, of which 5 were waited for; matrix products, arithmetic and copies ran while one was open for 0% of the time, Pallas kernels for 10%

profile of v4, /device:TPU:0, one launch (start us, length us, event | category | flops | bytes accessed | tf_op | source)
XLA Modules:
  0.0 37.3 jit_solution(10971512921893869723)
XLA Ops:
  0.6 0.0 copy-start
  0.6 1.3 %shard_map.77 = (f32[18,8,128]{2,1,0:T(8,128)S(1)}, f32[4,8,8,512]{3,2,1,0:T(8,128)S(1)}, f32[4,8,8,512]{3,2,1,0:T(8,128)S(1)}) custom-call(f32[16,8,128]{2,1,0:T(8,128)} %coupling.1, f32[8,128]{1,0:T(8,128)} %velocity.1, s32[8,128]{1,0:T(8,128)} %label.1, s32[8,128]{1,0:T(8,128)} %mask.1, f32[4,16,8,512]{3,2,1,0:T(8,128)} %forcing.1), custom_call_target="tpu_custom_call" | custom-call | tf_op jit(solution)/shard_map/pallas_call | solution.py:545
  2.0 0.5 %collective-permute-start.2 = (f32[4,8,8,512]{3,2,1,0:T(8,128)S(1)}, f32[4,8,8,512]{3,2,1,0:T(8,128)S(1)}, u32[]{:S(2)}, u32[]{:S(2)}) collective-permute-start(f32[4,8,8,512]{3,2,1,0:T(8,128)S(1)} %get-tuple-element.40), channel_id=1, source_target_pairs={{0,1},{1,0},{2,3},{3,2},{4,5},{5,4},{6,7},{7,6},{8,9},{9,8},{10,11... | collective-permute-start | bytes 1572872 | tf_op jit(solution)/shard_map/ppermute | solution.py:583
  2.5 2.6 %collective-permute-start = (f32[18,8,128]{2,1,0:T(8,128)S(1)}, f32[18,8,128]{2,1,0:T(8,128)S(1)}, u32[]{:S(2)}, u32[]{:S(2)}) collective-permute-start(f32[18,8,128]{2,1,0:T(8,128)S(1)} %get-tuple-element.39.own), channel_id=1, source_target_pairs={{0,3},{1,2},{2,1},{3,0},{4,7},{5,6},{6,5},{7,4},{8,11},{9,10},{10,... | collective-permute-start | bytes 221192 | tf_op jit(solution)/shard_map/ppermute | solution.py:583
  5.1 0.1 collective-permute-start.1
  5.2 2.5 %collective-permute-done.cross = f32[18,8,128]{2,1,0:T(8,128)S(1)} collective-permute-done((f32[18,8,128]{2,1,0:T(8,128)S(1)}, f32[18,8,128]{2,1,0:T(8,128)S(1)}, u32[]{:S(2)}, u32[]{:S(2)}) %collective-permute-start) | collective-permute-done | bytes 73760 | tf_op jit(solution)/shard_map/ppermute | solution.py:583
  7.7 0.0 collective-permute-done.1.peer
  7.7 0.0 collective-permute-done.2.received
  7.7 0.1 collective-permute-start.3
  7.8 1.2 %collective-permute-done.3.diag = f32[18,8,128]{2,1,0:T(8,128)S(1)} collective-permute-done((f32[18,8,128]{2,1,0:T(8,128)S(1)}, f32[18,8,128]{2,1,0:T(8,128)S(1)}, u32[]{:S(2)}, u32[]{:S(2)}) %collective-permute-start.3) | collective-permute-done | bytes 73760 | tf_op jit(solution)/shard_map/ppermute | solution.py:583
  9.0 0.0 copy-done
  9.0 0.1 shard_map.78
  9.0 1.5 %collective-permute-start.4 = (f32[24,512]{1,0:T(8,128)S(1)}, f32[24,512]{1,0:T(8,128)S(1)}, u32[]{:S(2)}, u32[]{:S(2)}) collective-permute-start(f32[24,512]{1,0:T(8,128)S(1)} %get-tuple-element.46), channel_id=1, source_target_pairs={{0,5},{1,4},{2,7},{3,6},{4,1},{5,0},{6,3},{7,2},{8,13},{9,12},{10,... | collective-permute-start | bytes 147464 | tf_op jit(solution)/shard_map/ppermute | solution.py:583
  10.5 0.2 collective-permute-start.5
  10.7 0.1 shard_map.83
  10.8 2.7 %collective-permute-start.6 = (f32[64,512]{1,0:T(8,128)S(1)}, f32[64,512]{1,0:T(8,128)S(1)}, u32[]{:S(2)}, u32[]{:S(2)}) collective-permute-start(f32[64,512]{1,0:T(8,128)S(1)} %get-tuple-element.54), channel_id=1, source_target_pairs={{0,5},{1,4},{2,7},{3,6},{4,1},{5,0},{6,3},{7,2},{8,13},{9,12},{10,... | collective-permute-start | bytes 393224 | tf_op jit(solution)/shard_map/ppermute | solution.py:583
  13.4 0.2 collective-permute-start.7
  13.6 0.3 shard_map.79
  13.9 1.5 %shard_map.80.inside = f32[8,512]{1,0:T(8,128)S(1)} custom-call(f32[4,8,8,512]{3,2,1,0:T(8,128)S(1)} %get-tuple-element.38.own.kept, f32[4,8,8,512]{3,2,1,0:T(8,128)S(1)} %collective-permute-done.2.received, f32[19,8,512]{2,1,0:T(8,128)S(1)} %get-tuple-element.44.planes), custom_call_target="tpu_custom_call" | custom-call | tf_op jit(solution)/shard_map/pallas_call | solution.py:545
  15.4 0.0 collective-permute-done.4.near
  15.4 0.0 collective-permute-done.5.far
  15.4 1.5 %collective-permute-start.8 = (f32[8,8,512]{2,1,0:T(8,128)S(1)}, f32[8,8,512]{2,1,0:T(8,128)S(1)}, u32[]{:S(2)}, u32[]{:S(2)}) collective-permute-start(f32[8,8,512]{2,1,0:T(8,128)S(1)} %get-tuple-element.58.boundary), channel_id=1, source_target_pairs={{0,3},{1,2},{2,1},{3,0},{4,7},{5,6},{6,5},{7,4},{8,11},{9,10},{10,... | collective-permute-start | bytes 393224 | tf_op jit(solution)/shard_map/ppermute | solution.py:583
  16.9 0.6 %shard_map.81 = (f32[8,512]{1,0:T(8,128)S(1)}, f32[19,8,512]{2,1,0:T(8,128)S(1)}) custom-call(f32[8,8,8,512]{3,2,1,0:T(8,128)S(1)} %get-tuple-element.53.local, f32[19,8,512]{2,1,0:T(8,128)S(1)} %get-tuple-element.44.planes, f32[24,512]{1,0:T(8,128)S(1)} %collective-permute-done.4.near, f32[24,512]{1,0:T(8,128)S(1)} %collective-permute-done.5.far, ...), custom_call_target="tpu_custom_call" | custom-call | tf_op jit(solution)/shard_map/pallas_call | solution.py:545
  17.5 1.2 %collective-permute-start.9 = (f32[8,512]{1,0:T(8,128)S(1)}, f32[8,512]{1,0:T(8,128)S(1)}, u32[]{:S(2)}, u32[]{:S(2)}) collective-permute-start(f32[8,512]{1,0:T(8,128)S(1)} %get-tuple-element.60.mine), channel_id=1, source_target_pairs={{0,9},{1,8},{2,11},{3,10},{4,13},{5,12},{6,15},{7,14},{8,1},{9,0},... | collective-permute-start | bytes 49160 | tf_op jit(solution)/shard_map/ppermute | solution.py:583
  18.8 2.6 %collective-permute-start.10 = (f32[8,512]{1,0:T(8,128)S(1)}, f32[8,512]{1,0:T(8,128)S(1)}, u32[]{:S(2)}, u32[]{:S(2)}) collective-permute-start(f32[8,512]{1,0:T(8,128)S(1)} %get-tuple-element.60.mine), channel_id=1, source_target_pairs={{0,17},{1,16},{2,19},{3,18},{4,21},{5,20},{6,23},{7,22},{8,25},{9,... | collective-permute-start | bytes 49160 | tf_op jit(solution)/shard_map/ppermute | solution.py:583
  21.3 0.0 collective-permute-done.6.near
  21.3 2.3 %collective-permute-start.11 = (f32[8,512]{1,0:T(8,128)S(1)}, f32[8,512]{1,0:T(8,128)S(1)}, u32[]{:S(2)}, u32[]{:S(2)}) collective-permute-start(f32[8,512]{1,0:T(8,128)S(1)} %get-tuple-element.60.mine), channel_id=1, source_target_pairs={{0,24},{1,25},{2,26},{3,27},{4,28},{5,29},{6,30},{7,31},{8,16},{9,... | collective-permute-start | bytes 49160 | tf_op jit(solution)/shard_map/ppermute | solution.py:583
  23.6 0.4 %shard_map.82 = (f32[4,8,8,512]{3,2,1,0:T(8,128)S(1)}, f32[4,8,512]{2,1,0:T(8,128)S(1)}, f32[8,8,512]{2,1,0:T(8,128)S(1)}, f32[6,8,512]{2,1,0:T(8,128)S(1)}) custom-call(f32[19,8,512]{2,1,0:T(8,128)S(1)} %get-tuple-element.44.planes, f32[19,8,512]{2,1,0:T(8,128)S(1)} %get-tuple-element.51.halo), custom_call_target="tpu_custom_call" | custom-call | tf_op jit(solution)/shard_map/pallas_call | solution.py:545
  24.0 0.0 collective-permute-done.7.far
  24.0 0.8 %shard_map.84 = (f32[8,8,8,512]{3,2,1,0:T(8,128)S(1)}, f32[88,512]{1,0:T(8,128)S(1)}) custom-call(f32[8,8,8,512]{3,2,1,0:T(8,128)S(1)} %get-tuple-element.53.local, f32[19,8,512]{2,1,0:T(8,128)S(1)} %get-tuple-element.44.planes, f32[19,8,512]{2,1,0:T(8,128)S(1)} %get-tuple-element.51.halo, f32[64,512]{1,0:T(8,128)S(1)} %collective-permute-done.6.near, ...), custom_call_target="tpu_custom_call" | custom-call | tf_op jit(solution)/shard_map/pallas_call | solution.py:545
  24.8 0.0 collective-permute-done.8.boundary_other
  24.9 0.0 collective-permute-done.9.refs_0_
  24.9 0.0 collective-permute-done.10.refs_1_
  24.9 2.0 %collective-permute-done.11.refs_2_ = f32[8,512]{1,0:T(8,128)S(1)} collective-permute-done((f32[8,512]{1,0:T(8,128)S(1)}, f32[8,512]{1,0:T(8,128)S(1)}, u32[]{:S(2)}, u32[]{:S(2)}) %collective-permute-start.11) | collective-permute-done | bytes 16416 | tf_op jit(solution)/shard_map/ppermute | solution.py:583
  26.9 0.1 collective-permute-start.12
  27.0 1.5 %collective-permute-start.13 = (f32[8,512]{1,0:T(8,128)S(1)}, f32[8,512]{1,0:T(8,128)S(1)}, u32[]{:S(2)}, u32[]{:S(2)}) collective-permute-start(f32[8,512]{1,0:T(8,128)S(1)} %slice.4), channel_id=1, source_target_pairs={{0,5},{1,4},{2,7},{3,6},{4,1},{5,0},{6,3},{7,2},{8,13},{9,12},{10,... | collective-permute-start | bytes 49160 | tf_op jit(solution)/shard_map/ppermute | solution.py:583
  28.4 1.7 %collective-permute-start.14 = (f32[8,512]{1,0:T(8,128)S(1)}, f32[8,512]{1,0:T(8,128)S(1)}, u32[]{:S(2)}, u32[]{:S(2)}) collective-permute-start(f32[8,512]{1,0:T(8,128)S(1)} %slice.4), channel_id=1, source_target_pairs={{0,6},{1,7},{2,4},{3,5},{4,2},{5,3},{6,0},{7,1},{8,14},{9,15},{10,... | collective-permute-start | bytes 49160 | tf_op jit(solution)/shard_map/ppermute | solution.py:583
  30.2 0.0 collective-permute-done.13.near
  30.2 3.6 %collective-permute-done.14.diag = f32[8,512]{1,0:T(8,128)S(1)} collective-permute-done((f32[8,512]{1,0:T(8,128)S(1)}, f32[8,512]{1,0:T(8,128)S(1)}, u32[]{:S(2)}, u32[]{:S(2)}) %collective-permute-start.14) | collective-permute-done | bytes 16416 | tf_op jit(solution)/shard_map/ppermute | solution.py:583
  33.8 0.0 collective-permute-done.12.message
  33.8 0.2 shard_map.86
  34.1 0.2 shard_map.87
  34.3 0.1 collective-permute-start.15
  34.4 0.4 %collective-permute-start.16 = (f32[8,512]{1,0:T(8,128)S(1)}, f32[8,512]{1,0:T(8,128)S(1)}, u32[]{:S(2)}, u32[]{:S(2)}) collective-permute-start(f32[8,512]{1,0:T(8,128)S(1)} %get-tuple-element.70.mine_sums), channel_id=1, source_target_pairs={{0,1},{1,0},{2,3},{3,2},{4,5},{5,4},{6,7},{7,6},{8,9},{9,8},{10,11... | collective-permute-start | bytes 49160 | tf_op jit(solution)/shard_map/ppermute | solution.py:583
  34.9 0.2 shard_map.88.kept
  35.1 1.2 %collective-permute-done.16.other_sums = f32[8,512]{1,0:T(8,128)S(1)} collective-permute-done((f32[8,512]{1,0:T(8,128)S(1)}, f32[8,512]{1,0:T(8,128)S(1)}, u32[]{:S(2)}, u32[]{:S(2)}) %collective-permute-start.16) | collective-permute-done | bytes 16416 | tf_op jit(solution)/shard_map/ppermute | solution.py:583
  36.3 0.0 collective-permute-done.15.received
  36.3 1.0 %shard_map.89 = (f32[4,16,8,512]{3,2,1,0:T(8,128)}, f32[16,512]{1,0:T(8,128)}) custom-call(f32[4,8,8,512]{3,2,1,0:T(8,128)S(1)} %shard_map.88.kept, f32[4,8,8,512]{3,2,1,0:T(8,128)S(1)} %collective-permute-done.15.received, f32[8,512]{1,0:T(8,128)S(1)} %get-tuple-element.70.mine_sums, f32[8,512]{1,0:T(8,128)S(1)} %collective-permute-done.16.other_sums), custom_call_target="tpu_custom_call" | custom-call | tf_op jit(solution)/shard_map/pallas_call | solution.py:545
  (2 shorter events, 0.0 us)
Async XLA Ops:
  0.6 8.3 %copy-start = (f32[8,512]{1,0:T(8,128)S(1)}, f32[8,512]{1,0:T(8,128)}, u32[]{:S(2)}) copy-start(f32[8,512]{1,0:T(8,128)} %horiz.1) | copy-start | bytes 49156
  2.0 5.7 %collective-permute-start.2 = (f32[4,8,8,512]{3,2,1,0:T(8,128)S(1)}, f32[4,8,8,512]{3,2,1,0:T(8,128)S(1)}, u32[]{:S(2)}, u32[]{:S(2)}) collective-permute-start(f32[4,8,8,512]{3,2,1,0:T(8,128)S(1)} %get-tuple-element.40), channel_id=1, source_target_pairs={{0,1},{1,0},{2,3},{3,2},{4,5},{5,4},{6,7},{7,6},{8,9},{9,8},{10,11... | collective-permute-start | bytes 1572872 | tf_op jit(solution)/shard_map/ppermute | solution.py:583
  2.5 5.2 %collective-permute-start = (f32[18,8,128]{2,1,0:T(8,128)S(1)}, f32[18,8,128]{2,1,0:T(8,128)S(1)}, u32[]{:S(2)}, u32[]{:S(2)}) collective-permute-start(f32[18,8,128]{2,1,0:T(8,128)S(1)} %get-tuple-element.39.own), channel_id=1, source_target_pairs={{0,3},{1,2},{2,1},{3,0},{4,7},{5,6},{6,5},{7,4},{8,11},{9,10},{10,... | collective-permute-start | bytes 221192 | tf_op jit(solution)/shard_map/ppermute | solution.py:583
  5.1 2.6 %collective-permute-start.1 = (f32[18,8,128]{2,1,0:T(8,128)S(1)}, f32[18,8,128]{2,1,0:T(8,128)S(1)}, u32[]{:S(2)}, u32[]{:S(2)}) collective-permute-start(f32[18,8,128]{2,1,0:T(8,128)S(1)} %get-tuple-element.39.own), channel_id=1, source_target_pairs={{0,1},{1,0},{2,3},{3,2},{4,5},{5,4},{6,7},{7,6},{8,9},{9,8},{10,11... | collective-permute-start | bytes 221192 | tf_op jit(solution)/shard_map/ppermute | solution.py:583
  7.7 1.3 %collective-permute-start.3 = (f32[18,8,128]{2,1,0:T(8,128)S(1)}, f32[18,8,128]{2,1,0:T(8,128)S(1)}, u32[]{:S(2)}, u32[]{:S(2)}) collective-permute-start(f32[18,8,128]{2,1,0:T(8,128)S(1)} %collective-permute-done.cross), channel_id=1, source_target_pairs={{0,1},{1,0},{2,3},{3,2},{4,5},{5,4},{6,7},{7,6},{8,9},{9,8},{10,11... | collective-permute-start | bytes 221192 | tf_op jit(solution)/shard_map/ppermute | solution.py:583
  9.0 6.4 %collective-permute-start.4 = (f32[24,512]{1,0:T(8,128)S(1)}, f32[24,512]{1,0:T(8,128)S(1)}, u32[]{:S(2)}, u32[]{:S(2)}) collective-permute-start(f32[24,512]{1,0:T(8,128)S(1)} %get-tuple-element.46), channel_id=1, source_target_pairs={{0,5},{1,4},{2,7},{3,6},{4,1},{5,0},{6,3},{7,2},{8,13},{9,12},{10,... | collective-permute-start | bytes 147464 | tf_op jit(solution)/shard_map/ppermute | solution.py:583
  10.5 4.9 %collective-permute-start.5 = (f32[24,512]{1,0:T(8,128)S(1)}, f32[24,512]{1,0:T(8,128)S(1)}, u32[]{:S(2)}, u32[]{:S(2)}) collective-permute-start(f32[24,512]{1,0:T(8,128)S(1)} %get-tuple-element.47), channel_id=1, source_target_pairs={{0,1},{1,0},{2,3},{3,2},{4,9},{5,8},{6,11},{7,10},{8,5},{9,4},{10,... | collective-permute-start | bytes 147464 | tf_op jit(solution)/shard_map/ppermute | solution.py:583
  10.8 10.6 %collective-permute-start.6 = (f32[64,512]{1,0:T(8,128)S(1)}, f32[64,512]{1,0:T(8,128)S(1)}, u32[]{:S(2)}, u32[]{:S(2)}) collective-permute-start(f32[64,512]{1,0:T(8,128)S(1)} %get-tuple-element.54), channel_id=1, source_target_pairs={{0,5},{1,4},{2,7},{3,6},{4,1},{5,0},{6,3},{7,2},{8,13},{9,12},{10,... | collective-permute-start | bytes 393224 | tf_op jit(solution)/shard_map/ppermute | solution.py:583
  13.4 10.6 %collective-permute-start.7 = (f32[64,512]{1,0:T(8,128)S(1)}, f32[64,512]{1,0:T(8,128)S(1)}, u32[]{:S(2)}, u32[]{:S(2)}) collective-permute-start(f32[64,512]{1,0:T(8,128)S(1)} %get-tuple-element.55), channel_id=1, source_target_pairs={{0,1},{1,0},{2,3},{3,2},{4,8},{5,9},{6,10},{7,11},{8,4},{9,5},{10,... | collective-permute-start | bytes 393224 | tf_op jit(solution)/shard_map/ppermute | solution.py:583
  15.4 9.4 %collective-permute-start.8 = (f32[8,8,512]{2,1,0:T(8,128)S(1)}, f32[8,8,512]{2,1,0:T(8,128)S(1)}, u32[]{:S(2)}, u32[]{:S(2)}) collective-permute-start(f32[8,8,512]{2,1,0:T(8,128)S(1)} %get-tuple-element.58.boundary), channel_id=1, source_target_pairs={{0,3},{1,2},{2,1},{3,0},{4,7},{5,6},{6,5},{7,4},{8,11},{9,10},{10,... | collective-permute-start | bytes 393224 | tf_op jit(solution)/shard_map/ppermute | solution.py:583
  17.5 7.3 %collective-permute-start.9 = (f32[8,512]{1,0:T(8,128)S(1)}, f32[8,512]{1,0:T(8,128)S(1)}, u32[]{:S(2)}, u32[]{:S(2)}) collective-permute-start(f32[8,512]{1,0:T(8,128)S(1)} %get-tuple-element.60.mine), channel_id=1, source_target_pairs={{0,9},{1,8},{2,11},{3,10},{4,13},{5,12},{6,15},{7,14},{8,1},{9,0},... | collective-permute-start | bytes 49160 | tf_op jit(solution)/shard_map/ppermute | solution.py:583
  18.8 6.1 %collective-permute-start.10 = (f32[8,512]{1,0:T(8,128)S(1)}, f32[8,512]{1,0:T(8,128)S(1)}, u32[]{:S(2)}, u32[]{:S(2)}) collective-permute-start(f32[8,512]{1,0:T(8,128)S(1)} %get-tuple-element.60.mine), channel_id=1, source_target_pairs={{0,17},{1,16},{2,19},{3,18},{4,21},{5,20},{6,23},{7,22},{8,25},{9,... | collective-permute-start | bytes 49160 | tf_op jit(solution)/shard_map/ppermute | solution.py:583
  21.3 5.5 %collective-permute-start.11 = (f32[8,512]{1,0:T(8,128)S(1)}, f32[8,512]{1,0:T(8,128)S(1)}, u32[]{:S(2)}, u32[]{:S(2)}) collective-permute-start(f32[8,512]{1,0:T(8,128)S(1)} %get-tuple-element.60.mine), channel_id=1, source_target_pairs={{0,24},{1,25},{2,26},{3,27},{4,28},{5,29},{6,30},{7,31},{8,16},{9,... | collective-permute-start | bytes 49160 | tf_op jit(solution)/shard_map/ppermute | solution.py:583
  26.9 7.0 %collective-permute-start.12 = (f32[88,512]{1,0:T(8,128)S(1)}, f32[88,512]{1,0:T(8,128)S(1)}, u32[]{:S(2)}, u32[]{:S(2)}) collective-permute-start(f32[88,512]{1,0:T(8,128)S(1)} %shard_map.85.message_mine), channel_id=1, source_target_pairs={{0,3},{1,2},{2,1},{3,0},{4,7},{5,6},{6,5},{7,4},{8,11},{9,10},{10,... | collective-permute-start | bytes 540680 | tf_op jit(solution)/shard_map/ppermute | solution.py:583
  27.0 3.2 %collective-permute-start.13 = (f32[8,512]{1,0:T(8,128)S(1)}, f32[8,512]{1,0:T(8,128)S(1)}, u32[]{:S(2)}, u32[]{:S(2)}) collective-permute-start(f32[8,512]{1,0:T(8,128)S(1)} %slice.4), channel_id=1, source_target_pairs={{0,5},{1,4},{2,7},{3,6},{4,1},{5,0},{6,3},{7,2},{8,13},{9,12},{10,... | collective-permute-start | bytes 49160 | tf_op jit(solution)/shard_map/ppermute | solution.py:583
  28.4 5.4 %collective-permute-start.14 = (f32[8,512]{1,0:T(8,128)S(1)}, f32[8,512]{1,0:T(8,128)S(1)}, u32[]{:S(2)}, u32[]{:S(2)}) collective-permute-start(f32[8,512]{1,0:T(8,128)S(1)} %slice.4), channel_id=1, source_target_pairs={{0,6},{1,7},{2,4},{3,5},{4,2},{5,3},{6,0},{7,1},{8,14},{9,15},{10,... | collective-permute-start | bytes 49160 | tf_op jit(solution)/shard_map/ppermute | solution.py:583
  34.3 2.0 %collective-permute-start.15 = (f32[4,8,8,512]{3,2,1,0:T(8,128)S(1)}, f32[4,8,8,512]{3,2,1,0:T(8,128)S(1)}, u32[]{:S(2)}, u32[]{:S(2)}) collective-permute-start(f32[4,8,8,512]{3,2,1,0:T(8,128)S(1)} %shard_map.87), channel_id=1, source_target_pairs={{0,1},{1,0},{2,3},{3,2},{4,5},{5,4},{6,7},{7,6},{8,9},{9,8},{10,11... | collective-permute-start | bytes 1572872 | tf_op jit(solution)/shard_map/ppermute | solution.py:583
  34.4 1.9 %collective-permute-start.16 = (f32[8,512]{1,0:T(8,128)S(1)}, f32[8,512]{1,0:T(8,128)S(1)}, u32[]{:S(2)}, u32[]{:S(2)}) collective-permute-start(f32[8,512]{1,0:T(8,128)S(1)} %get-tuple-element.70.mine_sums), channel_id=1, source_target_pairs={{0,1},{1,0},{2,3},{3,2},{4,5},{5,4},{6,7},{7,6},{8,9},{9,8},{10,11... | collective-permute-start | bytes 49160 | tf_op jit(solution)/shard_map/ppermute | solution.py:583

commit v5 on v4

--- a/solution.py
+++ b/solution.py
@@ -136,14 +136,25 @@
             row_far[at, :] = far
 
 
-def place_kernel(kept, received, mine_sums, other_sums, out, sums, sems):
+def place_kept_kernel(kept, out, sem):
+    functionals = kept.shape[1]
+    at = pl.ds(pl.multiple_of(owned_half() * functionals, functionals), functionals)
+    copy = pltpu.make_async_copy(kept, out.at[:, at], sem)
+    copy.start()
+    copy.wait()
+
+
+def place_kernel(partly, received, mine_sums, other_sums, out, sums, sems):
     mine = owned_half()
-    functionals = kept.shape[1]
-    copies = []
-    for i, (source, group, which) in enumerate(((received, other_sums, 1 - mine), (kept, mine_sums, mine))):
-        at = pl.ds(pl.multiple_of(which * functionals, functionals), functionals)
-        copies.append(pltpu.make_async_copy(source, out.at[:, at], sems.at[2 * i]))
-        copies.append(pltpu.make_async_copy(group, sums.at[at], sems.at[2 * i + 1]))
+    functionals = received.shape[1]
+    at, other = (
+        pl.ds(pl.multiple_of(which * functionals, functionals), functionals) for which in (mine, 1 - mine)
+    )
+    copies = (
+        pltpu.make_async_copy(received, out.at[:, other], sems.at[0]),
+        pltpu.make_async_copy(mine_sums, sums.at[at], sems.at[1]),
+        pltpu.make_async_copy(other_sums, sums.at[other], sems.at[2]),
+    )
     for copy in copies:
         copy.start()
     for copy in copies:
@@ -544,10 +555,13 @@
         ]
         return pl.pallas_call(
             kernel,
-            out_shape=[jax.ShapeDtypeStruct(s, jnp.float32) for s in out_shapes],
+            out_shape=[
+                (pltpu.HBM if i in any_outputs else jax.ShapeDtypeStruct)(s, jnp.float32)
+                for i, s in enumerate(out_shapes)
+            ],
             in_specs=in_specs,
             out_specs=[
-                pl.BlockSpec(memory_space=pl.ANY if i in any_outputs else pltpu.VMEM)
+                pl.BlockSpec(memory_space=pltpu.HBM if i in any_outputs else pltpu.VMEM)
                 for i in range(len(out_shapes))
             ],
             scratch_shapes=list(scratch),
@@ -699,14 +713,18 @@
     (kept,) = call(functools.partial(final_kernel, other_core=False), [quarter])(
         base, around, second, spread, response
     )
-    received, other_sums, kept = join((across(sent, 1), across(sums, 1), kept))
+    whole = (held, functionals_all, rows, width)
+    (partly,) = call(place_kept_kernel, [whole], [dma], any_inputs=(0,), any_outputs=(0,))(kept)
+    received, other_sums, partly = join((across(sent, 1), across(sums, 1), partly))
     adjoint, sums = call(
         place_kernel,
-        [(held, functionals_all, rows, width), (functionals_all, GROUPS)],
-        [dma((4,))],
-        any_inputs=(0, 1, 2, 3),
+        [whole, (functionals_all, GROUPS)],
+        [dma((3,))],
+        any_inputs=(1, 2, 3),
+        hbm_inputs=(0,),
         any_outputs=(0, 1),
-    )(kept, received, sums, other_sums)
+        aliases={0: 0},
+    )(partly, received, sums, other_sums)
     return (adjoint, sums)
 
 

time: 37.4 us -> 37.3 us (level)
  waiting for transfers between devices: 10.6 us -> 9.75 us
  Pallas kernels: 6.74 us -> 7.38 us
    ppermute x17, waiting for transfers between devices: 10.6 us -> 9.75 us  [send(): return lax.ppermute(array, ('tile', 'layer'), pairs)]
    pallas_call x13 -> x14, Pallas kernels: 6.74 us -> 7.38 us  [run(): pl.pallas_call(kernel, out_shape=[(pltpu.HBM if i in any_outputs else jax...]
  transfers between devices with their start and end apart: 17 -> 17, of which waited for: 5 -> 5; matrix products, arithmetic and copies ran while one was open for 0% -> 0% of each run, Pallas kernels for 10% -> 13%
where the time goes in v5:
time: 37.3 us; the launch traced here: 37.1 us
  starting transfers between devices  19.2 us (51%)
  waiting for transfers between devices  9.75 us (26%)
  Pallas kernels  7.38 us (20%)
  between operations  0.79 us (2%)
    ppermute x17, starting transfers between devices, send(): return lax.ppermute(array, ('tile', 'layer'), pairs)  19.2 us
    ppermute x17, waiting for transfers between devices, send(): return lax.ppermute(array, ('tile', 'layer'), pairs)  9.75 us
    pallas_call x14, Pallas kernels, run(): pl.pallas_call(kernel, out_shape=[(pltpu.HBM if i in any_outputs else jax...  7.38 us
  transfers between devices with their start and end apart: 17, of which 5 were waited for; matrix products, arithmetic and copies ran while one was open for 0% of the time, Pallas kernels for 13%

profile of v5, /device:TPU:0, one launch (start us, length us, event | category | flops | bytes accessed | tf_op | source)
XLA Modules:
  0.0 37.1 jit_solution(4579319728172221596)
XLA Ops:
  0.6 0.0 copy-start
  0.6 1.3 %shard_map.77 = (f32[18,8,128]{2,1,0:T(8,128)S(1)}, f32[4,8,8,512]{3,2,1,0:T(8,128)S(1)}, f32[4,8,8,512]{3,2,1,0:T(8,128)S(1)}) custom-call(f32[16,8,128]{2,1,0:T(8,128)} %coupling.1, f32[8,128]{1,0:T(8,128)} %velocity.1, s32[8,128]{1,0:T(8,128)} %label.1, s32[8,128]{1,0:T(8,128)} %mask.1, f32[4,16,8,512]{3,2,1,0:T(8,128)} %forcing.1), custom_call_target="tpu_custom_call" | custom-call | tf_op jit(solution)/shard_map/pallas_call | solution.py:556
  2.0 0.5 %collective-permute-start.2 = (f32[4,8,8,512]{3,2,1,0:T(8,128)S(1)}, f32[4,8,8,512]{3,2,1,0:T(8,128)S(1)}, u32[]{:S(2)}, u32[]{:S(2)}) collective-permute-start(f32[4,8,8,512]{3,2,1,0:T(8,128)S(1)} %get-tuple-element.40), channel_id=1, source_target_pairs={{0,1},{1,0},{2,3},{3,2},{4,5},{5,4},{6,7},{7,6},{8,9},{9,8},{10,11... | collective-permute-start | bytes 1572872 | tf_op jit(solution)/shard_map/ppermute | solution.py:597
  2.5 2.6 %collective-permute-start = (f32[18,8,128]{2,1,0:T(8,128)S(1)}, f32[18,8,128]{2,1,0:T(8,128)S(1)}, u32[]{:S(2)}, u32[]{:S(2)}) collective-permute-start(f32[18,8,128]{2,1,0:T(8,128)S(1)} %get-tuple-element.39.own), channel_id=1, source_target_pairs={{0,3},{1,2},{2,1},{3,0},{4,7},{5,6},{6,5},{7,4},{8,11},{9,10},{10,... | collective-permute-start | bytes 221192 | tf_op jit(solution)/shard_map/ppermute | solution.py:597
  5.1 0.1 collective-permute-start.1
  5.2 2.5 %collective-permute-done.cross = f32[18,8,128]{2,1,0:T(8,128)S(1)} collective-permute-done((f32[18,8,128]{2,1,0:T(8,128)S(1)}, f32[18,8,128]{2,1,0:T(8,128)S(1)}, u32[]{:S(2)}, u32[]{:S(2)}) %collective-permute-start) | collective-permute-done | bytes 73760 | tf_op jit(solution)/shard_map/ppermute | solution.py:597
  7.7 0.0 collective-permute-done.1.peer
  7.7 0.0 collective-permute-done.2.received
  7.7 0.1 collective-permute-start.3
  7.8 1.2 %collective-permute-done.3.diag = f32[18,8,128]{2,1,0:T(8,128)S(1)} collective-permute-done((f32[18,8,128]{2,1,0:T(8,128)S(1)}, f32[18,8,128]{2,1,0:T(8,128)S(1)}, u32[]{:S(2)}, u32[]{:S(2)}) %collective-permute-start.3) | collective-permute-done | bytes 73760 | tf_op jit(solution)/shard_map/ppermute | solution.py:597
  9.0 0.1 shard_map.78
  9.0 1.5 %collective-permute-start.4 = (f32[24,512]{1,0:T(8,128)S(1)}, f32[24,512]{1,0:T(8,128)S(1)}, u32[]{:S(2)}, u32[]{:S(2)}) collective-permute-start(f32[24,512]{1,0:T(8,128)S(1)} %get-tuple-element.46), channel_id=1, source_target_pairs={{0,5},{1,4},{2,7},{3,6},{4,1},{5,0},{6,3},{7,2},{8,13},{9,12},{10,... | collective-permute-start | bytes 147464 | tf_op jit(solution)/shard_map/ppermute | solution.py:597
  10.5 0.2 collective-permute-start.5
  10.7 0.1 shard_map.83
  10.8 2.7 %collective-permute-start.6 = (f32[64,512]{1,0:T(8,128)S(1)}, f32[64,512]{1,0:T(8,128)S(1)}, u32[]{:S(2)}, u32[]{:S(2)}) collective-permute-start(f32[64,512]{1,0:T(8,128)S(1)} %get-tuple-element.54), channel_id=1, source_target_pairs={{0,5},{1,4},{2,7},{3,6},{4,1},{5,0},{6,3},{7,2},{8,13},{9,12},{10,... | collective-permute-start | bytes 393224 | tf_op jit(solution)/shard_map/ppermute | solution.py:597
  13.4 0.2 collective-permute-start.7
  13.6 0.3 shard_map.79
  13.9 1.5 %shard_map.80.inside = f32[8,512]{1,0:T(8,128)S(1)} custom-call(f32[4,8,8,512]{3,2,1,0:T(8,128)S(1)} %get-tuple-element.38.own.kept, f32[4,8,8,512]{3,2,1,0:T(8,128)S(1)} %collective-permute-done.2.received, f32[19,8,512]{2,1,0:T(8,128)S(1)} %get-tuple-element.44.planes), custom_call_target="tpu_custom_call" | custom-call | tf_op jit(solution)/shard_map/pallas_call | solution.py:556
  15.4 0.0 collective-permute-done.4.near
  15.4 0.0 collective-permute-done.5.far
  15.4 1.5 %collective-permute-start.8 = (f32[8,8,512]{2,1,0:T(8,128)S(1)}, f32[8,8,512]{2,1,0:T(8,128)S(1)}, u32[]{:S(2)}, u32[]{:S(2)}) collective-permute-start(f32[8,8,512]{2,1,0:T(8,128)S(1)} %get-tuple-element.58.boundary), channel_id=1, source_target_pairs={{0,3},{1,2},{2,1},{3,0},{4,7},{5,6},{6,5},{7,4},{8,11},{9,10},{10,... | collective-permute-start | bytes 393224 | tf_op jit(solution)/shard_map/ppermute | solution.py:597
  16.9 0.6 %shard_map.81 = (f32[8,512]{1,0:T(8,128)S(1)}, f32[19,8,512]{2,1,0:T(8,128)S(1)}) custom-call(f32[8,8,8,512]{3,2,1,0:T(8,128)S(1)} %get-tuple-element.53.local, f32[19,8,512]{2,1,0:T(8,128)S(1)} %get-tuple-element.44.planes, f32[24,512]{1,0:T(8,128)S(1)} %collective-permute-done.4.near, f32[24,512]{1,0:T(8,128)S(1)} %collective-permute-done.5.far, ...), custom_call_target="tpu_custom_call" | custom-call | tf_op jit(solution)/shard_map/pallas_call | solution.py:556
  17.5 1.2 %collective-permute-start.9 = (f32[8,512]{1,0:T(8,128)S(1)}, f32[8,512]{1,0:T(8,128)S(1)}, u32[]{:S(2)}, u32[]{:S(2)}) collective-permute-start(f32[8,512]{1,0:T(8,128)S(1)} %get-tuple-element.60.mine), channel_id=1, source_target_pairs={{0,9},{1,8},{2,11},{3,10},{4,13},{5,12},{6,15},{7,14},{8,1},{9,0},... | collective-permute-start | bytes 49160 | tf_op jit(solution)/shard_map/ppermute | solution.py:597
  18.8 2.6 %collective-permute-start.10 = (f32[8,512]{1,0:T(8,128)S(1)}, f32[8,512]{1,0:T(8,128)S(1)}, u32[]{:S(2)}, u32[]{:S(2)}) collective-permute-start(f32[8,512]{1,0:T(8,128)S(1)} %get-tuple-element.60.mine), channel_id=1, source_target_pairs={{0,17},{1,16},{2,19},{3,18},{4,21},{5,20},{6,23},{7,22},{8,25},{9,... | collective-permute-start | bytes 49160 | tf_op jit(solution)/shard_map/ppermute | solution.py:597
  21.3 0.0 collective-permute-done.6.near
  21.3 2.3 %collective-permute-start.11 = (f32[8,512]{1,0:T(8,128)S(1)}, f32[8,512]{1,0:T(8,128)S(1)}, u32[]{:S(2)}, u32[]{:S(2)}) collective-permute-start(f32[8,512]{1,0:T(8,128)S(1)} %get-tuple-element.60.mine), channel_id=1, source_target_pairs={{0,24},{1,25},{2,26},{3,27},{4,28},{5,29},{6,30},{7,31},{8,16},{9,... | collective-permute-start | bytes 49160 | tf_op jit(solution)/shard_map/ppermute | solution.py:597
  23.6 0.4 %shard_map.82 = (f32[4,8,8,512]{3,2,1,0:T(8,128)S(1)}, f32[4,8,512]{2,1,0:T(8,128)S(1)}, f32[8,8,512]{2,1,0:T(8,128)S(1)}, f32[6,8,512]{2,1,0:T(8,128)S(1)}) custom-call(f32[19,8,512]{2,1,0:T(8,128)S(1)} %get-tuple-element.44.planes, f32[19,8,512]{2,1,0:T(8,128)S(1)} %get-tuple-element.51.halo), custom_call_target="tpu_custom_call" | custom-call | tf_op jit(solution)/shard_map/pallas_call | solution.py:556
  24.0 0.0 collective-permute-done.7.far
  24.0 0.8 %shard_map.84 = (f32[8,8,8,512]{3,2,1,0:T(8,128)S(1)}, f32[88,512]{1,0:T(8,128)S(1)}) custom-call(f32[8,8,8,512]{3,2,1,0:T(8,128)S(1)} %get-tuple-element.53.local, f32[19,8,512]{2,1,0:T(8,128)S(1)} %get-tuple-element.44.planes, f32[19,8,512]{2,1,0:T(8,128)S(1)} %get-tuple-element.51.halo, f32[64,512]{1,0:T(8,128)S(1)} %collective-permute-done.6.near, ...), custom_call_target="tpu_custom_call" | custom-call | tf_op jit(solution)/shard_map/pallas_call | solution.py:556
  24.8 0.0 collective-permute-done.8.boundary_other
  24.9 0.0 collective-permute-done.9.refs_0_
  24.9 0.0 collective-permute-done.10.refs_1_
  24.9 2.0 %collective-permute-done.11.refs_2_ = f32[8,512]{1,0:T(8,128)S(1)} collective-permute-done((f32[8,512]{1,0:T(8,128)S(1)}, f32[8,512]{1,0:T(8,128)S(1)}, u32[]{:S(2)}, u32[]{:S(2)}) %collective-permute-start.11) | collective-permute-done | bytes 16416 | tf_op jit(solution)/shard_map/ppermute | solution.py:597
  26.9 0.1 collective-permute-start.12
  27.0 1.5 %collective-permute-start.13 = (f32[8,512]{1,0:T(8,128)S(1)}, f32[8,512]{1,0:T(8,128)S(1)}, u32[]{:S(2)}, u32[]{:S(2)}) collective-permute-start(f32[8,512]{1,0:T(8,128)S(1)} %slice.4), channel_id=1, source_target_pairs={{0,5},{1,4},{2,7},{3,6},{4,1},{5,0},{6,3},{7,2},{8,13},{9,12},{10,... | collective-permute-start | bytes 49160 | tf_op jit(solution)/shard_map/ppermute | solution.py:597
  28.4 1.7 %collective-permute-start.14 = (f32[8,512]{1,0:T(8,128)S(1)}, f32[8,512]{1,0:T(8,128)S(1)}, u32[]{:S(2)}, u32[]{:S(2)}) collective-permute-start(f32[8,512]{1,0:T(8,128)S(1)} %slice.4), channel_id=1, source_target_pairs={{0,6},{1,7},{2,4},{3,5},{4,2},{5,3},{6,0},{7,1},{8,14},{9,15},{10,... | collective-permute-start | bytes 49160 | tf_op jit(solution)/shard_map/ppermute | solution.py:597
  30.2 0.0 collective-permute-done.13.near
  30.2 3.6 %collective-permute-done.14.diag = f32[8,512]{1,0:T(8,128)S(1)} collective-permute-done((f32[8,512]{1,0:T(8,128)S(1)}, f32[8,512]{1,0:T(8,128)S(1)}, u32[]{:S(2)}, u32[]{:S(2)}) %collective-permute-start.14) | collective-permute-done | bytes 16416 | tf_op jit(solution)/shard_map/ppermute | solution.py:597
  33.8 0.0 collective-permute-done.12.message
  33.8 0.2 shard_map.86
  34.1 0.2 shard_map.87
  34.3 0.1 collective-permute-start.15
  34.4 0.4 %collective-permute-start.16 = (f32[8,512]{1,0:T(8,128)S(1)}, f32[8,512]{1,0:T(8,128)S(1)}, u32[]{:S(2)}, u32[]{:S(2)}) collective-permute-start(f32[8,512]{1,0:T(8,128)S(1)} %get-tuple-element.70.mine_sums), channel_id=1, source_target_pairs={{0,1},{1,0},{2,3},{3,2},{4,5},{5,4},{6,7},{7,6},{8,9},{9,8},{10,11... | collective-permute-start | bytes 49160 | tf_op jit(solution)/shard_map/ppermute | solution.py:597
  34.9 0.2 shard_map.88.kept
  35.0 0.8 %shard_map.89.partly = f32[4,16,8,512]{3,2,1,0:T(8,128)} custom-call(f32[4,8,8,512]{3,2,1,0:T(8,128)S(1)} %shard_map.88.kept), custom_call_target="tpu_custom_call" | custom-call | tf_op jit(solution)/shard_map/pallas_call | solution.py:556
  35.9 0.4 %collective-permute-done.16.other_sums = f32[8,512]{1,0:T(8,128)S(1)} collective-permute-done((f32[8,512]{1,0:T(8,128)S(1)}, f32[8,512]{1,0:T(8,128)S(1)}, u32[]{:S(2)}, u32[]{:S(2)}) %collective-permute-start.16) | collective-permute-done | bytes 16416 | tf_op jit(solution)/shard_map/ppermute | solution.py:597
  36.3 0.0 collective-permute-done.15.received
  36.3 0.8 %shard_map.90 = (f32[4,16,8,512]{3,2,1,0:T(8,128)}, f32[16,512]{1,0:T(8,128)}) custom-call(f32[4,16,8,512]{3,2,1,0:T(8,128)} %shard_map.89.partly, f32[4,8,8,512]{3,2,1,0:T(8,128)S(1)} %collective-permute-done.15.received, f32[8,512]{1,0:T(8,128)S(1)} %get-tuple-element.70.mine_sums, ...), custom_call_target="tpu_custom_call", output_to_operand_aliasing={{0}: (0, {})} | custom-call | tf_op jit(solution)/shard_map/pallas_call | solution.py:556
  (3 shorter events, 0.0 us)
Async XLA Ops:
  0.6 8.3 %copy-start = (f32[8,512]{1,0:T(8,128)S(1)}, f32[8,512]{1,0:T(8,128)}, u32[]{:S(2)}) copy-start(f32[8,512]{1,0:T(8,128)} %horiz.1) | copy-start | bytes 49156
  2.0 5.7 %collective-permute-start.2 = (f32[4,8,8,512]{3,2,1,0:T(8,128)S(1)}, f32[4,8,8,512]{3,2,1,0:T(8,128)S(1)}, u32[]{:S(2)}, u32[]{:S(2)}) collective-permute-start(f32[4,8,8,512]{3,2,1,0:T(8,128)S(1)} %get-tuple-element.40), channel_id=1, source_target_pairs={{0,1},{1,0},{2,3},{3,2},{4,5},{5,4},{6,7},{7,6},{8,9},{9,8},{10,11... | collective-permute-start | bytes 1572872 | tf_op jit(solution)/shard_map/ppermute | solution.py:597
  2.5 5.2 %collective-permute-start = (f32[18,8,128]{2,1,0:T(8,128)S(1)}, f32[18,8,128]{2,1,0:T(8,128)S(1)}, u32[]{:S(2)}, u32[]{:S(2)}) collective-permute-start(f32[18,8,128]{2,1,0:T(8,128)S(1)} %get-tuple-element.39.own), channel_id=1, source_target_pairs={{0,3},{1,2},{2,1},{3,0},{4,7},{5,6},{6,5},{7,4},{8,11},{9,10},{10,... | collective-permute-start | bytes 221192 | tf_op jit(solution)/shard_map/ppermute | solution.py:597
  5.1 2.6 %collective-permute-start.1 = (f32[18,8,128]{2,1,0:T(8,128)S(1)}, f32[18,8,128]{2,1,0:T(8,128)S(1)}, u32[]{:S(2)}, u32[]{:S(2)}) collective-permute-start(f32[18,8,128]{2,1,0:T(8,128)S(1)} %get-tuple-element.39.own), channel_id=1, source_target_pairs={{0,1},{1,0},{2,3},{3,2},{4,5},{5,4},{6,7},{7,6},{8,9},{9,8},{10,11... | collective-permute-start | bytes 221192 | tf_op jit(solution)/shard_map/ppermute | solution.py:597
  7.7 1.3 %collective-permute-start.3 = (f32[18,8,128]{2,1,0:T(8,128)S(1)}, f32[18,8,128]{2,1,0:T(8,128)S(1)}, u32[]{:S(2)}, u32[]{:S(2)}) collective-permute-start(f32[18,8,128]{2,1,0:T(8,128)S(1)} %collective-permute-done.cross), channel_id=1, source_target_pairs={{0,1},{1,0},{2,3},{3,2},{4,5},{5,4},{6,7},{7,6},{8,9},{9,8},{10,11... | collective-permute-start | bytes 221192 | tf_op jit(solution)/shard_map/ppermute | solution.py:597
  9.0 6.4 %collective-permute-start.4 = (f32[24,512]{1,0:T(8,128)S(1)}, f32[24,512]{1,0:T(8,128)S(1)}, u32[]{:S(2)}, u32[]{:S(2)}) collective-permute-start(f32[24,512]{1,0:T(8,128)S(1)} %get-tuple-element.46), channel_id=1, source_target_pairs={{0,5},{1,4},{2,7},{3,6},{4,1},{5,0},{6,3},{7,2},{8,13},{9,12},{10,... | collective-permute-start | bytes 147464 | tf_op jit(solution)/shard_map/ppermute | solution.py:597
  10.5 4.9 %collective-permute-start.5 = (f32[24,512]{1,0:T(8,128)S(1)}, f32[24,512]{1,0:T(8,128)S(1)}, u32[]{:S(2)}, u32[]{:S(2)}) collective-permute-start(f32[24,512]{1,0:T(8,128)S(1)} %get-tuple-element.47), channel_id=1, source_target_pairs={{0,1},{1,0},{2,3},{3,2},{4,9},{5,8},{6,11},{7,10},{8,5},{9,4},{10,... | collective-permute-start | bytes 147464 | tf_op jit(solution)/shard_map/ppermute | solution.py:597
  10.8 10.6 %collective-permute-start.6 = (f32[64,512]{1,0:T(8,128)S(1)}, f32[64,512]{1,0:T(8,128)S(1)}, u32[]{:S(2)}, u32[]{:S(2)}) collective-permute-start(f32[64,512]{1,0:T(8,128)S(1)} %get-tuple-element.54), channel_id=1, source_target_pairs={{0,5},{1,4},{2,7},{3,6},{4,1},{5,0},{6,3},{7,2},{8,13},{9,12},{10,... | collective-permute-start | bytes 393224 | tf_op jit(solution)/shard_map/ppermute | solution.py:597
  13.4 10.6 %collective-permute-start.7 = (f32[64,512]{1,0:T(8,128)S(1)}, f32[64,512]{1,0:T(8,128)S(1)}, u32[]{:S(2)}, u32[]{:S(2)}) collective-permute-start(f32[64,512]{1,0:T(8,128)S(1)} %get-tuple-element.55), channel_id=1, source_target_pairs={{0,1},{1,0},{2,3},{3,2},{4,8},{5,9},{6,10},{7,11},{8,4},{9,5},{10,... | collective-permute-start | bytes 393224 | tf_op jit(solution)/shard_map/ppermute | solution.py:597
  15.4 9.4 %collective-permute-start.8 = (f32[8,8,512]{2,1,0:T(8,128)S(1)}, f32[8,8,512]{2,1,0:T(8,128)S(1)}, u32[]{:S(2)}, u32[]{:S(2)}) collective-permute-start(f32[8,8,512]{2,1,0:T(8,128)S(1)} %get-tuple-element.58.boundary), channel_id=1, source_target_pairs={{0,3},{1,2},{2,1},{3,0},{4,7},{5,6},{6,5},{7,4},{8,11},{9,10},{10,... | collective-permute-start | bytes 393224 | tf_op jit(solution)/shard_map/ppermute | solution.py:597
  17.5 7.3 %collective-permute-start.9 = (f32[8,512]{1,0:T(8,128)S(1)}, f32[8,512]{1,0:T(8,128)S(1)}, u32[]{:S(2)}, u32[]{:S(2)}) collective-permute-start(f32[8,512]{1,0:T(8,128)S(1)} %get-tuple-element.60.mine), channel_id=1, source_target_pairs={{0,9},{1,8},{2,11},{3,10},{4,13},{5,12},{6,15},{7,14},{8,1},{9,0},... | collective-permute-start | bytes 49160 | tf_op jit(solution)/shard_map/ppermute | solution.py:597
  18.8 6.1 %collective-permute-start.10 = (f32[8,512]{1,0:T(8,128)S(1)}, f32[8,512]{1,0:T(8,128)S(1)}, u32[]{:S(2)}, u32[]{:S(2)}) collective-permute-start(f32[8,512]{1,0:T(8,128)S(1)} %get-tuple-element.60.mine), channel_id=1, source_target_pairs={{0,17},{1,16},{2,19},{3,18},{4,21},{5,20},{6,23},{7,22},{8,25},{9,... | collective-permute-start | bytes 49160 | tf_op jit(solution)/shard_map/ppermute | solution.py:597
  21.3 5.5 %collective-permute-start.11 = (f32[8,512]{1,0:T(8,128)S(1)}, f32[8,512]{1,0:T(8,128)S(1)}, u32[]{:S(2)}, u32[]{:S(2)}) collective-permute-start(f32[8,512]{1,0:T(8,128)S(1)} %get-tuple-element.60.mine), channel_id=1, source_target_pairs={{0,24},{1,25},{2,26},{3,27},{4,28},{5,29},{6,30},{7,31},{8,16},{9,... | collective-permute-start | bytes 49160 | tf_op jit(solution)/shard_map/ppermute | solution.py:597
  26.9 7.0 %collective-permute-start.12 = (f32[88,512]{1,0:T(8,128)S(1)}, f32[88,512]{1,0:T(8,128)S(1)}, u32[]{:S(2)}, u32[]{:S(2)}) collective-permute-start(f32[88,512]{1,0:T(8,128)S(1)} %shard_map.85.message_mine), channel_id=1, source_target_pairs={{0,3},{1,2},{2,1},{3,0},{4,7},{5,6},{6,5},{7,4},{8,11},{9,10},{10,... | collective-permute-start | bytes 540680 | tf_op jit(solution)/shard_map/ppermute | solution.py:597
  27.0 3.2 %collective-permute-start.13 = (f32[8,512]{1,0:T(8,128)S(1)}, f32[8,512]{1,0:T(8,128)S(1)}, u32[]{:S(2)}, u32[]{:S(2)}) collective-permute-start(f32[8,512]{1,0:T(8,128)S(1)} %slice.4), channel_id=1, source_target_pairs={{0,5},{1,4},{2,7},{3,6},{4,1},{5,0},{6,3},{7,2},{8,13},{9,12},{10,... | collective-permute-start | bytes 49160 | tf_op jit(solution)/shard_map/ppermute | solution.py:597
  28.4 5.4 %collective-permute-start.14 = (f32[8,512]{1,0:T(8,128)S(1)}, f32[8,512]{1,0:T(8,128)S(1)}, u32[]{:S(2)}, u32[]{:S(2)}) collective-permute-start(f32[8,512]{1,0:T(8,128)S(1)} %slice.4), channel_id=1, source_target_pairs={{0,6},{1,7},{2,4},{3,5},{4,2},{5,3},{6,0},{7,1},{8,14},{9,15},{10,... | collective-permute-start | bytes 49160 | tf_op jit(solution)/shard_map/ppermute | solution.py:597
  34.3 2.0 %collective-permute-start.15 = (f32[4,8,8,512]{3,2,1,0:T(8,128)S(1)}, f32[4,8,8,512]{3,2,1,0:T(8,128)S(1)}, u32[]{:S(2)}, u32[]{:S(2)}) collective-permute-start(f32[4,8,8,512]{3,2,1,0:T(8,128)S(1)} %shard_map.87), channel_id=1, source_target_pairs={{0,1},{1,0},{2,3},{3,2},{4,5},{5,4},{6,7},{7,6},{8,9},{9,8},{10,11... | collective-permute-start | bytes 1572872 | tf_op jit(solution)/shard_map/ppermute | solution.py:597
  34.4 1.9 %collective-permute-start.16 = (f32[8,512]{1,0:T(8,128)S(1)}, f32[8,512]{1,0:T(8,128)S(1)}, u32[]{:S(2)}, u32[]{:S(2)}) collective-permute-start(f32[8,512]{1,0:T(8,128)S(1)} %get-tuple-element.70.mine_sums), channel_id=1, source_target_pairs={{0,1},{1,0},{2,3},{3,2},{4,5},{5,4},{6,7},{7,6},{8,9},{9,8},{10,11... | collective-permute-start | bytes 49160 | tf_op jit(solution)/shard_map/ppermute | solution.py:597

commit v6 on v5

--- a/solution.py
+++ b/solution.py
@@ -375,8 +375,9 @@
         total = total + parts[0][...]
     if len(parts) == 3:
         total = total + (parts[1][...] + parts[2][...])
-    size = mine.shape[0]
-    out[out.shape[0] - size :, :] = total
+    size = out.shape[0] - mine.shape[0]
+    out[0:size, :] = message[0:size, :]
+    out[size:, :] = total
 
 
 def middle_kernel(local, planes, halo, near, far, base, message, factors, outside):
@@ -691,11 +692,7 @@
         [(half, functionals, rows, width), (functionals * (rows + 3), width)],
         [factors, pltpu.VMEM((2, half, functionals, width), f32)],
     )(after(local, spread), planes, halo, rows_near, rows_far)
-    (message,) = call(
-        fold_kernel,
-        [message.shape],
-        aliases={len(parts) + 1: 0},
-    )(after(sums, boundary_other), *parts, message)
+    (message,) = call(fold_kernel, [message.shape])(after(sums, boundary_other), *parts, message)
     message_other = across(message, 3)
     sums = message[functionals * (rows + 2) :]
     near = send(sums, lambda t, i: (t ^ 1, i ^ 1))

time: 37.3 us -> 37.3 us (level)
  no operation moved by 1% of the time
where the time goes in v6:
time: 37.3 us; the launch traced here: 37.1 us
  starting transfers between devices  19.2 us (51%)
  waiting for transfers between devices  9.75 us (26%)
  Pallas kernels  7.39 us (20%)
  between operations  0.79 us (2%)
    ppermute x17, starting transfers between devices, send(): return lax.ppermute(array, ('tile', 'layer'), pairs)  19.2 us
    ppermute x17, waiting for transfers between devices, send(): return lax.ppermute(array, ('tile', 'layer'), pairs)  9.75 us
    pallas_call x14, Pallas kernels, run(): pl.pallas_call(kernel, out_shape=[(pltpu.HBM if i in any_outputs else jax...  7.39 us
  transfers between devices with their start and end apart: 17, of which 5 were waited for; matrix products, arithmetic and copies ran while one was open for 0% of the time, Pallas kernels for 13%

profile of v6, /device:TPU:0, one launch (start us, length us, event | category | flops | bytes accessed | tf_op | source)
XLA Modules:
  0.0 37.1 jit_solution(8260083291790478515)
XLA Ops:
  0.6 0.0 copy-start
  0.6 1.3 %shard_map.77 = (f32[18,8,128]{2,1,0:T(8,128)S(1)}, f32[4,8,8,512]{3,2,1,0:T(8,128)S(1)}, f32[4,8,8,512]{3,2,1,0:T(8,128)S(1)}) custom-call(f32[16,8,128]{2,1,0:T(8,128)} %coupling.1, f32[8,128]{1,0:T(8,128)} %velocity.1, s32[8,128]{1,0:T(8,128)} %label.1, s32[8,128]{1,0:T(8,128)} %mask.1, f32[4,16,8,512]{3,2,1,0:T(8,128)} %forcing.1), custom_call_target="tpu_custom_call" | custom-call | tf_op jit(solution)/shard_map/pallas_call | solution.py:557
  2.0 0.5 %collective-permute-start.2 = (f32[4,8,8,512]{3,2,1,0:T(8,128)S(1)}, f32[4,8,8,512]{3,2,1,0:T(8,128)S(1)}, u32[]{:S(2)}, u32[]{:S(2)}) collective-permute-start(f32[4,8,8,512]{3,2,1,0:T(8,128)S(1)} %get-tuple-element.40), channel_id=1, source_target_pairs={{0,1},{1,0},{2,3},{3,2},{4,5},{5,4},{6,7},{7,6},{8,9},{9,8},{10,11... | collective-permute-start | bytes 1572872 | tf_op jit(solution)/shard_map/ppermute | solution.py:598
  2.5 2.6 %collective-permute-start = (f32[18,8,128]{2,1,0:T(8,128)S(1)}, f32[18,8,128]{2,1,0:T(8,128)S(1)}, u32[]{:S(2)}, u32[]{:S(2)}) collective-permute-start(f32[18,8,128]{2,1,0:T(8,128)S(1)} %get-tuple-element.39.own), channel_id=1, source_target_pairs={{0,3},{1,2},{2,1},{3,0},{4,7},{5,6},{6,5},{7,4},{8,11},{9,10},{10,... | collective-permute-start | bytes 221192 | tf_op jit(solution)/shard_map/ppermute | solution.py:598
  5.1 0.1 collective-permute-start.1
  5.2 2.5 %collective-permute-done.cross = f32[18,8,128]{2,1,0:T(8,128)S(1)} collective-permute-done((f32[18,8,128]{2,1,0:T(8,128)S(1)}, f32[18,8,128]{2,1,0:T(8,128)S(1)}, u32[]{:S(2)}, u32[]{:S(2)}) %collective-permute-start) | collective-permute-done | bytes 73760 | tf_op jit(solution)/shard_map/ppermute | solution.py:598
  7.7 0.0 collective-permute-done.1.peer
  7.7 0.0 collective-permute-done.2.received
  7.7 0.1 collective-permute-start.3
  7.8 1.2 %collective-permute-done.3.diag = f32[18,8,128]{2,1,0:T(8,128)S(1)} collective-permute-done((f32[18,8,128]{2,1,0:T(8,128)S(1)}, f32[18,8,128]{2,1,0:T(8,128)S(1)}, u32[]{:S(2)}, u32[]{:S(2)}) %collective-permute-start.3) | collective-permute-done | bytes 73760 | tf_op jit(solution)/shard_map/ppermute | solution.py:598
  9.0 0.1 shard_map.78
  9.0 1.5 %collective-permute-start.4 = (f32[24,512]{1,0:T(8,128)S(1)}, f32[24,512]{1,0:T(8,128)S(1)}, u32[]{:S(2)}, u32[]{:S(2)}) collective-permute-start(f32[24,512]{1,0:T(8,128)S(1)} %get-tuple-element.46), channel_id=1, source_target_pairs={{0,5},{1,4},{2,7},{3,6},{4,1},{5,0},{6,3},{7,2},{8,13},{9,12},{10,... | collective-permute-start | bytes 147464 | tf_op jit(solution)/shard_map/ppermute | solution.py:598
  10.5 0.2 collective-permute-start.5
  10.7 0.1 shard_map.83
  10.8 2.7 %collective-permute-start.6 = (f32[64,512]{1,0:T(8,128)S(1)}, f32[64,512]{1,0:T(8,128)S(1)}, u32[]{:S(2)}, u32[]{:S(2)}) collective-permute-start(f32[64,512]{1,0:T(8,128)S(1)} %get-tuple-element.54), channel_id=1, source_target_pairs={{0,5},{1,4},{2,7},{3,6},{4,1},{5,0},{6,3},{7,2},{8,13},{9,12},{10,... | collective-permute-start | bytes 393224 | tf_op jit(solution)/shard_map/ppermute | solution.py:598
  13.4 0.2 collective-permute-start.7
  13.6 0.3 shard_map.79
  13.9 1.5 %shard_map.80.inside = f32[8,512]{1,0:T(8,128)S(1)} custom-call(f32[4,8,8,512]{3,2,1,0:T(8,128)S(1)} %get-tuple-element.38.own.kept, f32[4,8,8,512]{3,2,1,0:T(8,128)S(1)} %collective-permute-done.2.received, f32[19,8,512]{2,1,0:T(8,128)S(1)} %get-tuple-element.44.planes), custom_call_target="tpu_custom_call" | custom-call | tf_op jit(solution)/shard_map/pallas_call | solution.py:557
  15.4 0.0 collective-permute-done.4.near
  15.4 0.0 collective-permute-done.5.far
  15.4 1.5 %collective-permute-start.8 = (f32[8,8,512]{2,1,0:T(8,128)S(1)}, f32[8,8,512]{2,1,0:T(8,128)S(1)}, u32[]{:S(2)}, u32[]{:S(2)}) collective-permute-start(f32[8,8,512]{2,1,0:T(8,128)S(1)} %get-tuple-element.58.boundary), channel_id=1, source_target_pairs={{0,3},{1,2},{2,1},{3,0},{4,7},{5,6},{6,5},{7,4},{8,11},{9,10},{10,... | collective-permute-start | bytes 393224 | tf_op jit(solution)/shard_map/ppermute | solution.py:598
  16.9 0.6 %shard_map.81 = (f32[8,512]{1,0:T(8,128)S(1)}, f32[19,8,512]{2,1,0:T(8,128)S(1)}) custom-call(f32[8,8,8,512]{3,2,1,0:T(8,128)S(1)} %get-tuple-element.53.local, f32[19,8,512]{2,1,0:T(8,128)S(1)} %get-tuple-element.44.planes, f32[24,512]{1,0:T(8,128)S(1)} %collective-permute-done.4.near, f32[24,512]{1,0:T(8,128)S(1)} %collective-permute-done.5.far, ...), custom_call_target="tpu_custom_call" | custom-call | tf_op jit(solution)/shard_map/pallas_call | solution.py:557
  17.5 1.2 %collective-permute-start.9 = (f32[8,512]{1,0:T(8,128)S(1)}, f32[8,512]{1,0:T(8,128)S(1)}, u32[]{:S(2)}, u32[]{:S(2)}) collective-permute-start(f32[8,512]{1,0:T(8,128)S(1)} %get-tuple-element.60.mine), channel_id=1, source_target_pairs={{0,9},{1,8},{2,11},{3,10},{4,13},{5,12},{6,15},{7,14},{8,1},{9,0},... | collective-permute-start | bytes 49160 | tf_op jit(solution)/shard_map/ppermute | solution.py:598
  18.8 2.6 %collective-permute-start.10 = (f32[8,512]{1,0:T(8,128)S(1)}, f32[8,512]{1,0:T(8,128)S(1)}, u32[]{:S(2)}, u32[]{:S(2)}) collective-permute-start(f32[8,512]{1,0:T(8,128)S(1)} %get-tuple-element.60.mine), channel_id=1, source_target_pairs={{0,17},{1,16},{2,19},{3,18},{4,21},{5,20},{6,23},{7,22},{8,25},{9,... | collective-permute-start | bytes 49160 | tf_op jit(solution)/shard_map/ppermute | solution.py:598
  21.3 0.0 collective-permute-done.6.near
  21.3 2.3 %collective-permute-start.11 = (f32[8,512]{1,0:T(8,128)S(1)}, f32[8,512]{1,0:T(8,128)S(1)}, u32[]{:S(2)}, u32[]{:S(2)}) collective-permute-start(f32[8,512]{1,0:T(8,128)S(1)} %get-tuple-element.60.mine), channel_id=1, source_target_pairs={{0,24},{1,25},{2,26},{3,27},{4,28},{5,29},{6,30},{7,31},{8,16},{9,... | collective-permute-start | bytes 49160 | tf_op jit(solution)/shard_map/ppermute | solution.py:598
  23.6 0.4 %shard_map.82 = (f32[4,8,8,512]{3,2,1,0:T(8,128)S(1)}, f32[4,8,512]{2,1,0:T(8,128)S(1)}, f32[8,8,512]{2,1,0:T(8,128)S(1)}, f32[6,8,512]{2,1,0:T(8,128)S(1)}) custom-call(f32[19,8,512]{2,1,0:T(8,128)S(1)} %get-tuple-element.44.planes, f32[19,8,512]{2,1,0:T(8,128)S(1)} %get-tuple-element.51.halo), custom_call_target="tpu_custom_call" | custom-call | tf_op jit(solution)/shard_map/pallas_call | solution.py:557
  24.0 0.0 collective-permute-done.7.far
  24.0 0.8 %shard_map.84 = (f32[8,8,8,512]{3,2,1,0:T(8,128)S(1)}, f32[88,512]{1,0:T(8,128)S(1)}) custom-call(f32[8,8,8,512]{3,2,1,0:T(8,128)S(1)} %get-tuple-element.53.local, f32[19,8,512]{2,1,0:T(8,128)S(1)} %get-tuple-element.44.planes, f32[19,8,512]{2,1,0:T(8,128)S(1)} %get-tuple-element.51.halo, f32[64,512]{1,0:T(8,128)S(1)} %collective-permute-done.6.near, ...), custom_call_target="tpu_custom_call" | custom-call | tf_op jit(solution)/shard_map/pallas_call | solution.py:557
  24.8 0.0 collective-permute-done.8.boundary_other
  24.9 0.0 collective-permute-done.9.refs_0_
  24.9 0.0 collective-permute-done.10.refs_1_
  24.9 2.0 %collective-permute-done.11.refs_2_ = f32[8,512]{1,0:T(8,128)S(1)} collective-permute-done((f32[8,512]{1,0:T(8,128)S(1)}, f32[8,512]{1,0:T(8,128)S(1)}, u32[]{:S(2)}, u32[]{:S(2)}) %collective-permute-start.11) | collective-permute-done | bytes 16416 | tf_op jit(solution)/shard_map/ppermute | solution.py:598
  26.9 0.1 collective-permute-start.12
  27.0 1.5 %collective-permute-start.13 = (f32[8,512]{1,0:T(8,128)S(1)}, f32[8,512]{1,0:T(8,128)S(1)}, u32[]{:S(2)}, u32[]{:S(2)}) collective-permute-start(f32[8,512]{1,0:T(8,128)S(1)} %slice.4), channel_id=1, source_target_pairs={{0,5},{1,4},{2,7},{3,6},{4,1},{5,0},{6,3},{7,2},{8,13},{9,12},{10,... | collective-permute-start | bytes 49160 | tf_op jit(solution)/shard_map/ppermute | solution.py:598
  28.4 1.7 %collective-permute-start.14 = (f32[8,512]{1,0:T(8,128)S(1)}, f32[8,512]{1,0:T(8,128)S(1)}, u32[]{:S(2)}, u32[]{:S(2)}) collective-permute-start(f32[8,512]{1,0:T(8,128)S(1)} %slice.4), channel_id=1, source_target_pairs={{0,6},{1,7},{2,4},{3,5},{4,2},{5,3},{6,0},{7,1},{8,14},{9,15},{10,... | collective-permute-start | bytes 49160 | tf_op jit(solution)/shard_map/ppermute | solution.py:598
  30.2 0.0 collective-permute-done.13.near
  30.2 3.6 %collective-permute-done.14.diag = f32[8,512]{1,0:T(8,128)S(1)} collective-permute-done((f32[8,512]{1,0:T(8,128)S(1)}, f32[8,512]{1,0:T(8,128)S(1)}, u32[]{:S(2)}, u32[]{:S(2)}) %collective-permute-start.14) | collective-permute-done | bytes 16416 | tf_op jit(solution)/shard_map/ppermute | solution.py:598
  33.9 0.0 collective-permute-done.12.message
  33.9 0.2 shard_map.86
  34.1 0.2 shard_map.87
  34.3 0.1 collective-permute-start.15
  34.4 0.4 %collective-permute-start.16 = (f32[8,512]{1,0:T(8,128)S(1)}, f32[8,512]{1,0:T(8,128)S(1)}, u32[]{:S(2)}, u32[]{:S(2)}) collective-permute-start(f32[8,512]{1,0:T(8,128)S(1)} %get-tuple-element.70.mine_sums), channel_id=1, source_target_pairs={{0,1},{1,0},{2,3},{3,2},{4,5},{5,4},{6,7},{7,6},{8,9},{9,8},{10,11... | collective-permute-start | bytes 49160 | tf_op jit(solution)/shard_map/ppermute | solution.py:598
  34.9 0.2 shard_map.88.kept
  35.1 0.8 %shard_map.89.partly = f32[4,16,8,512]{3,2,1,0:T(8,128)} custom-call(f32[4,8,8,512]{3,2,1,0:T(8,128)S(1)} %shard_map.88.kept), custom_call_target="tpu_custom_call" | custom-call | tf_op jit(solution)/shard_map/pallas_call | solution.py:557
  35.9 0.4 %collective-permute-done.16.other_sums = f32[8,512]{1,0:T(8,128)S(1)} collective-permute-done((f32[8,512]{1,0:T(8,128)S(1)}, f32[8,512]{1,0:T(8,128)S(1)}, u32[]{:S(2)}, u32[]{:S(2)}) %collective-permute-start.16) | collective-permute-done | bytes 16416 | tf_op jit(solution)/shard_map/ppermute | solution.py:598
  36.3 0.0 collective-permute-done.15.received
  36.3 0.8 %shard_map.90 = (f32[4,16,8,512]{3,2,1,0:T(8,128)}, f32[16,512]{1,0:T(8,128)}) custom-call(f32[4,16,8,512]{3,2,1,0:T(8,128)} %shard_map.89.partly, f32[4,8,8,512]{3,2,1,0:T(8,128)S(1)} %collective-permute-done.15.received, f32[8,512]{1,0:T(8,128)S(1)} %get-tuple-element.70.mine_sums, ...), custom_call_target="tpu_custom_call", output_to_operand_aliasing={{0}: (0, {})} | custom-call | tf_op jit(solution)/shard_map/pallas_call | solution.py:557
  (3 shorter events, 0.0 us)
Async XLA Ops:
  0.6 8.3 %copy-start = (f32[8,512]{1,0:T(8,128)S(1)}, f32[8,512]{1,0:T(8,128)}, u32[]{:S(2)}) copy-start(f32[8,512]{1,0:T(8,128)} %horiz.1) | copy-start | bytes 49156
  2.0 5.7 %collective-permute-start.2 = (f32[4,8,8,512]{3,2,1,0:T(8,128)S(1)}, f32[4,8,8,512]{3,2,1,0:T(8,128)S(1)}, u32[]{:S(2)}, u32[]{:S(2)}) collective-permute-start(f32[4,8,8,512]{3,2,1,0:T(8,128)S(1)} %get-tuple-element.40), channel_id=1, source_target_pairs={{0,1},{1,0},{2,3},{3,2},{4,5},{5,4},{6,7},{7,6},{8,9},{9,8},{10,11... | collective-permute-start | bytes 1572872 | tf_op jit(solution)/shard_map/ppermute | solution.py:598
  2.5 5.2 %collective-permute-start = (f32[18,8,128]{2,1,0:T(8,128)S(1)}, f32[18,8,128]{2,1,0:T(8,128)S(1)}, u32[]{:S(2)}, u32[]{:S(2)}) collective-permute-start(f32[18,8,128]{2,1,0:T(8,128)S(1)} %get-tuple-element.39.own), channel_id=1, source_target_pairs={{0,3},{1,2},{2,1},{3,0},{4,7},{5,6},{6,5},{7,4},{8,11},{9,10},{10,... | collective-permute-start | bytes 221192 | tf_op jit(solution)/shard_map/ppermute | solution.py:598
  5.1 2.6 %collective-permute-start.1 = (f32[18,8,128]{2,1,0:T(8,128)S(1)}, f32[18,8,128]{2,1,0:T(8,128)S(1)}, u32[]{:S(2)}, u32[]{:S(2)}) collective-permute-start(f32[18,8,128]{2,1,0:T(8,128)S(1)} %get-tuple-element.39.own), channel_id=1, source_target_pairs={{0,1},{1,0},{2,3},{3,2},{4,5},{5,4},{6,7},{7,6},{8,9},{9,8},{10,11... | collective-permute-start | bytes 221192 | tf_op jit(solution)/shard_map/ppermute | solution.py:598
  7.7 1.3 %collective-permute-start.3 = (f32[18,8,128]{2,1,0:T(8,128)S(1)}, f32[18,8,128]{2,1,0:T(8,128)S(1)}, u32[]{:S(2)}, u32[]{:S(2)}) collective-permute-start(f32[18,8,128]{2,1,0:T(8,128)S(1)} %collective-permute-done.cross), channel_id=1, source_target_pairs={{0,1},{1,0},{2,3},{3,2},{4,5},{5,4},{6,7},{7,6},{8,9},{9,8},{10,11... | collective-permute-start | bytes 221192 | tf_op jit(solution)/shard_map/ppermute | solution.py:598
  9.0 6.4 %collective-permute-start.4 = (f32[24,512]{1,0:T(8,128)S(1)}, f32[24,512]{1,0:T(8,128)S(1)}, u32[]{:S(2)}, u32[]{:S(2)}) collective-permute-start(f32[24,512]{1,0:T(8,128)S(1)} %get-tuple-element.46), channel_id=1, source_target_pairs={{0,5},{1,4},{2,7},{3,6},{4,1},{5,0},{6,3},{7,2},{8,13},{9,12},{10,... | collective-permute-start | bytes 147464 | tf_op jit(solution)/shard_map/ppermute | solution.py:598
  10.5 4.9 %collective-permute-start.5 = (f32[24,512]{1,0:T(8,128)S(1)}, f32[24,512]{1,0:T(8,128)S(1)}, u32[]{:S(2)}, u32[]{:S(2)}) collective-permute-start(f32[24,512]{1,0:T(8,128)S(1)} %get-tuple-element.47), channel_id=1, source_target_pairs={{0,1},{1,0},{2,3},{3,2},{4,9},{5,8},{6,11},{7,10},{8,5},{9,4},{10,... | collective-permute-start | bytes 147464 | tf_op jit(solution)/shard_map/ppermute | solution.py:598
  10.8 10.6 %collective-permute-start.6 = (f32[64,512]{1,0:T(8,128)S(1)}, f32[64,512]{1,0:T(8,128)S(1)}, u32[]{:S(2)}, u32[]{:S(2)}) collective-permute-start(f32[64,512]{1,0:T(8,128)S(1)} %get-tuple-element.54), channel_id=1, source_target_pairs={{0,5},{1,4},{2,7},{3,6},{4,1},{5,0},{6,3},{7,2},{8,13},{9,12},{10,... | collective-permute-start | bytes 393224 | tf_op jit(solution)/shard_map/ppermute | solution.py:598
  13.4 10.6 %collective-permute-start.7 = (f32[64,512]{1,0:T(8,128)S(1)}, f32[64,512]{1,0:T(8,128)S(1)}, u32[]{:S(2)}, u32[]{:S(2)}) collective-permute-start(f32[64,512]{1,0:T(8,128)S(1)} %get-tuple-element.55), channel_id=1, source_target_pairs={{0,1},{1,0},{2,3},{3,2},{4,8},{5,9},{6,10},{7,11},{8,4},{9,5},{10,... | collective-permute-start | bytes 393224 | tf_op jit(solution)/shard_map/ppermute | solution.py:598
  15.4 9.4 %collective-permute-start.8 = (f32[8,8,512]{2,1,0:T(8,128)S(1)}, f32[8,8,512]{2,1,0:T(8,128)S(1)}, u32[]{:S(2)}, u32[]{:S(2)}) collective-permute-start(f32[8,8,512]{2,1,0:T(8,128)S(1)} %get-tuple-element.58.boundary), channel_id=1, source_target_pairs={{0,3},{1,2},{2,1},{3,0},{4,7},{5,6},{6,5},{7,4},{8,11},{9,10},{10,... | collective-permute-start | bytes 393224 | tf_op jit(solution)/shard_map/ppermute | solution.py:598
  17.5 7.3 %collective-permute-start.9 = (f32[8,512]{1,0:T(8,128)S(1)}, f32[8,512]{1,0:T(8,128)S(1)}, u32[]{:S(2)}, u32[]{:S(2)}) collective-permute-start(f32[8,512]{1,0:T(8,128)S(1)} %get-tuple-element.60.mine), channel_id=1, source_target_pairs={{0,9},{1,8},{2,11},{3,10},{4,13},{5,12},{6,15},{7,14},{8,1},{9,0},... | collective-permute-start | bytes 49160 | tf_op jit(solution)/shard_map/ppermute | solution.py:598
  18.8 6.1 %collective-permute-start.10 = (f32[8,512]{1,0:T(8,128)S(1)}, f32[8,512]{1,0:T(8,128)S(1)}, u32[]{:S(2)}, u32[]{:S(2)}) collective-permute-start(f32[8,512]{1,0:T(8,128)S(1)} %get-tuple-element.60.mine), channel_id=1, source_target_pairs={{0,17},{1,16},{2,19},{3,18},{4,21},{5,20},{6,23},{7,22},{8,25},{9,... | collective-permute-start | bytes 49160 | tf_op jit(solution)/shard_map/ppermute | solution.py:598
  21.3 5.5 %collective-permute-start.11 = (f32[8,512]{1,0:T(8,128)S(1)}, f32[8,512]{1,0:T(8,128)S(1)}, u32[]{:S(2)}, u32[]{:S(2)}) collective-permute-start(f32[8,512]{1,0:T(8,128)S(1)} %get-tuple-element.60.mine), channel_id=1, source_target_pairs={{0,24},{1,25},{2,26},{3,27},{4,28},{5,29},{6,30},{7,31},{8,16},{9,... | collective-permute-start | bytes 49160 | tf_op jit(solution)/shard_map/ppermute | solution.py:598
  26.9 7.0 %collective-permute-start.12 = (f32[88,512]{1,0:T(8,128)S(1)}, f32[88,512]{1,0:T(8,128)S(1)}, u32[]{:S(2)}, u32[]{:S(2)}) collective-permute-start(f32[88,512]{1,0:T(8,128)S(1)} %shard_map.85.message_mine), channel_id=1, source_target_pairs={{0,3},{1,2},{2,1},{3,0},{4,7},{5,6},{6,5},{7,4},{8,11},{9,10},{10,... | collective-permute-start | bytes 540680 | tf_op jit(solution)/shard_map/ppermute | solution.py:598
  27.0 3.2 %collective-permute-start.13 = (f32[8,512]{1,0:T(8,128)S(1)}, f32[8,512]{1,0:T(8,128)S(1)}, u32[]{:S(2)}, u32[]{:S(2)}) collective-permute-start(f32[8,512]{1,0:T(8,128)S(1)} %slice.4), channel_id=1, source_target_pairs={{0,5},{1,4},{2,7},{3,6},{4,1},{5,0},{6,3},{7,2},{8,13},{9,12},{10,... | collective-permute-start | bytes 49160 | tf_op jit(solution)/shard_map/ppermute | solution.py:598
  28.4 5.4 %collective-permute-start.14 = (f32[8,512]{1,0:T(8,128)S(1)}, f32[8,512]{1,0:T(8,128)S(1)}, u32[]{:S(2)}, u32[]{:S(2)}) collective-permute-start(f32[8,512]{1,0:T(8,128)S(1)} %slice.4), channel_id=1, source_target_pairs={{0,6},{1,7},{2,4},{3,5},{4,2},{5,3},{6,0},{7,1},{8,14},{9,15},{10,... | collective-permute-start | bytes 49160 | tf_op jit(solution)/shard_map/ppermute | solution.py:598
  34.3 2.0 %collective-permute-start.15 = (f32[4,8,8,512]{3,2,1,0:T(8,128)S(1)}, f32[4,8,8,512]{3,2,1,0:T(8,128)S(1)}, u32[]{:S(2)}, u32[]{:S(2)}) collective-permute-start(f32[4,8,8,512]{3,2,1,0:T(8,128)S(1)} %shard_map.87), channel_id=1, source_target_pairs={{0,1},{1,0},{2,3},{3,2},{4,5},{5,4},{6,7},{7,6},{8,9},{9,8},{10,11... | collective-permute-start | bytes 1572872 | tf_op jit(solution)/shard_map/ppermute | solution.py:598
  34.4 1.9 %collective-permute-start.16 = (f32[8,512]{1,0:T(8,128)S(1)}, f32[8,512]{1,0:T(8,128)S(1)}, u32[]{:S(2)}, u32[]{:S(2)}) collective-permute-start(f32[8,512]{1,0:T(8,128)S(1)} %get-tuple-element.70.mine_sums), channel_id=1, source_target_pairs={{0,1},{1,0},{2,3},{3,2},{4,5},{5,4},{6,7},{7,6},{8,9},{9,8},{10,11... | collective-permute-start | bytes 49160 | tf_op jit(solution)/shard_map/ppermute | solution.py:598
